TPU v7x, 256 devices: a whole 4x4x8 slice. The times are simulated.
256 devices in a mesh: dp: 16 (over y, z_hi, core), proto: 16 (over z_lo, x).
Axes of the slice: x: 4, y: 4, z: 8 (z_hi: 2, z_lo: 4; z = z_hi * 4 + z_lo), core: 2. Of those that a mesh axis runs over, the one named last changes fastest.
Arguments:
- teacher_hidden: bfloat16 [12288, 2048], P('dp', 'proto'), may hold values from -4 to 7
- student_hidden: bfloat16 [12288, 2048], P('dp', 'proto'), may hold values from -6 to 6
- teacher_bottleneck: bfloat16 [2048, 256], P('proto'), may hold values from -1 to 1
- student_bottleneck: bfloat16 [2048, 256], P('proto'), may hold values from -0.125 to 0.125
- teacher_prototypes: bfloat16 [256, 65536], P(None, 'proto'), may hold values from -7 to 7
- student_prototypes: bfloat16 [256, 65536], P(None, 'proto'), may hold values from -0.375 to 0.375
Outputs:
- grad_prototypes: float32 [256, 65536], P('dp', 'proto')
- grad_bottleneck: float32 [2048, 256], P('proto', 'dp')
All inputs are finite; a program needn't handle non-finite values.
Results may differ from a plain program's by a relative error of at most 0.012.
Values may be sent and summed in bfloat16 or wider, within the bound.
No kernel may reach another device: no remote copies, remote signals or barrier semaphores. Data moves between devices by JAX's collectives and lax.ppermute only.
A program may use at most 128 MiB of HBM per device.

v0:
```python
import jax
import jax.numpy as jnp
from jax import lax
from jax.sharding import PartitionSpec as P

PROTOS = 65536
ITERS = 3


TEACHER_TEMP = 0.07
STUDENT_TEMP = 0.1
EPSILON = 1e-06


def unit_rows(values):
    scale = lax.rsqrt(jnp.sum(values * values, axis=1, keepdims=True) + EPSILON)
    return (values * scale, scale)


def unit_cols(weights):
    values = weights.astype(jnp.float32)
    scale = lax.rsqrt(jnp.sum(values * values, axis=0, keepdims=True) + EPSILON)
    return (values * scale, scale)


def on_device(
    teacher_hidden,
    student_hidden,
    teacher_bottleneck,
    student_bottleneck,
    teacher_prototypes,
    student_prototypes,
):
    teach_part = jnp.dot(teacher_hidden, teacher_bottleneck, preferred_element_type=jnp.float32)
    stud_part = jnp.dot(student_hidden, student_bottleneck, preferred_element_type=jnp.float32)
    teach_proj, stud_proj = lax.psum((teach_part, stud_part), "proto")
    teach_unit, unused_scale = unit_rows(teach_proj)
    stud_unit, stud_scale = unit_rows(stud_proj)
    teach_low = teach_unit.astype(jnp.bfloat16)
    stud_low = stud_unit.astype(jnp.bfloat16)
    teach_norm, unused_cols = unit_cols(teacher_prototypes)
    stud_norm, col_norm = unit_cols(student_prototypes)
    teach_wlow = teach_norm.astype(jnp.bfloat16)
    stud_wlow = stud_norm.astype(jnp.bfloat16)
    expo = jnp.exp(
        jnp.dot(teach_low, teach_wlow, preferred_element_type=jnp.float32) / TEACHER_TEMP
    )
    stud_expo = jnp.exp(
        jnp.dot(stud_low, stud_wlow, preferred_element_type=jnp.float32) / STUDENT_TEMP
    )
    totals = lax.psum(jnp.sum(stud_expo, axis=1), "proto")
    row_scale = jnp.ones((expo.shape[0],), jnp.float32)
    col_scale = jnp.ones((expo.shape[1],), jnp.float32)
    for step in range(ITERS):
        col_part = jnp.dot(row_scale, expo, precision=lax.Precision.HIGHEST)
        col_scale = 1.0 / lax.psum(col_part, "dp")
        row_part = jnp.dot(expo, col_scale, precision=lax.Precision.HIGHEST)
        row_scale = 1.0 / lax.psum(row_part, "proto")
    factor = PROTOS / 32.0
    assign = row_scale[:, None] * expo * col_scale[None, :]
    logit_grad = (factor * (stud_expo / totals[:, None] - assign) / STUDENT_TEMP).astype(
        jnp.bfloat16
    )
    feat_part = lax.dot_general(
        logit_grad, stud_wlow, (((1,), (1,)), ((), ())), preferred_element_type=jnp.float32
    )
    feat_grad = lax.psum(feat_part, "proto")
    share = stud_norm.shape[0] // lax.axis_size("dp")
    offset = lax.axis_index("dp") * share
    proto_part = lax.dot_general(
        stud_low, logit_grad, (((0,), (0,)), ((), ())), preferred_element_type=jnp.float32
    )
    proto_sum = lax.psum(proto_part, "dp")
    dots = jnp.sum(stud_norm * proto_sum, axis=0)
    grad_rows = lax.dynamic_slice_in_dim(proto_sum, offset, share, 0)
    norm_rows = lax.dynamic_slice_in_dim(stud_norm, offset, share, 0)
    grad_prototypes = col_norm * (grad_rows - norm_rows * dots[None, :])
    inner = jnp.sum(stud_unit * feat_grad, axis=1, keepdims=True)
    proj_grad = (stud_scale * (feat_grad - stud_unit * inner)).astype(jnp.bfloat16)
    bottle_part = lax.dot_general(
        student_hidden, proj_grad, (((0,), (0,)), ((), ())), preferred_element_type=jnp.float32
    )
    grad_bottleneck = lax.psum_scatter(bottle_part, "dp", scatter_dimension=1, tiled=True)
    return (grad_prototypes, grad_bottleneck)


def solution(mesh):
    return jax.shard_map(
        on_device,
        mesh=mesh,
        in_specs=(
            P("dp", "proto"),
            P("dp", "proto"),
            P("proto", None),
            P("proto", None),
            P(None, "proto"),
            P(None, "proto"),
        ),
        out_specs=(P("dp", "proto"), P("proto", "dp")),
        check_vma=False,
    )
```

profile of v0, /device:TPU:32, one launch (start us, length us, event | category | flops | bytes accessed | tf_op | source)
XLA Modules:
  0.0 1116.4 jit_solution(10399091941311452883)
XLA Ops:
  7.2 0.0 copy-start
  7.2 0.0 copy-start.4
  7.2 0.0 all-reduce.10.cloned.1.call-start
  7.2 0.9 copy-done
  8.1 2.0 fusion.18
  10.1 2.1 fusion.19
  12.1 0.0 all-reduce.10.cloned.1.call-update
  12.2 0.0 all-reduce.8.cloned.1.call-start
  12.2 2.0 fusion.2
  14.3 0.0 copy-done.4
  14.3 0.4 fusion.1
  14.7 160.4 %all-reduce.10.cloned.1.call-done = (f32[768,256]{1,0:T(8,128)}, f32[768,256]{1,0:T(8,128)}) async-done(((f32[768,256]{1,0:T(8,128)}, f32[768,256]{1,0:T(8,128)}), (f32[768,256]{1,0:T(8,128)}, f32[768,256]{1,0:T(8,128)})) %all-reduce.10.cloned.1.call-update) | async-done | bytes 1572880 | tf_op jit(solution)/shard_map/psum | solution.py:36
  175.1 1.3 multiply_reduce_fusion.2
  176.4 3.9 multiply_exponential_fusion
  180.3 0.0 copy-start.1
  180.3 6.0 fusion.14
  186.3 0.0 copy-done.1
  186.3 84.6 %psum.80 = f32[4096]{0:T(1024)S(1)} all-reduce(f32[4096]{0:T(1024)S(1)} %bitcast.31), channel_id=1, replica_groups=mesh['dp'=16,'proto'=16] {'dp'}, use_global_device_ids=true, to_apply=%region_8.0 | all-reduce | flops 4096 | bytes 32768 | tf_op jit(solution)/shard_map/psum | solution.py:56
  270.9 13.3 %convolution_reduce_fusion.2 = f32[768]{0:T(1024)S(1)} fusion(f32[768,4096]{1,0:T(8,128)} %copy-done.1, f32[4096,1]{0,1:T(1,128)S(1)} %bitcast.27), kind=kOutput, calls=%fused_computation.19 | convolution fusion | flops 37748736 | bytes 12602368 | tf_op jit(solution)/shard_map/dot_general | solution.py:57
  284.2 41.2 %psum.81 = f32[768]{0:T(1024)S(1)} all-reduce(f32[768]{0:T(1024)S(1)} %convolution_reduce_fusion.2), channel_id=1, replica_groups=mesh['dp'=16,'proto'=16] {'proto'}, use_global_device_ids=true, to_apply=%region_9.0 | all-reduce | flops 768 | bytes 6144 | tf_op jit(solution)/shard_map/psum | solution.py:58
  325.4 8.5 fusion.20
  333.9 84.2 %psum.82 = f32[4096]{0:T(1024)S(1)} all-reduce(f32[4096]{0:T(1024)S(1)} %bitcast.28), channel_id=1, replica_groups=mesh['dp'=16,'proto'=16] {'dp'}, use_global_device_ids=true, to_apply=%region_10.0 | all-reduce | flops 4096 | bytes 32768 | tf_op jit(solution)/shard_map/psum | solution.py:56
  418.2 13.3 %convolution_reduce_fusion.1 = f32[768]{0:T(1024)S(1)} fusion(f32[768,4096]{1,0:T(8,128)} %copy-done.1, f32[4096,1]{0,1:T(1,128)S(1)} %bitcast.29), kind=kOutput, calls=%fused_computation.18 | convolution fusion | flops 37748736 | bytes 12602368 | tf_op jit(solution)/shard_map/dot_general | solution.py:57
  431.5 37.9 %psum.83 = f32[768]{0:T(1024)S(1)} all-reduce(f32[768]{0:T(1024)S(1)} %convolution_reduce_fusion.1), channel_id=1, replica_groups=mesh['dp'=16,'proto'=16] {'proto'}, use_global_device_ids=true, to_apply=%region_11.0 | all-reduce | flops 768 | bytes 6144 | tf_op jit(solution)/shard_map/psum | solution.py:58
  469.4 8.5 fusion.21
  477.9 84.1 %psum.84 = f32[4096]{0:T(1024)S(1)} all-reduce(f32[4096]{0:T(1024)S(1)} %bitcast.30), channel_id=1, replica_groups=mesh['dp'=16,'proto'=16] {'dp'}, use_global_device_ids=true, to_apply=%region_12.0 | all-reduce | flops 4096 | bytes 32768 | tf_op jit(solution)/shard_map/psum | solution.py:56
  562.1 13.4 %convolution_reduce_fusion = f32[768]{0:T(1024)S(1)} fusion(f32[768,4096]{1,0:T(8,128)} %copy-done.1, f32[4096,1]{0,1:T(1,128)S(1)} %bitcast.26), kind=kOutput, calls=%fused_computation.17 | convolution fusion | flops 37748736 | bytes 12602368 | tf_op jit(solution)/shard_map/dot_general | solution.py:57
  575.5 0.0 copy-done.3
  575.5 0.2 multiply_reduce_fusion.3
  575.7 6.0 fusion
  581.6 40.3 %all-reduce = (f32[768]{0:T(1024)S(1)}, f32[768]{0:T(1024)S(1)}) all-reduce(f32[768]{0:T(1024)S(1)} %convolution_reduce_fusion, f32[768]{0:T(1024)S(1)} %get-tuple-element.8), channel_id=1, replica_groups=mesh['dp'=16,'proto'=16] {'proto'}, use_global_device_ids=true, to_apply=%region_13.0 | all-reduce | flops 1536 | bytes 12288 | tf_op jit(solution)/shard_map/psum | solution.py:58
  622.0 9.9 multiply_convert_fusion
  631.8 0.0 copy-start.2
  631.8 2.7 copy-done.2
  634.5 2.8 fusion.7
  637.3 0.0 all-reduce.8.cloned.1.call-update
  637.3 0.3 all-reduce.6.cloned.1.call-start
  637.6 6.7 fusion.17
  644.3 0.0 all-reduce.6.cloned.1.call-update
  644.4 0.0 reduce-scatter.2.cloned.1.call-start
  644.4 147.7 %all-reduce.8.cloned.1.call-done = f32[768,256]{1,0:T(8,128)} async-done(((f32[768,256]{1,0:T(8,128)}), f32[768,256]{1,0:T(8,128)}) %all-reduce.8.cloned.1.call-update) | async-done | bytes 786448 | tf_op jit(solution)/shard_map/psum | solution.py:67
  792.1 1.4 multiply_reduce_fusion.1
  793.6 2.3 convolution_bitcast_fusion
  795.9 0.0 reduce-scatter.2.cloned.1.call-update
  795.9 234.3 %all-reduce.6.cloned.1.call-done = f32[256,4096]{1,0:T(8,128)} async-done(((f32[256,4096]{1,0:T(8,128)}), f32[256,4096]{1,0:T(8,128)}) %all-reduce.6.cloned.1.call-update) | async-done | bytes 4194320 | tf_op jit(solution)/shard_map/psum | solution.py:73
  1030.2 2.9 multiply_reduce_fusion
  1033.1 1.7 subtract_multiply_fusion
  1034.8 74.8 %reduce-scatter.2.cloned.1.call-done = f32[128,16]{0,1:T(8,128)} async-done(((f32[128,256]{0,1:T(8,128)}), f32[128,16]{0,1:T(8,128)}) %reduce-scatter.2.cloned.1.call-update) | async-done | bytes 8208 | tf_op jit(solution)/shard_map/reduce_scatter | solution.py:83
  (13 shorter events, 0.1 us)
Async XLA Ops:
  7.2 0.9 copy-start
  7.2 7.1 copy-start.4
  7.2 167.9 %all-reduce.10.cloned.1.call-start = ((), (), s32[]{:S(2)}) async-start(), calls=%async_computation.4 | async-start | bytes 3145728 | tf_op jit(solution)/shard_map/psum | solution.py:36
  12.2 780.0 %all-reduce.8.cloned.1.call-start = ((), (), s32[]{:S(2)}) async-start(), calls=%async_computation.2 | async-start | bytes 1572864 | tf_op jit(solution)/shard_map/psum | solution.py:67
  180.3 6.0 copy-start.1
  562.1 13.4 %copy-start.3 = (f32[768,256]{1,0:T(8,128)S(1)}, f32[768,256]{1,0:T(8,128)}, u32[]{:S(2)}) copy-start(f32[768,256]{1,0:T(8,128)} %get-tuple-element.5) | copy-start | bytes 2359300
  631.8 2.7 copy-start.2
  637.3 392.8 %all-reduce.6.cloned.1.call-start = ((), (), s32[]{:S(2)}) async-start(), calls=%async_computation.1 | async-start | bytes 8388608 | tf_op jit(solution)/shard_map/psum | solution.py:73
  644.4 465.3 %reduce-scatter.2.cloned.1.call-start = ((), (), s32[]{:S(2)}) async-start(), calls=%async_computation.3 | async-start | bytes 139264 | tf_op jit(solution)/shard_map/reduce_scatter | solution.py:83
Sparse Core Ops, SparseCore 0:
  12.3 162.7 all-reduce.9
  637.5 154.6 all-reduce.7
  794.8 235.3 all-reduce.5
  1034.6 74.9 reduce-scatter.1
where the time goes:
time: 1130 us; the launch traced here: 1120 us
  waiting for transfers between devices  617 us (55%)
  blocking collectives  372 us (33%)
  matrix products  88.7 us (8%)
  other arithmetic  19.9 us (2%)
  between operations  14.2 us (1%)
    psum x3, blocking collectives, on_device(): col_scale = 1.0 / lax.psum(col_part, 'dp')  253 us
    psum x1, waiting for transfers between devices, on_device(): proto_sum = lax.psum(proto_part, 'dp')  234 us
    psum x1, waiting for transfers between devices, on_device(): teach_proj, stud_proj = lax.psum((teach_part, stud_part), 'proto')  160 us
    psum x1, waiting for transfers between devices, on_device(): feat_grad = lax.psum(feat_part, 'proto')  148 us
    psum x3, blocking collectives, on_device(): row_scale = 1.0 / lax.psum(row_part, 'proto')  119 us
    reduce_scatter x1, waiting for transfers between devices, on_device(): lax.psum_scatter(bottle_part, 'dp', scatter_dimension=1, tiled=True)  74.8 us
    dot_general x3, matrix products, on_device(): row_part = jnp.dot(expo, col_scale, precision=lax.Precision.HIGHEST)  40 us
    dot_general x3, matrix products, on_device(): col_part = jnp.dot(row_scale, expo, precision=lax.Precision.HIGHEST)  23 us
  transfers between devices with their start and end apart: 4, of which 4 were waited for; matrix products, arithmetic and copies ran while one was open for 2% of the time, Pallas kernels for 0%

commit v1 on v0

v1 whole, which is shorter than its diff:
```python
import jax
import jax.numpy as jnp
from jax import lax
from jax.sharding import PartitionSpec as P

PROTOS = 65536
ITERS = 3


TEACHER_TEMP = 0.07
STUDENT_TEMP = 0.1
EPSILON = 1e-06

Y_GROUPS = [[y * 4 + z * 2 + c for y in range(4)] for z in range(2) for c in range(2)]


def unit_rows(values):
    scale = lax.rsqrt(jnp.sum(values * values, axis=1, keepdims=True) + EPSILON)
    return (values * scale, scale)


def unit_cols(weights):
    values = weights.astype(jnp.float32)
    scale = lax.rsqrt(jnp.sum(values * values, axis=0, keepdims=True) + EPSILON)
    return (values * scale, scale)


def scatter_rows(part, axis, groups=None):
    count = lax.axis_size(axis) if groups is None else len(groups[0])
    blocks = part.astype(jnp.bfloat16).reshape((count, part.shape[0] // count) + part.shape[1:])
    got = lax.all_to_all(blocks, axis, 0, 0, tiled=True, axis_index_groups=groups)
    return jnp.sum(got.astype(jnp.float32), axis=0)


def gather_all(share, axis):
    count = lax.axis_size(axis)
    copies = jnp.broadcast_to(share[None], (count,) + share.shape)
    return lax.all_to_all(copies, axis, 0, 0, tiled=True)


def gather_rows(share, axis):
    got = gather_all(share, axis)
    return got.reshape((-1,) + share.shape[1:])


def sum_over(vector, axis):
    return jnp.sum(gather_all(vector.reshape(-1, 128), axis), axis=0).reshape(vector.shape)


def on_device(
    teacher_hidden,
    student_hidden,
    teacher_bottleneck,
    student_bottleneck,
    teacher_prototypes,
    student_prototypes,
):
    teach_part = jnp.dot(teacher_hidden, teacher_bottleneck, preferred_element_type=jnp.float32)
    stud_part = jnp.dot(student_hidden, student_bottleneck, preferred_element_type=jnp.float32)
    both = jnp.concatenate([teach_part, stud_part], axis=1)
    share = scatter_rows(both, "proto")
    teach_unit, unused_scale = unit_rows(share[:, :256])
    stud_unit_rows, stud_scale_rows = unit_rows(share[:, 256:])
    low = jnp.concatenate(
        [teach_unit.astype(jnp.bfloat16), stud_unit_rows.astype(jnp.bfloat16)], axis=1
    )
    low = gather_rows(low, "proto")
    teach_low = low[:, :256]
    stud_low = low[:, 256:]
    teach_norm, unused_cols = unit_cols(teacher_prototypes)
    stud_norm, col_norm = unit_cols(student_prototypes)
    teach_wlow = teach_norm.astype(jnp.bfloat16)
    stud_wlow = stud_norm.astype(jnp.bfloat16)
    expo = jnp.exp(
        jnp.dot(teach_low, teach_wlow, preferred_element_type=jnp.float32) / TEACHER_TEMP
    )
    stud_expo = jnp.exp(
        jnp.dot(stud_low, stud_wlow, preferred_element_type=jnp.float32) / STUDENT_TEMP
    )
    totals_part = jnp.sum(stud_expo, axis=1)
    row_scale = jnp.ones((expo.shape[0],), jnp.float32)
    for step in range(ITERS):
        col_part = jnp.sum(expo * row_scale[:, None], axis=0)
        col_scale = 1.0 / sum_over(col_part, "dp")
        row_part = jnp.sum(expo * col_scale[None, :], axis=1)
        if step == 0:
            sums = sum_over(jnp.concatenate([row_part, totals_part]), "proto")
            row_scale = 1.0 / sums[: expo.shape[0]]
            totals = sums[expo.shape[0] :]
        else:
            row_scale = 1.0 / sum_over(row_part, "proto")
    factor = PROTOS / 32.0
    assign = row_scale[:, None] * expo * col_scale[None, :]
    logit_grad = (factor * (stud_expo / totals[:, None] - assign) / STUDENT_TEMP).astype(
        jnp.bfloat16
    )
    feat_part = lax.dot_general(
        logit_grad, stud_wlow, (((1,), (1,)), ((), ())), preferred_element_type=jnp.float32
    )
    proto_part = lax.dot_general(
        stud_low, logit_grad, (((0,), (0,)), ((), ())), preferred_element_type=jnp.float32
    )
    dots = jnp.sum(stud_norm * proto_part, axis=0, keepdims=True)
    grad_part = col_norm * (proto_part - stud_norm * dots)

    feat_grad = scatter_rows(feat_part, "proto")
    inner = jnp.sum(stud_unit_rows * feat_grad, axis=1, keepdims=True)
    proj_share = (stud_scale_rows * (feat_grad - stud_unit_rows * inner)).astype(jnp.bfloat16)
    proj_grad = gather_rows(proj_share, "proto")
    bottle_part = lax.dot_general(
        proj_grad, student_hidden, (((0,), (0,)), ((), ())), preferred_element_type=jnp.float32
    )
    grad_bottleneck = scatter_rows(bottle_part, "dp").T

    where = lax.axis_index("dp")
    core = where % 2
    high = (where // 2) % 2
    blocks = grad_part.reshape(4, 2, 2, 16, -1)
    keep = jnp.where(core == 0, blocks[:, :, 0], blocks[:, :, 1])
    send = jnp.where(core == 0, blocks[:, :, 1], blocks[:, :, 0]).astype(jnp.bfloat16)
    got = lax.ppermute(send, "dp", [(i, i ^ 1) for i in range(16)])
    pair = keep + got.astype(jnp.float32)
    quarter = scatter_rows(pair, "dp", Y_GROUPS)[0]
    keep = jnp.where(high == 0, quarter[0], quarter[1])
    send = jnp.where(high == 0, quarter[1], quarter[0]).astype(jnp.bfloat16)
    got = lax.ppermute(send, "dp", [(i, i ^ 2) for i in range(16)])
    grad_prototypes = keep + got.astype(jnp.float32)
    return (grad_prototypes, grad_bottleneck)


def solution(mesh):
    return jax.shard_map(
        on_device,
        mesh=mesh,
        in_specs=(
            P("dp", "proto"),
            P("dp", "proto"),
            P("proto", None),
            P("proto", None),
            P(None, "proto"),
            P(None, "proto"),
        ),
        out_specs=(P("dp", "proto"), P("proto", "dp")),
        check_vma=False,
    )
```

time: 1130 us -> 273 us (0.24); the launches traced: 1120 us -> 271 us
  waiting for transfers between devices: 617 us -> 62.9 us
  blocking collectives: 372 us -> 86.1 us
  matrix products: 88.7 us -> 23.5 us
  starting transfers between devices: 0.38 us -> 41.1 us
  other arithmetic: 19.9 us -> 51.2 us
  between operations: 14.2 us -> 0.93 us
    psum x3 -> x0, waiting for transfers between devices: 542 us -> none  [the longest x1 234 us: on_device(): proto_sum = lax.psum(proto_part, 'dp')]
    psum x6 -> x0, blocking collectives: 372 us -> none  [the longest x3 253 us: on_device(): col_scale = 1.0 / lax.psum(col_part, 'dp')]
    all_to_all x0 -> x5, blocking collectives: none -> 86.1 us  [the longest x4 57.1 us: gather_all(): return lax.all_to_all(copies, axis, 0, 0, tiled=True)]
    reduce_scatter x1 -> x0, waiting for transfers between devices: 74.8 us -> none  [on_device(): lax.psum_scatter(bottle_part, 'dp', scatter_dimension=1, tiled=True)]
    dot_general x7 -> x1, matrix products: 65.3 us -> 0.94 us  [on_device(): lax.dot_general(proj_grad, student_hidden, (((0,), (0,)), ((), ())), pref...]
    all_to_all x0 -> x7, waiting for transfers between devices: none -> 60.3 us  [the longest x4 40.1 us: gather_all(): return lax.all_to_all(copies, axis, 0, 0, tiled=True)]
    all_to_all x0 -> x7, starting transfers between devices: none -> 35.3 us  [the longest x4 23 us: gather_all(): return lax.all_to_all(copies, axis, 0, 0, tiled=True)]
    reduce_sum x2 -> x16, other arithmetic: 4.34 us -> 30.1 us  [the longest x3 16.4 us: on_device(): row_part = jnp.sum(expo * col_scale[None, :], axis=1)]
  transfers between devices with their start and end apart: 4 -> 9, of which waited for: 4 -> 8; matrix products, arithmetic and copies ran while one was open for 2% -> 7% of each run, Pallas kernels for 0% -> 0%
where the time goes in v1:
time: 273 us; the launch traced here: 271 us
  blocking collectives  86.1 us (32%)
  waiting for transfers between devices  62.9 us (23%)
  other arithmetic  51.2 us (19%)
  starting transfers between devices  41.1 us (15%)
  matrix products  23.5 us (9%)
  local copies, waits for them, and re-layouts  5.09 us (2%)
    all_to_all x4, blocking collectives, gather_all(): return lax.all_to_all(copies, axis, 0, 0, tiled=True)  57.1 us
    all_to_all x4, waiting for transfers between devices, gather_all(): return lax.all_to_all(copies, axis, 0, 0, tiled=True)  40.1 us
    all_to_all x1, blocking collectives, scatter_rows(): lax.all_to_all(blocks, axis, 0, 0, tiled=True, axis_index_groups=groups)  29 us
    all_to_all x4, starting transfers between devices, gather_all(): return lax.all_to_all(copies, axis, 0, 0, tiled=True)  23 us
    all_to_all x3, waiting for transfers between devices, scatter_rows(): lax.all_to_all(blocks, axis, 0, 0, tiled=True, axis_index_groups=groups)  20.3 us
    reduce_sum x3, other arithmetic, on_device(): row_part = jnp.sum(expo * col_scale[None, :], axis=1)  16.4 us
    reduce_sum x2, other arithmetic, on_device(): col_part = jnp.sum(expo * row_scale[:, None], axis=0)  12.4 us
    all_to_all x3, starting transfers between devices, scatter_rows(): lax.all_to_all(blocks, axis, 0, 0, tiled=True, axis_index_groups=groups)  12.3 us
  transfers between devices with their start and end apart: 9, of which 8 were waited for; matrix products, arithmetic and copies ran while one was open for 7% of the time, Pallas kernels for 0%

profile of v1, /device:TPU:32, one launch (start us, length us, event | category | flops | bytes accessed | tf_op | source)
XLA Modules:
  0.0 270.8 jit_solution(10040712946015641841)
XLA Ops:
  0.6 1.2 convolution_convert_fusion.1
  1.9 1.1 convolution_convert_fusion
  3.0 29.0 %all_to_all.60 = bf16[16,48,512]{2,1,0:T(8,128)(2,1)S(1)} all-to-all(bf16[16,48,512]{2,1,0:T(8,128)(2,1)S(1)} %pad_maximum_fusion), channel_id=1, replica_groups=mesh['dp'=16,'proto'=16] {'proto'}, dimensions={0} | all-to-all | bytes 1572864 | tf_op jit(solution)/shard_map/all_to_all | solution.py:31
  32.4 1.0 broadcast_in_dim.26
  33.3 5.1 %all-to-all-start.1 = ((bf16[16,48,512]{2,1,0:T(8,128)(2,1)}), bf16[16,48,512]{2,1,0:T(8,128)(2,1)S(1)}, u32[]{:S(2)}, u32[]{:S(2)}) async-start(bf16[16,48,512]{2,1,0:T(8,128)(2,1)} %broadcast_in_dim.26), calls=%async_computation.1 | async-start | bytes 1572864 | tf_op jit(solution)/shard_map/all_to_all | solution.py:38
  38.4 2.0 fusion.8
  40.5 0.4 fusion.7
  41.0 17.1 %all-to-all-done.1 = bf16[16,48,512]{2,1,0:T(8,128)(2,1)S(1)} async-done(((bf16[16,48,512]{2,1,0:T(8,128)(2,1)}), bf16[16,48,512]{2,1,0:T(8,128)(2,1)S(1)}, u32[]{:S(2)}, u32[]{:S(2)}) %all-to-all-start.1) | async-done | bytes 786464 | tf_op jit(solution)/shard_map/all_to_all | solution.py:38
  58.0 7.7 %fusion.29 = (f32[4096]{0:T(1024)S(1)}, f32[768,4096]{1,0:T(8,128)}) fusion(bf16[256,4096]{1,0:T(8,128)(2,1)} %param.10, f32[4096]{0:T(1024)S(1)} %add_rsqrt_fusion, bf16[768,512]{1,0:T(8,128)(2,1)S(1)} %bitcast.74), kind=kOutput, calls=%fused_computation.69 | convolution fusion | flops 1620045824 | bytes 15106048 | tf_op jit(solution)/shard_map/dot_general | solution.py:75
  65.7 0.7 broadcast_in_dim.28
  66.4 8.5 %all-to-all-start.2 = ((f32[16,32,128]{2,1,0:T(8,128)}), f32[16,32,128]{2,1,0:T(8,128)S(1)}, u32[]{:S(2)}, u32[]{:S(2)}) async-start(f32[16,32,128]{2,1,0:T(8,128)} %broadcast_in_dim.28), calls=%async_computation.2 | async-start | bytes 524288 | tf_op jit(solution)/shard_map/all_to_all | solution.py:38
  74.9 5.7 %fusion = (f32[768]{0:T(1024)S(1)}, f32[768,4096]{1,0:T(8,128)}) fusion(bf16[256,4096]{1,0:T(8,128)(2,1)S(1)} %copy-done.1, f32[4096]{0:T(1024)S(1)} %add_rsqrt_fusion.1, bf16[768,512]{1,0:T(8,128)(2,1)S(1)} %bitcast.75), kind=kOutput, calls=%fused_computation.8 | convolution fusion | flops 1620049152 | bytes 15092736 | tf_op jit(solution)/shard_map/dot_general | solution.py:78
  80.7 9.0 %all-to-all-done.2 = f32[16,32,128]{2,1,0:T(8,128)S(1)} async-done(((f32[16,32,128]{2,1,0:T(8,128)}), f32[16,32,128]{2,1,0:T(8,128)S(1)}, u32[]{:S(2)}, u32[]{:S(2)}) %all-to-all-start.2) | async-done | bytes 262176 | tf_op jit(solution)/shard_map/all_to_all | solution.py:38
  89.7 5.5 %multiply_reduce_fusion.4 = f32[768]{0:T(1024)S(1)} fusion(f32[768,4096]{1,0:T(8,128)} %get-tuple-element.11, f32[4096]{0:T(1024)S(1)} %divide_bitcast_fusion.2), kind=kLoop, calls=%fused_computation.5 | loop fusion | flops 6290688 | bytes 12602368 | tf_op jit(solution)/shard_map/reduce_sum | solution.py:85
  95.2 11.5 %all_to_all.61 = f32[16,12,128]{2,1,0:T(8,128)S(1)} all-to-all(f32[16,12,128]{2,1,0:T(8,128)S(1)} %broadcast_in_dim.29), channel_id=1, replica_groups=mesh['dp'=16,'proto'=16] {'proto'}, dimensions={0} | all-to-all | bytes 196608 | tf_op jit(solution)/shard_map/all_to_all | solution.py:38
  106.7 6.2 %multiply_reduce_fusion.3 = f32[4096]{0:T(1024)S(1)} fusion(f32[768,4096]{1,0:T(8,128)} %get-tuple-element.11, f32[768]{0:T(1024)S(1)} %get-tuple-element.7), kind=kLoop, calls=%fused_computation.4 | loop fusion | flops 6287360 | bytes 12602368 | tf_op jit(solution)/shard_map/reduce_sum | solution.py:83
  113.0 17.4 %all_to_all.62 = f32[16,32,128]{2,1,0:T(8,128)S(1)} all-to-all(f32[16,32,128]{2,1,0:T(8,128)S(1)} %broadcast_in_dim.31), channel_id=1, replica_groups=mesh['dp'=16,'proto'=16] {'dp'}, dimensions={0} | all-to-all | bytes 524288 | tf_op jit(solution)/shard_map/all_to_all | solution.py:38
  130.4 5.5 %multiply_reduce_fusion.2 = f32[768]{0:T(1024)S(1)} fusion(f32[768,4096]{1,0:T(8,128)} %get-tuple-element.11, f32[4096]{0:T(1024)S(1)} %divide_bitcast_fusion.1), kind=kLoop, calls=%fused_computation.3 | loop fusion | flops 6290688 | bytes 12602368 | tf_op jit(solution)/shard_map/reduce_sum | solution.py:85
  135.9 10.9 %all_to_all.63 = f32[16,6,128]{2,1,0:T(8,128)S(1)} all-to-all(f32[16,6,128]{2,1,0:T(8,128)S(1)} %broadcast_in_dim.33), channel_id=1, replica_groups=mesh['dp'=16,'proto'=16] {'proto'}, dimensions={0} | all-to-all | bytes 98304 | tf_op jit(solution)/shard_map/all_to_all | solution.py:38
  146.8 6.2 %multiply_reduce_fusion.1 = f32[4096]{0:T(1024)S(1)} fusion(f32[768,4096]{1,0:T(8,128)} %get-tuple-element.11, f32[768]{0:T(1024)S(1)} %divide_bitcast_fusion.4), kind=kLoop, calls=%fused_computation.2 | loop fusion | flops 6287360 | bytes 12602368 | tf_op jit(solution)/shard_map/reduce_sum | solution.py:83
  153.0 17.4 %all_to_all.64 = f32[16,32,128]{2,1,0:T(8,128)S(1)} all-to-all(f32[16,32,128]{2,1,0:T(8,128)S(1)} %broadcast_in_dim.35), channel_id=1, replica_groups=mesh['dp'=16,'proto'=16] {'dp'}, dimensions={0} | all-to-all | bytes 524288 | tf_op jit(solution)/shard_map/all_to_all | solution.py:38
  170.4 5.5 %multiply_reduce_fusion = f32[768]{0:T(1024)S(1)} fusion(f32[768,4096]{1,0:T(8,128)} %get-tuple-element.11, f32[4096]{0:T(1024)S(1)} %divide_bitcast_fusion), kind=kLoop, calls=%fused_computation.1 | loop fusion | flops 6290688 | bytes 12602368 | tf_op jit(solution)/shard_map/reduce_sum | solution.py:85
  175.9 0.6 broadcast_in_dim.37
  176.6 4.3 %all-to-all-start.7 = ((f32[16,6,128]{2,1,0:T(8,128)}), f32[16,6,128]{2,1,0:T(8,128)S(1)}, u32[]{:S(2)}, u32[]{:S(2)}) async-start(f32[16,6,128]{2,1,0:T(8,128)} %broadcast_in_dim.37), calls=%async_computation.7 | async-start | bytes 131072 | tf_op jit(solution)/shard_map/all_to_all | solution.py:38
  180.9 6.6 %all-to-all-done.7 = f32[16,6,128]{2,1,0:T(8,128)S(1)} async-done(((f32[16,6,128]{2,1,0:T(8,128)}), f32[16,6,128]{2,1,0:T(8,128)S(1)}, u32[]{:S(2)}, u32[]{:S(2)}) %all-to-all-start.7) | async-done | bytes 49184 | tf_op jit(solution)/shard_map/all_to_all | solution.py:38
  187.5 9.9 %multiply_convert_fusion = bf16[768,4096]{1,0:T(8,128)(2,1)S(1)} fusion(f32[768,4096]{1,0:T(8,128)} %get-tuple-element.11, f32[768,4096]{1,0:T(8,128)} %get-tuple-element.9, f32[768]{0:T(1024)S(1)} %divide_bitcast_fusion.3, f32[4096]{0:T(1024)S(1)} %divide_bitcast_fusion, f32[768]{0:T(1024)S(1)} %get-tuple-element.6), kind=kLoop, calls=%fused_computation | loop fusion | flops 22020096 | bytes 31479808 | tf_op jit(solution)/shard_map/convert_element_type | solution.py:94
  197.4 2.7 fusion.17
  200.0 4.2 %fusion.4 = (f32[4096]{0:T(1024)S(1)}, f32[256,4096]{1,0:T(8,128)}) fusion(bf16[256,4096]{1,0:T(8,128)(2,1)S(1)} %copy-done.1, f32[4096]{0:T(1024)S(1)} %add_rsqrt_fusion.1, bf16[768,4096]{1,0:T(8,128)(2,1)S(1)} %multiply_convert_fusion, bf16[768,512]{1,0:T(8,128)(2,1)S(1)} %bitcast.76), kind=kOutput, calls=%fused_computation.16 | convolution fusion | flops 1614802944 | bytes 13008896 | tf_op jit(solution)/shard_map/dot_general | solution.py:100
  204.2 5.2 %all-to-all-start.9 = ((bf16[16,48,256]{2,1,0:T(8,128)(2,1)}), bf16[16,48,256]{2,1,0:T(8,128)(2,1)S(1)}, u32[]{:S(2)}, u32[]{:S(2)}) async-start(bf16[16,48,256]{2,1,0:T(8,128)(2,1)} %bitcast.82), calls=%async_computation.9 | async-start | bytes 786432 | tf_op jit(solution)/shard_map/all_to_all | solution.py:31
  209.5 2.9 %fusion.6 = f32[256,4096]{1,0:T(8,128)S(1)} fusion(f32[256,4096]{1,0:T(8,128)} %get-tuple-element.13, bf16[256,4096]{1,0:T(8,128)(2,1)S(1)} %copy-done.1, f32[4096]{0:T(1024)S(1)} %get-tuple-element.12, f32[4096]{0:T(1024)S(1)} %add_rsqrt_fusion.1), kind=kLoop, calls=%fused_computation.18 | loop fusion | flops 5242880 | bytes 10518528 | tf_op jit(solution)/shard_map/mul | solution.py:104
  212.4 1.9 copy-done.2
  214.3 1.2 fusion.20
  215.5 4.6 %all-to-all-done.9 = bf16[16,48,256]{2,1,0:T(8,128)(2,1)S(1)} async-done(((bf16[16,48,256]{2,1,0:T(8,128)(2,1)}), bf16[16,48,256]{2,1,0:T(8,128)(2,1)S(1)}, u32[]{:S(2)}, u32[]{:S(2)}) %all-to-all-start.9) | async-done | bytes 393248 | tf_op jit(solution)/shard_map/all_to_all | solution.py:31
  220.2 0.2 multiply_reduce_fusion.5
  220.5 0.8 broadcast_in_dim.38
  221.2 5.1 %all-to-all-start.10 = ((bf16[16,48,256]{2,1,0:T(8,128)(2,1)}), bf16[16,48,256]{2,1,0:T(8,128)(2,1)S(1)}, u32[]{:S(2)}, u32[]{:S(2)}) async-start(bf16[16,48,256]{2,1,0:T(8,128)(2,1)} %broadcast_in_dim.38), calls=%async_computation.10 | async-start | bytes 786432 | tf_op jit(solution)/shard_map/all_to_all | solution.py:38
  226.3 3.5 %fusion.21 = bf16[4,1,2,16,4096]{4,3,2,1,0:T(8,128)(2,1)} fusion(bf16[4,2,16,4096]{3,2,1,0:T(8,128)(2,1)S(1)} %collective-permute-done, f32[4,2,2,16,4096]{4,3,2,1,0:T(8,128)} %bitcast.73, pred[]{:T(512)S(6)} %eq.12), kind=kLoop, calls=%fused_computation.37 | loop fusion | flops 2097152 | bytes 6291457 | tf_op jit(solution)/shard_map/reshape | solution.py:30
  229.9 7.4 %all-to-all-done.10 = bf16[16,48,256]{2,1,0:T(8,128)(2,1)S(1)} async-done(((bf16[16,48,256]{2,1,0:T(8,128)(2,1)}), bf16[16,48,256]{2,1,0:T(8,128)(2,1)S(1)}, u32[]{:S(2)}, u32[]{:S(2)}) %all-to-all-start.10) | async-done | bytes 393248 | tf_op jit(solution)/shard_map/all_to_all | solution.py:38
  237.2 3.5 %all-to-all-start.8 = ((bf16[4,1,2,16,4096]{4,3,2,1,0:T(8,128)(2,1)}), bf16[4,1,2,16,4096]{4,3,2,1,0:T(8,128)(2,1)S(1)}, u32[]{:S(2)}, u32[]{:S(2)}) async-start(bf16[4,1,2,16,4096]{4,3,2,1,0:T(8,128)(2,1)} %fusion.21), calls=%async_computation.8 | async-start | bytes 2097152 | tf_op jit(solution)/shard_map/all_to_all | solution.py:31
  240.8 0.9 convolution_convert_fusion.2
  241.7 11.3 %all-to-all-done.8 = bf16[4,1,2,16,4096]{4,3,2,1,0:T(8,128)(2,1)S(1)} async-done(((bf16[4,1,2,16,4096]{4,3,2,1,0:T(8,128)(2,1)}), bf16[4,1,2,16,4096]{4,3,2,1,0:T(8,128)(2,1)S(1)}, u32[]{:S(2)}, u32[]{:S(2)}) %all-to-all-start.8) | async-done | bytes 1048608 | tf_op jit(solution)/shard_map/all_to_all | solution.py:31
  253.1 3.5 %all-to-all-start.11 = ((bf16[16,16,128]{2,1,0:T(8,128)(2,1)}), bf16[16,16,128]{2,1,0:T(8,128)(2,1)S(1)}, u32[]{:S(2)}, u32[]{:S(2)}) async-start(bf16[16,16,128]{2,1,0:T(8,128)(2,1)} %bitcast.26), calls=%async_computation.11 | async-start | bytes 131072 | tf_op jit(solution)/shard_map/all_to_all | solution.py:31
  256.6 0.2 convert_reduce_fusion
  256.8 5.8 %collective-permute-start.1 = (bf16[16,4096]{1,0:T(8,128)(2,1)S(1)}, bf16[16,4096]{1,0:T(8,128)(2,1)S(1)}, u32[]{:S(2)}, u32[]{:S(2)}) collective-permute-start(bf16[16,4096]{1,0:T(8,128)(2,1)S(1)} %fusion.26), channel_id=1, source_target_pairs={{0,32},{16,48},{32,0},{48,16},{64,96},{80,112},{96,64},{112,80},{1... | collective-permute-start | bytes 393224 | tf_op jit(solution)/shard_map/ppermute | solution.py:126
  262.6 4.3 %all-to-all-done.11 = bf16[16,16,128]{2,1,0:T(8,128)(2,1)S(1)} async-done(((bf16[16,16,128]{2,1,0:T(8,128)(2,1)}), bf16[16,16,128]{2,1,0:T(8,128)(2,1)S(1)}, u32[]{:S(2)}, u32[]{:S(2)}) %all-to-all-start.11) | async-done | bytes 65568 | tf_op jit(solution)/shard_map/all_to_all | solution.py:31
  266.9 0.6 convert_reduce_fusion.3
  267.5 2.5 collective-permute-done.1
  270.0 0.7 bitcast_add_fusion.1
  (35 shorter events, 0.9 us)
Async XLA Ops:
  0.6 1.2 copy-start
  3.0 37.5 %copy-start.1 = (bf16[256,4096]{1,0:T(8,128)(2,1)S(1)}, bf16[256,4096]{1,0:T(8,128)(2,1)}, u32[]{:S(2)}) copy-start(bf16[256,4096]{1,0:T(8,128)(2,1)} %param.11) | copy-start | bytes 6291460
  33.3 24.7 %all-to-all-start.1 = ((bf16[16,48,512]{2,1,0:T(8,128)(2,1)}), bf16[16,48,512]{2,1,0:T(8,128)(2,1)S(1)}, u32[]{:S(2)}, u32[]{:S(2)}) async-start(bf16[16,48,512]{2,1,0:T(8,128)(2,1)} %broadcast_in_dim.26), calls=%async_computation.1 | async-start | bytes 1572864 | tf_op jit(solution)/shard_map/all_to_all | solution.py:38
  66.4 23.2 %all-to-all-start.2 = ((f32[16,32,128]{2,1,0:T(8,128)}), f32[16,32,128]{2,1,0:T(8,128)S(1)}, u32[]{:S(2)}, u32[]{:S(2)}) async-start(f32[16,32,128]{2,1,0:T(8,128)} %broadcast_in_dim.28), calls=%async_computation.2 | async-start | bytes 524288 | tf_op jit(solution)/shard_map/all_to_all | solution.py:38
  176.6 10.9 %all-to-all-start.7 = ((f32[16,6,128]{2,1,0:T(8,128)}), f32[16,6,128]{2,1,0:T(8,128)S(1)}, u32[]{:S(2)}, u32[]{:S(2)}) async-start(f32[16,6,128]{2,1,0:T(8,128)} %broadcast_in_dim.37), calls=%async_computation.7 | async-start | bytes 131072 | tf_op jit(solution)/shard_map/all_to_all | solution.py:38
  204.2 15.9 %all-to-all-start.9 = ((bf16[16,48,256]{2,1,0:T(8,128)(2,1)}), bf16[16,48,256]{2,1,0:T(8,128)(2,1)S(1)}, u32[]{:S(2)}, u32[]{:S(2)}) async-start(bf16[16,48,256]{2,1,0:T(8,128)(2,1)} %bitcast.82), calls=%async_computation.9 | async-start | bytes 786432 | tf_op jit(solution)/shard_map/all_to_all | solution.py:31
  212.4 1.9 copy-start.2
  215.5 10.8 %collective-permute-start = (bf16[4,2,16,4096]{3,2,1,0:T(8,128)(2,1)}, bf16[4,2,16,4096]{3,2,1,0:T(8,128)(2,1)S(1)}, u32[]{:S(2)}, u32[]{:S(2)}) collective-permute-start(bf16[4,2,16,4096]{3,2,1,0:T(8,128)(2,1)} %fusion.20), channel_id=1, source_target_pairs={{0,16},{16,0},{32,48},{48,32},{64,80},{80,64},{96,112},{112,96},{1... | collective-permute-start | bytes 3145736 | tf_op jit(solution)/shard_map/ppermute | solution.py:121
  221.2 16.0 %all-to-all-start.10 = ((bf16[16,48,256]{2,1,0:T(8,128)(2,1)}), bf16[16,48,256]{2,1,0:T(8,128)(2,1)S(1)}, u32[]{:S(2)}, u32[]{:S(2)}) async-start(bf16[16,48,256]{2,1,0:T(8,128)(2,1)} %broadcast_in_dim.38), calls=%async_computation.10 | async-start | bytes 786432 | tf_op jit(solution)/shard_map/all_to_all | solution.py:38
  237.2 15.8 %all-to-all-start.8 = ((bf16[4,1,2,16,4096]{4,3,2,1,0:T(8,128)(2,1)}), bf16[4,1,2,16,4096]{4,3,2,1,0:T(8,128)(2,1)S(1)}, u32[]{:S(2)}, u32[]{:S(2)}) async-start(bf16[4,1,2,16,4096]{4,3,2,1,0:T(8,128)(2,1)} %fusion.21), calls=%async_computation.8 | async-start | bytes 2097152 | tf_op jit(solution)/shard_map/all_to_all | solution.py:31
  253.1 13.8 %all-to-all-start.11 = ((bf16[16,16,128]{2,1,0:T(8,128)(2,1)}), bf16[16,16,128]{2,1,0:T(8,128)(2,1)S(1)}, u32[]{:S(2)}, u32[]{:S(2)}) async-start(bf16[16,16,128]{2,1,0:T(8,128)(2,1)} %bitcast.26), calls=%async_computation.11 | async-start | bytes 131072 | tf_op jit(solution)/shard_map/all_to_all | solution.py:31
  256.8 13.2 %collective-permute-start.1 = (bf16[16,4096]{1,0:T(8,128)(2,1)S(1)}, bf16[16,4096]{1,0:T(8,128)(2,1)S(1)}, u32[]{:S(2)}, u32[]{:S(2)}) collective-permute-start(bf16[16,4096]{1,0:T(8,128)(2,1)S(1)} %fusion.26), channel_id=1, source_target_pairs={{0,32},{16,48},{32,0},{48,16},{64,96},{80,112},{96,64},{112,80},{1... | collective-permute-start | bytes 393224 | tf_op jit(solution)/shard_map/ppermute | solution.py:126

commit v2 on v0

v2 whole, which is shorter than its diff:
```python
import jax
import jax.numpy as jnp
from jax import lax
from jax.experimental import pallas as pl
from jax.experimental.pallas import tpu as pltpu
from jax.sharding import PartitionSpec as P

PROTOS = 65536
ITERS = 3

TEACHER_TEMP = 0.07
STUDENT_TEMP = 0.1
EPSILON = 1e-06
LOG2E = 1.4426950408889634

LANES = 128
WIDE = 512
LIMIT = 16 * 2**20
KEEP = jnp.float32
BLOCK = 16


def unit_rows(values):
    scale = lax.rsqrt(jnp.sum(values * values, axis=1, keepdims=True) + EPSILON)
    return (values * scale, scale)


def col_scales(weights):
    values = weights.astype(jnp.float32)
    return lax.rsqrt(jnp.sum(values * values, axis=0, keepdims=True) + EPSILON)


def on_core(kernel, outs, args, scratch=(), pinned=(), smem=(), far=(), far_outs=()):
    args = [
        pltpu.with_memory_space_constraint(a, pltpu.VMEM if i in pinned else pltpu.HBM)
        if i in pinned or i in far
        else a
        for i, a in enumerate(args)
    ]

    def place(i, far_ones):
        return pl.BlockSpec(memory_space=pltpu.HBM if i in far_ones else pltpu.VMEM)

    return pl.pallas_call(
        kernel,
        out_shape=tuple(outs),
        in_specs=[
            pl.BlockSpec(memory_space=pltpu.SMEM) if i in smem else place(i, far)
            for i in range(len(args))
        ],
        out_specs=tuple(place(i, far_outs) for i in range(len(outs))),
        scratch_shapes=list(scratch),
        compiler_params=pltpu.CompilerParams(vmem_limit_bytes=LIMIT),
    )(*args)


def fetch(far_ref, near_ref, sems):
    copies = []
    for k in range(far_ref.shape[1] // WIDE):
        cols = pl.ds(k * WIDE, WIDE)
        copies.append(pltpu.make_async_copy(far_ref.at[:, cols], near_ref.at[:, cols], sems.at[k]))
        copies[-1].start()
    return copies


def column_of(rows, j):
    return jnp.broadcast_to(rows[j : j + 1, :], (LANES, LANES)).T


def put_row_sums(acc_ref, out_ref, sums_ref):
    sums_ref[...] = jnp.zeros_like(sums_ref)
    for j in range(acc_ref.shape[0] // LANES):
        sums_ref[pl.ds(j, 1), :] = jnp.sum(
            acc_ref[pl.ds(j * LANES, LANES), :].T, axis=0, keepdims=True
        )
    sums = sums_ref[...]
    high = sums.astype(jnp.bfloat16).astype(jnp.float32)
    block = jnp.concatenate([high, sums - high], axis=0).astype(jnp.bfloat16)
    for p in range(out_ref.shape[0]):
        out_ref[p, pl.ds(0, BLOCK), :] = block


def get_row_sums(got_ref, first):
    terms = jnp.sum(got_ref[:, pl.ds(first, BLOCK), :].astype(jnp.float32), axis=0)
    return terms[:8] + terms[8:]


def diagonal(rows, columns):
    shape = (rows, columns)
    return lax.broadcasted_iota(jnp.int32, shape, 0) == lax.broadcasted_iota(jnp.int32, shape, 1)


def share_kernel(got_ref, out_ref):
    unit, unused_scale = unit_rows(jnp.sum(got_ref[...].astype(jnp.float32), axis=0))
    unit = unit.astype(out_ref.dtype)
    for p in range(out_ref.shape[0]):
        out_ref[p] = unit


def proj_kernel(got_ref, share_ref, out_ref):
    unit, scale = unit_rows(share_ref[...])
    share, width = unit.shape
    got = jnp.sum(got_ref[...].astype(jnp.float32), axis=0)
    along = jnp.where(diagonal(share, width), got[share : share + 1], 0.0)
    low = unit.astype(jnp.bfloat16).astype(jnp.float32)
    feat = got[:share] + low * jnp.sum(along, axis=1, keepdims=True)
    inner = jnp.sum(unit * feat, axis=1, keepdims=True)
    rows = (scale * (feat - unit * inner)).astype(out_ref.dtype)
    for p in range(out_ref.shape[0]):
        out_ref[p] = rows


def teacher_kernel(low_ref, w_far, expo_ref, out_ref, w_ref, sems, sums_ref):
    loads = fetch(w_far, w_ref, sems)
    low = low_ref[...]
    for k in range(w_ref.shape[1] // WIDE):
        cols = pl.ds(k * WIDE, WIDE)
        loads[k].wait()
        scores = jnp.dot(low, w_ref[:, cols], preferred_element_type=jnp.float32)
        expo = jnp.exp2(scores * (LOG2E / TEACHER_TEMP))
        expo_ref[:, cols] = expo.astype(expo_ref.dtype)
        sums = jnp.sum(expo, axis=0, keepdims=True)
        for t in range(WIDE // LANES):
            sums_ref[pl.ds(k * (WIDE // LANES) + t, 1), :] = sums[:, t * LANES : (t + 1) * LANES]
    sums = sums_ref[...].astype(out_ref.dtype)
    for p in range(out_ref.shape[0]):
        out_ref[p] = sums


def student_kernel(got_ref, w_ref, expo_ref, totals_ref, low_ref, acc_ref, sums_ref):
    share = (got_ref.shape[1] - BLOCK) // 2
    for p in range(got_ref.shape[0]):
        for half in range(2):
            low_ref[pl.ds(p * share, share), pl.ds(half * LANES, LANES)] = got_ref[
                p, pl.ds(BLOCK + half * share, share), :
            ]
    low = low_ref[...]
    for k in range(w_ref.shape[1] // WIDE):
        cols = pl.ds(k * WIDE, WIDE)
        scores = jnp.dot(low, w_ref[:, cols], preferred_element_type=jnp.float32)
        expo = jnp.exp2(scores * (LOG2E / STUDENT_TEMP))
        expo_ref[:, cols] = expo.astype(expo_ref.dtype)
        part = sum(expo[:, t * LANES : (t + 1) * LANES] for t in range(WIDE // LANES))
        acc_ref[...] = part if k == 0 else acc_ref[...] + part
    put_row_sums(acc_ref, totals_ref, sums_ref)


def row_kernel(expo_ref, got_ref, *refs):
    extra_ref = refs[0] if len(refs) == 5 else None
    out_ref, scale_ref, acc_ref, sums_ref = refs[-4:]
    rows, columns = expo_ref.shape
    scale_ref[...] = 1.0 / jnp.sum(got_ref[...].astype(jnp.float32), axis=0)
    block = 64

    def body(i, _):
        at = pl.multiple_of(i * block, block)
        acc = [jnp.zeros((8, LANES), jnp.float32)] * (block // 8)
        for t in range(columns // LANES):
            scale = jnp.broadcast_to(scale_ref[pl.ds(t, 1), :], (8, LANES))
            for r in range(block // 16):
                piece = expo_ref[pl.ds(at + r * 16, 16), pl.ds(t * LANES, LANES)].astype(jnp.float32)
                acc[2 * r] += piece[:8] * scale
                acc[2 * r + 1] += piece[8:] * scale
        for r in range(block // 8):
            acc_ref[pl.ds(at + r * 8, 8), :] = acc[r]
        return 0

    lax.fori_loop(0, rows // block, body, 0)
    put_row_sums(acc_ref, out_ref, sums_ref)
    if extra_ref is not None and len(extra_ref.shape) == 3:
        for p in range(out_ref.shape[0]):
            out_ref[p, pl.ds(BLOCK, BLOCK), :] = extra_ref[0]
    elif extra_ref is not None:
        unit, unused_scale = unit_rows(extra_ref[...])
        unit = unit.astype(out_ref.dtype)
        share = unit.shape[0]
        for p in range(out_ref.shape[0]):
            out_ref[p, pl.ds(BLOCK, share), :] = unit[:, :LANES]
            out_ref[p, pl.ds(BLOCK + share, share), :] = unit[:, LANES:]


def col_kernel(expo_ref, got_ref, out_ref, scale_ref, sums_ref):
    rows, columns = expo_ref.shape
    scale = 1.0 / get_row_sums(got_ref, 0)
    for j in range(rows // LANES):
        scale_ref[pl.ds(j * LANES, LANES), :] = column_of(scale, j)
    tiles = 8

    for k in range(columns // (tiles * LANES)):

        def body(i, acc):
            acc = list(acc)
            at = pl.multiple_of(i * 64, 64)
            for r in range(4):
                weight = scale_ref[pl.ds(at + r * 16, 16), :]
                for t in range(tiles):
                    lanes = pl.ds((k * tiles + t) * LANES, LANES)
                    piece = expo_ref[pl.ds(at + r * 16, 16), lanes].astype(jnp.float32) * weight
                    acc[t] += piece[:8] + piece[8:]
            return tuple(acc)

        acc = lax.fori_loop(
            0, rows // 64, body, tuple(jnp.zeros((8, LANES), jnp.float32) for _ in range(tiles))
        )
        for t in range(tiles):
            sums_ref[pl.ds(k * tiles + t, 1), :] = jnp.sum(acc[t], axis=0, keepdims=True)
    sums = sums_ref[...].astype(out_ref.dtype)
    for p in range(out_ref.shape[0]):
        out_ref[p] = sums


def grad_kernel(
    core_ref, expo_ref, stud_ref, low_ref, wlow_ref, raw_ref, norm_ref, cols_ref, rows_ref,
    feat_far, keep_far, send_far, feat_ref, keep_ref, send_ref, out_sems,
    assign_ref, prob_ref, colscale_ref, acc_ref,
):
    rows, columns = expo_ref.shape
    factor = PROTOS / 32.0 / STUDENT_TEMP
    by_row = 1.0 / get_row_sums(rows_ref, 0)
    by_total = 1.0 / get_row_sums(rows_ref, BLOCK)
    colscale_ref[...] = 1.0 / jnp.sum(cols_ref[...].astype(jnp.float32), axis=0)
    for j in range(rows // LANES):
        at = pl.ds(j * LANES, LANES)
        assign_ref[at, :] = column_of(by_row, j) * factor
        prob_ref[at, :] = column_of(by_total, j) * factor
    core = core_ref[0]
    low = low_ref[...]
    stores = []
    for k in range(columns // WIDE):
        cols = pl.ds(k * WIDE, WIDE)
        pieces = []
        for t in range(WIDE // LANES):
            at = pl.ds(k * WIDE + t * LANES, LANES)
            scale = colscale_ref[pl.ds(k * (WIDE // LANES) + t, 1), :]
            pieces.append(
                (
                    stud_ref[:, at].astype(jnp.float32) * prob_ref[...]
                    - assign_ref[...] * (expo_ref[:, at].astype(jnp.float32) * scale)
                ).astype(jnp.bfloat16)
            )
        grad = jnp.concatenate(pieces, axis=1)
        feat = lax.dot_general(
            grad, wlow_ref[:, cols], (((1,), (1,)), ((), ())), preferred_element_type=jnp.float32
        )
        acc_ref[...] = feat if k == 0 else acc_ref[...] + feat
        proto = lax.dot_general(
            low, grad, (((0,), (0,)), ((), ())), preferred_element_type=jnp.float32
        )
        norm = norm_ref[:, cols]
        unit = raw_ref[:, cols].astype(jnp.float32) * norm
        dots = jnp.sum(unit * proto, axis=0, keepdims=True)
        part = norm * (proto - unit * dots)
        part = part.reshape(8, 2, 16, WIDE)
        slot = k % 2
        if k >= 2:
            for copy in stores[k - 2]:
                copy.wait()
        keep_ref[slot] = jnp.where(core == 0, part[:, 0], part[:, 1])
        send_ref[slot] = jnp.where(core == 0, part[:, 1], part[:, 0]).astype(jnp.bfloat16)
        stores.append(
            (
                pltpu.make_async_copy(
                    keep_ref.at[slot], keep_far.at[:, :, cols], out_sems.at[0, slot]
                ),
                pltpu.make_async_copy(
                    send_ref.at[slot], send_far.at[:, :, cols], out_sems.at[1, slot]
                ),
            )
        )
        for copy in stores[k]:
            copy.start()
    low = low.astype(jnp.float32)
    feat = acc_ref[...]
    inner = jnp.sum(low * feat, axis=1, keepdims=True)
    feat = (feat - low * inner).astype(jnp.bfloat16)
    count = feat_ref.shape[0]
    share = rows // count
    spot = diagonal(share, feat.shape[1])
    for p in range(count):
        mine = slice(p * share, (p + 1) * share)
        feat_ref[p, pl.ds(0, share), :] = feat[mine]
        along = jnp.sum(jnp.where(spot, inner[mine], 0.0), axis=0, keepdims=True)
        feat_ref[p, pl.ds(share, BLOCK), :] = jnp.broadcast_to(
            along, (BLOCK, feat.shape[1])
        ).astype(jnp.bfloat16)
    last = pltpu.make_async_copy(feat_ref, feat_far, out_sems.at[2, 0])
    last.start()
    for pair in stores[-2:]:
        for copy in pair:
            copy.wait()
    last.wait()


def exchange(copies, axis):
    return lax.all_to_all(copies, axis, 0, 0, tiled=True)


def spread_sum(parts, axis, dim, me, target, dtype=jnp.float32):
    total = lax.dynamic_index_in_dim(parts, me, dim, keepdims=False)
    for hop in (2, 1, 3):
        part = lax.dynamic_index_in_dim(parts, (me + hop) % 4, dim, keepdims=False).astype(dtype)
        got = lax.ppermute(part, axis, [(i, target(i, hop)) for i in range(16)])
        total = total + got.astype(jnp.float32)
    return total


def on_device(
    teacher_hidden,
    student_hidden,
    teacher_bottleneck,
    student_bottleneck,
    teacher_prototypes,
    student_prototypes,
):
    f32, bf16 = jnp.float32, jnp.bfloat16
    shape = jax.ShapeDtypeStruct
    rows = teacher_hidden.shape[0]
    columns = teacher_prototypes.shape[1]
    width = teacher_prototypes.shape[0]
    row_tiles, col_tiles = rows // LANES, columns // LANES
    n_dp, n_proto = lax.axis_size("dp"), lax.axis_size("proto")

    def blocks_of(part, count):
        return part.astype(bf16).reshape(count, part.shape[0] // count, part.shape[1])

    teach_part = jnp.dot(teacher_hidden, teacher_bottleneck, preferred_element_type=f32)
    got = exchange(blocks_of(teach_part, n_proto), "proto")

    me, where = lax.axis_index("proto"), lax.axis_index("dp")
    core, high, y_at = jnp.reshape(where % 2, (1,)), (where // 2) % 2, where // 4
    share = rows // n_proto
    teach_norm = col_scales(teacher_prototypes)
    stud_norm = col_scales(student_prototypes)
    teach_norm, stud_norm, stud_early = lax.optimization_barrier(
        (teach_norm, stud_norm, student_hidden)
    )
    stud_part = jnp.dot(stud_early, student_bottleneck, preferred_element_type=f32)
    stud_part = stud_part.reshape(4, 4, share, width)
    stud_line = spread_sum(stud_part, "proto", 1, me % 4, lambda i, hop: i // 4 * 4 + (i + hop) % 4)

    (copies,) = on_core(share_kernel, [shape(got.shape, bf16)], (got,))
    copies, teach_norm, stud_norm = lax.optimization_barrier((copies, teach_norm, stud_norm))
    teach_low = exchange(copies, "proto").reshape(rows, width)
    teach_wlow = (teacher_prototypes.astype(f32) * teach_norm).astype(bf16)
    teach_wlow, stud_line, stud_norm = lax.optimization_barrier((teach_wlow, stud_line, stud_norm))
    stud_wlow = (student_prototypes.astype(f32) * stud_norm).astype(bf16)
    stud_share = spread_sum(stud_line, "proto", 0, me // 4, lambda i, hop: (i + 4 * hop) % 16)

    teach_low, teach_wlow, stud_norm, stud_wlow, stud_share, core, high, y_at = (
        lax.optimization_barrier(
            (teach_low, teach_wlow, stud_norm, stud_wlow, stud_share, core, high, y_at)
        )
    )

    big = pltpu.VMEM((rows, columns), KEEP)
    chunks = columns // WIDE
    weights = [pltpu.VMEM((width, columns), bf16), pltpu.SemaphoreType.DMA((chunks,))]
    row_acc = [pltpu.VMEM((rows, LANES), f32), pltpu.VMEM((8, LANES), f32)]
    col_sums = pltpu.VMEM((col_tiles, LANES), f32)
    expo, copies = on_core(
        teacher_kernel,
        [big, shape((n_dp, col_tiles, LANES), bf16)],
        (teach_low, teach_wlow),
        scratch=weights + [col_sums],
        far=(1,),
    )
    for step in range(ITERS):
        got_cols = exchange(copies, "dp")
        count, extra = BLOCK, ()
        if step == ITERS - 2:
            count, extra = BLOCK + 2 * share, (stud_share,)
        if step == ITERS - 1:
            got_rows, got_cols = lax.optimization_barrier((got_rows, got_cols))
            stud_expo, totals, stud_low = on_core(
                student_kernel,
                [
                    pltpu.VMEM((rows, columns), bf16),
                    shape((1, BLOCK, LANES), bf16),
                    shape((rows, width), bf16),
                ],
                (got_rows, stud_wlow),
                scratch=row_acc,
            )
            count, extra = 2 * BLOCK, (totals,)
        (copies,) = on_core(
            row_kernel,
            [shape((n_proto, count, LANES), bf16)],
            (expo, got_cols) + extra,
            scratch=[col_sums] + row_acc,
            pinned=(0,),
        )
        got_rows = exchange(copies, "proto")
        if step < ITERS - 1:
            (copies,) = on_core(
                col_kernel,
                [shape((n_dp, col_tiles, LANES), bf16)],
                (expo, got_rows),
                scratch=[pltpu.VMEM((rows, LANES), f32), col_sums],
                pinned=(0,),
            )

    feat_part, keep, send = on_core(
        grad_kernel,
        [
            pltpu.HBM((n_proto, share + BLOCK, width), bf16),
            pltpu.HBM((8, 16, columns), f32),
            pltpu.HBM((8, 16, columns), bf16),
        ],
        (
            core, expo, stud_expo, stud_low, stud_wlow,
            student_prototypes, stud_norm, got_cols, got_rows,
        ),
        scratch=[
            pltpu.VMEM((n_proto, share + BLOCK, width), bf16),
            pltpu.VMEM((2, 8, 16, WIDE), f32),
            pltpu.VMEM((2, 8, 16, WIDE), bf16),
            pltpu.SemaphoreType.DMA((3, 2)),
            pltpu.VMEM((rows, LANES), f32),
            pltpu.VMEM((rows, LANES), f32),
            pltpu.VMEM((col_tiles, LANES), f32),
            pltpu.VMEM((rows, width), f32),
        ],
        pinned=(1, 2),
        smem=(0,),
        far_outs=(0, 1, 2),
    )

    got = exchange(feat_part, "proto")
    (copies,) = on_core(proj_kernel, [shape((n_proto, share, width), bf16)], (got, stud_share))
    proj_grad = exchange(copies, "proto").reshape(rows, width)
    bottle_part = lax.dot_general(
        proj_grad, student_hidden, (((0,), (0,)), ((), ())), preferred_element_type=f32
    )
    got_bottle = exchange(blocks_of(bottle_part, n_dp), "dp")
    grad_bottleneck = jnp.sum(got_bottle.astype(f32), axis=0).T

    got = lax.ppermute(send, "dp", [(i, i ^ 1) for i in range(16)])
    pair = (keep + got.astype(f32)).reshape(4, 2, 16, columns)
    quarter = spread_sum(pair, "dp", 0, y_at, lambda i, hop: (i + 4 * hop) % 16, bf16)
    keep = jnp.where(high == 0, quarter[0], quarter[1])
    send = jnp.where(high == 0, quarter[1], quarter[0]).astype(bf16)
    got = lax.ppermute(send, "dp", [(i, i ^ 2) for i in range(16)])
    grad_prototypes = keep + got.astype(f32)
    return (grad_prototypes, grad_bottleneck)


def solution(mesh):
    return jax.shard_map(
        on_device,
        mesh=mesh,
        in_specs=(
            P("dp", "proto"),
            P("dp", "proto"),
            P("proto", None),
            P("proto", None),
            P(None, "proto"),
            P(None, "proto"),
        ),
        out_specs=(P("dp", "proto"), P("proto", "dp")),
        check_vma=False,
    )
```

time: 1130 us -> 229 us (0.20); the launches traced: 1120 us -> 227 us
  waiting for transfers between devices: 617 us -> 51.8 us
  blocking collectives: 372 us -> 89.1 us
  matrix products: 88.7 us -> 4.1 us
  starting transfers between devices: 0.38 us -> 43.3 us
  Pallas kernels: 0 us -> 21.8 us
  between operations: 14.2 us -> 0.93 us
    psum x3 -> x0, waiting for transfers between devices: 542 us -> none  [the longest x1 234 us: on_device(): proto_sum = lax.psum(proto_part, 'dp')]
    psum x6 -> x0, blocking collectives: 372 us -> none  [the longest x3 253 us: on_device(): col_scale = 1.0 / lax.psum(col_part, 'dp')]
    all_to_all x0 -> x6, blocking collectives: none -> 89.1 us  [exchange(): return lax.all_to_all(copies, axis, 0, 0, tiled=True)]
    dot_general x13 -> x3, matrix products: 88.7 us -> 4.1 us  [the longest x1 2.08 us: on_device(): jnp.dot(teacher_hidden, teacher_bottleneck, preferred_element_type=f32)]
    reduce_scatter x1 -> x0, waiting for transfers between devices: 74.8 us -> none  [on_device(): lax.psum_scatter(bottle_part, 'dp', scatter_dimension=1, tiled=True)]
    all_to_all x0 -> x5, waiting for transfers between devices: none -> 44 us  [exchange(): return lax.all_to_all(copies, axis, 0, 0, tiled=True)]
    all_to_all x0 -> x5, starting transfers between devices: none -> 29.2 us  [exchange(): return lax.all_to_all(copies, axis, 0, 0, tiled=True)]
    pallas_call x0 -> x10, Pallas kernels: none -> 21.8 us  [on_core(): pl.pallas_call(kernel, out_shape=tuple(outs), in_specs=[pl.BlockSpec(memo...]
  transfers between devices with their start and end apart: 4 -> 16, of which waited for: 4 -> 6; matrix products, arithmetic and copies ran while one was open for 2% -> 6% of each run, Pallas kernels for 0% -> 0%
where the time goes in v2:
time: 229 us; the launch traced here: 227 us
  blocking collectives  89.1 us (39%)
  waiting for transfers between devices  51.8 us (23%)
  starting transfers between devices  43.3 us (19%)
  Pallas kernels  21.8 us (10%)
  other arithmetic  13.8 us (6%)
  matrix products  4.1 us (2%)
    all_to_all x6, blocking collectives, exchange(): return lax.all_to_all(copies, axis, 0, 0, tiled=True)  89.1 us
    all_to_all x5, waiting for transfers between devices, exchange(): return lax.all_to_all(copies, axis, 0, 0, tiled=True)  44 us
    all_to_all x5, starting transfers between devices, exchange(): return lax.all_to_all(copies, axis, 0, 0, tiled=True)  29.2 us
    pallas_call x10, Pallas kernels, on_core(): pl.pallas_call(kernel, out_shape=tuple(outs), in_specs=[pl.BlockSpec(memo...  21.8 us
    ppermute x9, starting transfers between devices, spread_sum(): got = lax.ppermute(part, axis, [(i, target(i, hop)) for i in range(16)])  13.7 us
    ppermute x9, waiting for transfers between devices, spread_sum(): got = lax.ppermute(part, axis, [(i, target(i, hop)) for i in range(16)])  7.81 us
  transfers between devices with their start and end apart: 16, of which 6 were waited for; matrix products, arithmetic and copies ran while one was open for 6% of the time, Pallas kernels for 0%

profile of v2, /device:TPU:32, one launch (start us, length us, event | category | flops | bytes accessed | tf_op | source)
XLA Modules:
  0.0 227.0 jit_solution(333728896379800218)
XLA Ops:
  0.7 2.1 convolution_convert_fusion
  2.7 8.5 %all-to-all-start = ((bf16[16,48,256]{2,1,0:T(8,128)(2,1)}), bf16[16,48,256]{2,1,0:T(8,128)(2,1)S(1)}, u32[]{:S(2)}, u32[]{:S(2)}) async-start(bf16[16,48,256]{2,1,0:T(8,128)(2,1)} %bitcast), calls=%async_computation | async-start | bytes 786432 | tf_op jit(solution)/shard_map/all_to_all | solution.py:295
  11.2 2.0 fusion
  13.8 1.1 fusion.14
  14.9 0.8 dynamic-slice_bitcast_fusion.2
  15.7 3.0 %collective-permute-start = (f32[4,48,256]{2,1,0:T(8,128)}, f32[4,48,256]{2,1,0:T(8,128)}, u32[]{:S(2)}, u32[]{:S(2)}) collective-permute-start(f32[4,48,256]{2,1,0:T(8,128)} %get-tuple-element.59), channel_id=1, source_target_pairs={{0,2},{1,3},{2,0},{3,1},{4,6},{5,7},{6,4},{7,5},{8,10},{9,11},{10,... | collective-permute-start | bytes 589832 | tf_op jit(solution)/shard_map/ppermute | solution.py:302
  18.7 0.6 collective-permute-start.1
  19.2 2.7 %collective-permute-start.2 = (f32[4,48,256]{2,1,0:T(8,128)}, f32[4,48,256]{2,1,0:T(8,128)}, u32[]{:S(2)}, u32[]{:S(2)}) collective-permute-start(f32[4,48,256]{2,1,0:T(8,128)} %get-tuple-element.60), channel_id=1, source_target_pairs={{0,3},{1,0},{2,1},{3,2},{4,7},{5,4},{6,5},{7,6},{8,11},{9,8},{10,9... | collective-permute-start | bytes 589832 | tf_op jit(solution)/shard_map/ppermute | solution.py:302
  21.9 4.5 %collective-permute-done = f32[4,48,256]{2,1,0:T(8,128)} collective-permute-done((f32[4,48,256]{2,1,0:T(8,128)}, f32[4,48,256]{2,1,0:T(8,128)}, u32[]{:S(2)}, u32[]{:S(2)}) %collective-permute-start) | collective-permute-done | bytes 196640 | tf_op jit(solution)/shard_map/ppermute | solution.py:302
  26.4 3.3 %collective-permute-done.1 = f32[4,48,256]{2,1,0:T(8,128)} collective-permute-done((f32[4,48,256]{2,1,0:T(8,128)}, f32[4,48,256]{2,1,0:T(8,128)}, u32[]{:S(2)}, u32[]{:S(2)}) %collective-permute-start.1) | collective-permute-done | bytes 196640 | tf_op jit(solution)/shard_map/ppermute | solution.py:302
  29.7 1.8 fusion.10
  31.5 0.9 shard_map.77
  32.4 3.4 %fusion.1.w_far = bf16[256,4096]{1,0:T(8,128)(2,1)} fusion(bf16[256,4096]{1,0:T(8,128)(2,1)} %param.10, f32[4096]{0:T(1024)S(1)} %add_rsqrt_fusion.1), kind=kLoop, calls=%fused_computation.5 | loop fusion | flops 3145728 | bytes 4210688 | tf_op jit(solution)/shard_map/convert_element_type | solution.py:344
  35.9 1.4 collective-permute-start.3
  37.6 1.7 collective-permute-start.5
  39.3 6.6 %all-to-all-start.1 = ((bf16[16,48,256]{2,1,0:T(8,128)(2,1)}), bf16[16,48,256]{2,1,0:T(8,128)(2,1)S(1)}, u32[]{:S(2)}, u32[]{:S(2)}) async-start(bf16[16,48,256]{2,1,0:T(8,128)(2,1)} %shard_map.77), calls=%async_computation.1 | async-start | bytes 786432 | tf_op jit(solution)/shard_map/all_to_all | solution.py:295
  45.9 1.7 fusion.3.w_ref.wlow_ref
  47.7 9.9 %all-to-all-done.1 = bf16[16,48,256]{2,1,0:T(8,128)(2,1)S(1)} async-done(((bf16[16,48,256]{2,1,0:T(8,128)(2,1)}), bf16[16,48,256]{2,1,0:T(8,128)(2,1)S(1)}, u32[]{:S(2)}, u32[]{:S(2)}) %all-to-all-start.1) | async-done | bytes 393248 | tf_op jit(solution)/shard_map/all_to_all | solution.py:295
  57.6 4.1 %shard_map.78 = (f32[768,4096]{1,0:T(8,128)S(1)}, bf16[16,32,128]{2,1,0:T(8,128)(2,1)S(1)}) custom-call(bf16[768,256]{1,0:T(8,128)(2,1)S(1)} %bitcast.58, bf16[256,4096]{1,0:T(8,128)(2,1)} %fusion.1.w_far), custom_call_target="tpu_custom_call" | custom-call | tf_op jit(solution)/shard_map/pallas_call | solution.py:44
  61.7 20.3 %all_to_all.55.got_ref = bf16[16,32,128]{2,1,0:T(8,128)(2,1)S(1)} all-to-all(bf16[16,32,128]{2,1,0:T(8,128)(2,1)S(1)} %get-tuple-element.43), channel_id=1, replica_groups=mesh['dp'=16,'proto'=16] {'dp'}, dimensions={0} | all-to-all | bytes 262144 | tf_op jit(solution)/shard_map/all_to_all | solution.py:295
  82.0 1.4 shard_map.79
  83.3 10.9 %all_to_all.56.got_ref = bf16[16,16,128]{2,1,0:T(8,128)(2,1)S(1)} all-to-all(bf16[16,16,128]{2,1,0:T(8,128)(2,1)S(1)} %shard_map.79), channel_id=1, replica_groups=mesh['dp'=16,'proto'=16] {'proto'}, dimensions={0} | all-to-all | bytes 131072 | tf_op jit(solution)/shard_map/all_to_all | solution.py:295
  94.2 1.3 shard_map.80
  95.5 14.6 %all_to_all.57.got_ref = bf16[16,32,128]{2,1,0:T(8,128)(2,1)S(1)} all-to-all(bf16[16,32,128]{2,1,0:T(8,128)(2,1)S(1)} %shard_map.80), channel_id=1, replica_groups=mesh['dp'=16,'proto'=16] {'dp'}, dimensions={0} | all-to-all | bytes 262144 | tf_op jit(solution)/shard_map/all_to_all | solution.py:295
  110.2 1.4 shard_map.81
  111.6 17.4 %all_to_all.58.got_ref = bf16[16,112,128]{2,1,0:T(8,128)(2,1)S(1)} all-to-all(bf16[16,112,128]{2,1,0:T(8,128)(2,1)S(1)} %shard_map.81), channel_id=1, replica_groups=mesh['dp'=16,'proto'=16] {'proto'}, dimensions={0} | all-to-all | bytes 917504 | tf_op jit(solution)/shard_map/all_to_all | solution.py:295
  129.0 1.3 shard_map.82
  130.3 14.6 %all_to_all.59.got_ref.cols_ref = bf16[16,32,128]{2,1,0:T(8,128)(2,1)S(1)} all-to-all(bf16[16,32,128]{2,1,0:T(8,128)(2,1)S(1)} %shard_map.82), channel_id=1, replica_groups=mesh['dp'=16,'proto'=16] {'dp'}, dimensions={0} | all-to-all | bytes 262144 | tf_op jit(solution)/shard_map/all_to_all | solution.py:295
  144.9 1.9 shard_map.83
  146.9 1.4 shard_map.84
  148.2 11.2 %all_to_all.60.rows_ref = bf16[16,32,128]{2,1,0:T(8,128)(2,1)S(1)} all-to-all(bf16[16,32,128]{2,1,0:T(8,128)(2,1)S(1)} %shard_map.84), channel_id=1, replica_groups=mesh['dp'=16,'proto'=16] {'proto'}, dimensions={0} | all-to-all | bytes 262144 | tf_op jit(solution)/shard_map/all_to_all | solution.py:295
  159.5 7.1 %shard_map.85 = (bf16[16,64,256]{2,1,0:T(8,128)(2,1)}, f32[8,16,4096]{2,1,0:T(8,128)}, bf16[8,16,4096]{2,1,0:T(8,128)(2,1)}) custom-call(s32[1]{0:T(128)} %bitcast.15.core_ref, f32[768,4096]{1,0:T(8,128)S(1)} %get-tuple-element.42.expo_ref, bf16[768,4096]{1,0:T(8,128)(2,1)S(1)} %get-tuple-element.47.stud_ref, ...), custom_call_target="tpu_custom_call" | custom-call | tf_op jit(solution)/shard_map/pallas_call | solution.py:44
  166.8 5.5 %all-to-all-start.8 = ((bf16[16,64,256]{2,1,0:T(8,128)(2,1)}), bf16[16,64,256]{2,1,0:T(8,128)(2,1)S(1)}, u32[]{:S(2)}, u32[]{:S(2)}) async-start(bf16[16,64,256]{2,1,0:T(8,128)(2,1)} %get-tuple-element.55), calls=%async_computation.8 | async-start | bytes 1048576 | tf_op jit(solution)/shard_map/all_to_all | solution.py:295
  172.3 1.8 convert_add_fusion
  174.1 1.3 copy-done.3
  175.5 0.9 collective-permute-start.7
  176.4 0.8 collective-permute-start.8
  177.2 2.5 %collective-permute-start.9 = (bf16[2,16,4096]{2,1,0:T(8,128)(2,1)S(1)}, bf16[2,16,4096]{2,1,0:T(8,128)(2,1)S(1)}, u32[]{:S(2)}, u32[]{:S(2)}) collective-permute-start(bf16[2,16,4096]{2,1,0:T(8,128)(2,1)S(1)} %get-tuple-element.57), channel_id=1, source_target_pairs={{0,192},{16,208},{32,224},{48,240},{64,0},{80,16},{96,32},{112,48}... | collective-permute-start | bytes 786440 | tf_op jit(solution)/shard_map/ppermute | solution.py:302
  179.7 8.4 %all-to-all-done.8.got_ref = bf16[16,64,256]{2,1,0:T(8,128)(2,1)S(1)} async-done(((bf16[16,64,256]{2,1,0:T(8,128)(2,1)}), bf16[16,64,256]{2,1,0:T(8,128)(2,1)S(1)}, u32[]{:S(2)}, u32[]{:S(2)}) %all-to-all-start.8) | async-done | bytes 524320 | tf_op jit(solution)/shard_map/all_to_all | solution.py:295
  188.0 0.9 shard_map.86
  189.0 5.1 %all-to-all-start.9 = ((bf16[16,48,256]{2,1,0:T(8,128)(2,1)}), bf16[16,48,256]{2,1,0:T(8,128)(2,1)S(1)}, u32[]{:S(2)}, u32[]{:S(2)}) async-start(bf16[16,48,256]{2,1,0:T(8,128)(2,1)} %shard_map.86), calls=%async_computation.9 | async-start | bytes 786432 | tf_op jit(solution)/shard_map/all_to_all | solution.py:295
  194.1 1.2 fusion.5
  195.5 15.8 %all-to-all-done.9 = bf16[16,48,256]{2,1,0:T(8,128)(2,1)S(1)} async-done(((bf16[16,48,256]{2,1,0:T(8,128)(2,1)}), bf16[16,48,256]{2,1,0:T(8,128)(2,1)S(1)}, u32[]{:S(2)}, u32[]{:S(2)}) %all-to-all-start.9) | async-done | bytes 393248 | tf_op jit(solution)/shard_map/all_to_all | solution.py:295
  211.3 0.9 convolution_convert_fusion.1
  212.2 3.5 %all-to-all-start.10 = ((bf16[16,16,128]{2,1,0:T(8,128)(2,1)}), bf16[16,16,128]{2,1,0:T(8,128)(2,1)S(1)}, u32[]{:S(2)}, u32[]{:S(2)}) async-start(bf16[16,16,128]{2,1,0:T(8,128)(2,1)} %bitcast.24), calls=%async_computation.10 | async-start | bytes 131072 | tf_op jit(solution)/shard_map/all_to_all | solution.py:295
  215.7 0.7 bitcast_add_fusion.1
  216.5 9.9 %all-to-all-done.10 = bf16[16,16,128]{2,1,0:T(8,128)(2,1)S(1)} async-done(((bf16[16,16,128]{2,1,0:T(8,128)(2,1)}), bf16[16,16,128]{2,1,0:T(8,128)(2,1)S(1)}, u32[]{:S(2)}, u32[]{:S(2)}) %all-to-all-start.10) | async-done | bytes 65568 | tf_op jit(solution)/shard_map/all_to_all | solution.py:295
  226.4 0.6 convert_reduce_fusion
  (29 shorter events, 1.4 us)
Async XLA Ops:
  0.6 13.1 %copy-start = (bf16[768,128]{1,0:T(8,128)(2,1)S(1)}, bf16[768,128]{1,0:T(8,128)(2,1)}, u32[]{:S(2)}) copy-start(bf16[768,128]{1,0:T(8,128)(2,1)} %param.7) | copy-start | bytes 589828
  0.6 12.6 %copy-start.1 = (bf16[256,4096]{1,0:T(8,128)(2,1)S(1)}, bf16[256,4096]{1,0:T(8,128)(2,1)}, u32[]{:S(2)}) copy-start(bf16[256,4096]{1,0:T(8,128)(2,1)} %raw_ref.1) | copy-start | bytes 6291460
  2.7 28.8 %all-to-all-start = ((bf16[16,48,256]{2,1,0:T(8,128)(2,1)}), bf16[16,48,256]{2,1,0:T(8,128)(2,1)S(1)}, u32[]{:S(2)}, u32[]{:S(2)}) async-start(bf16[16,48,256]{2,1,0:T(8,128)(2,1)} %bitcast), calls=%async_computation | async-start | bytes 786432 | tf_op jit(solution)/shard_map/all_to_all | solution.py:295
  15.7 10.7 %collective-permute-start = (f32[4,48,256]{2,1,0:T(8,128)}, f32[4,48,256]{2,1,0:T(8,128)}, u32[]{:S(2)}, u32[]{:S(2)}) collective-permute-start(f32[4,48,256]{2,1,0:T(8,128)} %get-tuple-element.59), channel_id=1, source_target_pairs={{0,2},{1,3},{2,0},{3,1},{4,6},{5,7},{6,4},{7,5},{8,10},{9,11},{10,... | collective-permute-start | bytes 589832 | tf_op jit(solution)/shard_map/ppermute | solution.py:302
  18.7 11.0 %collective-permute-start.1 = (f32[4,48,256]{2,1,0:T(8,128)}, f32[4,48,256]{2,1,0:T(8,128)}, u32[]{:S(2)}, u32[]{:S(2)}) collective-permute-start(f32[4,48,256]{2,1,0:T(8,128)} %get-tuple-element.61), channel_id=1, source_target_pairs={{0,1},{1,2},{2,3},{3,0},{4,5},{5,6},{6,7},{7,4},{8,9},{9,10},{10,1... | collective-permute-start | bytes 589832 | tf_op jit(solution)/shard_map/ppermute | solution.py:302
  19.2 10.5 %collective-permute-start.2 = (f32[4,48,256]{2,1,0:T(8,128)}, f32[4,48,256]{2,1,0:T(8,128)}, u32[]{:S(2)}, u32[]{:S(2)}) collective-permute-start(f32[4,48,256]{2,1,0:T(8,128)} %get-tuple-element.60), channel_id=1, source_target_pairs={{0,3},{1,0},{2,1},{3,2},{4,7},{5,4},{6,5},{7,6},{8,11},{9,8},{10,9... | collective-permute-start | bytes 589832 | tf_op jit(solution)/shard_map/ppermute | solution.py:302
  32.4 3.4 %copy-start.4 = (f32[4,48,256]{2,1,0:T(8,128)S(1)}, f32[4,48,256]{2,1,0:T(8,128)}, u32[]{:S(2)}) copy-start(f32[4,48,256]{2,1,0:T(8,128)} %fusion.10) | copy-start | bytes 589828
  35.9 11.8 %collective-permute-start.3 = (f32[48,256]{1,0:T(8,128)S(1)}, f32[48,256]{1,0:T(8,128)S(1)}, u32[]{:S(2)}, u32[]{:S(2)}) collective-permute-start(f32[48,256]{1,0:T(8,128)S(1)} %get-tuple-element.62), channel_id=1, source_target_pairs={{0,8},{1,9},{2,10},{3,11},{4,12},{5,13},{6,14},{7,15},{8,0},{9,1},... | collective-permute-start | bytes 147464 | tf_op jit(solution)/shard_map/ppermute | solution.py:302
  37.2 10.4 %collective-permute-start.4 = (f32[48,256]{1,0:T(8,128)S(1)}, f32[48,256]{1,0:T(8,128)S(1)}, u32[]{:S(2)}, u32[]{:S(2)}) collective-permute-start(f32[48,256]{1,0:T(8,128)S(1)} %get-tuple-element.64), channel_id=1, source_target_pairs={{0,4},{1,5},{2,6},{3,7},{4,8},{5,9},{6,10},{7,11},{8,12},{9,13},{1... | collective-permute-start | bytes 147464 | tf_op jit(solution)/shard_map/ppermute | solution.py:302
  37.6 10.0 %collective-permute-start.5 = (f32[48,256]{1,0:T(8,128)S(1)}, f32[48,256]{1,0:T(8,128)S(1)}, u32[]{:S(2)}, u32[]{:S(2)}) collective-permute-start(f32[48,256]{1,0:T(8,128)S(1)} %get-tuple-element.63), channel_id=1, source_target_pairs={{0,12},{1,13},{2,14},{3,15},{4,0},{5,1},{6,2},{7,3},{8,4},{9,5},{1... | collective-permute-start | bytes 147464 | tf_op jit(solution)/shard_map/ppermute | solution.py:302
  39.3 18.3 %all-to-all-start.1 = ((bf16[16,48,256]{2,1,0:T(8,128)(2,1)}), bf16[16,48,256]{2,1,0:T(8,128)(2,1)S(1)}, u32[]{:S(2)}, u32[]{:S(2)}) async-start(bf16[16,48,256]{2,1,0:T(8,128)(2,1)} %shard_map.77), calls=%async_computation.1 | async-start | bytes 786432 | tf_op jit(solution)/shard_map/all_to_all | solution.py:295
  129.0 16.0 %copy-start.2 = (bf16[256,4096]{1,0:T(8,128)(2,1)S(1)}, bf16[256,4096]{1,0:T(8,128)(2,1)}, u32[]{:S(2)}) copy-start(bf16[256,4096]{1,0:T(8,128)(2,1)} %fusion.3.w_ref.wlow_ref) | copy-start | bytes 6291460
  166.6 5.7 %collective-permute-start.6 = (bf16[8,16,4096]{2,1,0:T(8,128)(2,1)}, bf16[8,16,4096]{2,1,0:T(8,128)(2,1)S(1)}, u32[]{:S(2)}, u32[]{:S(2)}) collective-permute-start(bf16[8,16,4096]{2,1,0:T(8,128)(2,1)} %get-tuple-element.53), channel_id=1, source_target_pairs={{0,16},{16,0},{32,48},{48,32},{64,80},{80,64},{96,112},{112,96},{1... | collective-permute-start | bytes 3145736 | tf_op jit(solution)/shard_map/ppermute | solution.py:437
  166.8 21.2 %all-to-all-start.8 = ((bf16[16,64,256]{2,1,0:T(8,128)(2,1)}), bf16[16,64,256]{2,1,0:T(8,128)(2,1)S(1)}, u32[]{:S(2)}, u32[]{:S(2)}) async-start(bf16[16,64,256]{2,1,0:T(8,128)(2,1)} %get-tuple-element.55), calls=%async_computation.8 | async-start | bytes 1048576 | tf_op jit(solution)/shard_map/all_to_all | solution.py:295
  174.1 1.3 copy-start.3
  175.5 18.5 %collective-permute-start.7 = (bf16[2,16,4096]{2,1,0:T(8,128)(2,1)S(1)}, bf16[2,16,4096]{2,1,0:T(8,128)(2,1)S(1)}, u32[]{:S(2)}, u32[]{:S(2)}) collective-permute-start(bf16[2,16,4096]{2,1,0:T(8,128)(2,1)S(1)} %get-tuple-element.56), channel_id=1, source_target_pairs={{0,128},{16,144},{32,160},{48,176},{64,192},{80,208},{96,224},{112... | collective-permute-start | bytes 786440 | tf_op jit(solution)/shard_map/ppermute | solution.py:302
  176.4 17.6 %collective-permute-start.8 = (bf16[2,16,4096]{2,1,0:T(8,128)(2,1)S(1)}, bf16[2,16,4096]{2,1,0:T(8,128)(2,1)S(1)}, u32[]{:S(2)}, u32[]{:S(2)}) collective-permute-start(bf16[2,16,4096]{2,1,0:T(8,128)(2,1)S(1)} %get-tuple-element.58), channel_id=1, source_target_pairs={{0,64},{16,80},{32,96},{48,112},{64,128},{80,144},{96,160},{112,17... | collective-permute-start | bytes 786440 | tf_op jit(solution)/shard_map/ppermute | solution.py:302
  177.2 16.9 %collective-permute-start.9 = (bf16[2,16,4096]{2,1,0:T(8,128)(2,1)S(1)}, bf16[2,16,4096]{2,1,0:T(8,128)(2,1)S(1)}, u32[]{:S(2)}, u32[]{:S(2)}) collective-permute-start(bf16[2,16,4096]{2,1,0:T(8,128)(2,1)S(1)} %get-tuple-element.57), channel_id=1, source_target_pairs={{0,192},{16,208},{32,224},{48,240},{64,0},{80,16},{96,32},{112,48}... | collective-permute-start | bytes 786440 | tf_op jit(solution)/shard_map/ppermute | solution.py:302
  189.0 22.3 %all-to-all-start.9 = ((bf16[16,48,256]{2,1,0:T(8,128)(2,1)}), bf16[16,48,256]{2,1,0:T(8,128)(2,1)S(1)}, u32[]{:S(2)}, u32[]{:S(2)}) async-start(bf16[16,48,256]{2,1,0:T(8,128)(2,1)} %shard_map.86), calls=%async_computation.9 | async-start | bytes 786432 | tf_op jit(solution)/shard_map/all_to_all | solution.py:295
  195.3 20.5 %collective-permute-start.10 = (bf16[16,4096]{1,0:T(8,128)(2,1)S(1)}, bf16[16,4096]{1,0:T(8,128)(2,1)S(1)}, u32[]{:S(2)}, u32[]{:S(2)}) collective-permute-start(bf16[16,4096]{1,0:T(8,128)(2,1)S(1)} %fusion.11), channel_id=1, source_target_pairs={{0,32},{16,48},{32,0},{48,16},{64,96},{80,112},{96,64},{112,80},{1... | collective-permute-start | bytes 393224 | tf_op jit(solution)/shard_map/ppermute | solution.py:442
  212.2 14.2 %all-to-all-start.10 = ((bf16[16,16,128]{2,1,0:T(8,128)(2,1)}), bf16[16,16,128]{2,1,0:T(8,128)(2,1)S(1)}, u32[]{:S(2)}, u32[]{:S(2)}) async-start(bf16[16,16,128]{2,1,0:T(8,128)(2,1)} %bitcast.24), calls=%async_computation.10 | async-start | bytes 131072 | tf_op jit(solution)/shard_map/all_to_all | solution.py:295

commit v3 on v2

--- a/solution.py
+++ b/solution.py
@@ -54,15 +54,6 @@
     )(*args)
 
 
-def fetch(far_ref, near_ref, sems):
-    copies = []
-    for k in range(far_ref.shape[1] // WIDE):
-        cols = pl.ds(k * WIDE, WIDE)
-        copies.append(pltpu.make_async_copy(far_ref.at[:, cols], near_ref.at[:, cols], sems.at[k]))
-        copies[-1].start()
-    return copies
-
-
 def column_of(rows, j):
     return jnp.broadcast_to(rows[j : j + 1, :], (LANES, LANES)).T
 
@@ -110,12 +101,10 @@
         out_ref[p] = rows
 
 
-def teacher_kernel(low_ref, w_far, expo_ref, out_ref, w_ref, sems, sums_ref):
-    loads = fetch(w_far, w_ref, sems)
+def teacher_kernel(low_ref, w_ref, expo_ref, out_ref, sums_ref):
     low = low_ref[...]
     for k in range(w_ref.shape[1] // WIDE):
         cols = pl.ds(k * WIDE, WIDE)
-        loads[k].wait()
         scores = jnp.dot(low, w_ref[:, cols], preferred_element_type=jnp.float32)
         expo = jnp.exp2(scores * (LOG2E / TEACHER_TEMP))
         expo_ref[:, cols] = expo.astype(expo_ref.dtype)
@@ -331,19 +320,18 @@
     share = rows // n_proto
     teach_norm = col_scales(teacher_prototypes)
     stud_norm = col_scales(student_prototypes)
-    teach_norm, stud_norm, stud_early = lax.optimization_barrier(
-        (teach_norm, stud_norm, student_hidden)
-    )
-    stud_part = jnp.dot(stud_early, student_bottleneck, preferred_element_type=f32)
+    stud_part = jnp.dot(student_hidden, student_bottleneck, preferred_element_type=f32)
     stud_part = stud_part.reshape(4, 4, share, width)
     stud_line = spread_sum(stud_part, "proto", 1, me % 4, lambda i, hop: i // 4 * 4 + (i + hop) % 4)
 
     (copies,) = on_core(share_kernel, [shape(got.shape, bf16)], (got,))
-    copies, teach_norm, stud_norm = lax.optimization_barrier((copies, teach_norm, stud_norm))
+    copies, teach_norm, stud_norm, stud_line = lax.optimization_barrier(
+        (copies, teach_norm, stud_norm, stud_line)
+    )
     teach_low = exchange(copies, "proto").reshape(rows, width)
     teach_wlow = (teacher_prototypes.astype(f32) * teach_norm).astype(bf16)
-    teach_wlow, stud_line, stud_norm = lax.optimization_barrier((teach_wlow, stud_line, stud_norm))
     stud_wlow = (student_prototypes.astype(f32) * stud_norm).astype(bf16)
+    teach_wlow, stud_wlow, stud_line = lax.optimization_barrier((teach_wlow, stud_wlow, stud_line))
     stud_share = spread_sum(stud_line, "proto", 0, me // 4, lambda i, hop: (i + 4 * hop) % 16)
 
     teach_low, teach_wlow, stud_norm, stud_wlow, stud_share, core, high, y_at = (
@@ -353,16 +341,13 @@
     )
 
     big = pltpu.VMEM((rows, columns), KEEP)
-    chunks = columns // WIDE
-    weights = [pltpu.VMEM((width, columns), bf16), pltpu.SemaphoreType.DMA((chunks,))]
     row_acc = [pltpu.VMEM((rows, LANES), f32), pltpu.VMEM((8, LANES), f32)]
     col_sums = pltpu.VMEM((col_tiles, LANES), f32)
     expo, copies = on_core(
         teacher_kernel,
         [big, shape((n_dp, col_tiles, LANES), bf16)],
         (teach_low, teach_wlow),
-        scratch=weights + [col_sums],
-        far=(1,),
+        scratch=[col_sums],
     )
     for step in range(ITERS):
         got_cols = exchange(copies, "dp")
@@ -428,19 +413,20 @@
     got = exchange(feat_part, "proto")
     (copies,) = on_core(proj_kernel, [shape((n_proto, share, width), bf16)], (got, stud_share))
     proj_grad = exchange(copies, "proto").reshape(rows, width)
-    bottle_part = lax.dot_general(
-        proj_grad, student_hidden, (((0,), (0,)), ((), ())), preferred_element_type=f32
-    )
-    got_bottle = exchange(blocks_of(bottle_part, n_dp), "dp")
-    grad_bottleneck = jnp.sum(got_bottle.astype(f32), axis=0).T
-
     got = lax.ppermute(send, "dp", [(i, i ^ 1) for i in range(16)])
     pair = (keep + got.astype(f32)).reshape(4, 2, 16, columns)
     quarter = spread_sum(pair, "dp", 0, y_at, lambda i, hop: (i + 4 * hop) % 16, bf16)
+    proj_grad, quarter = lax.optimization_barrier((proj_grad, quarter))
     keep = jnp.where(high == 0, quarter[0], quarter[1])
     send = jnp.where(high == 0, quarter[1], quarter[0]).astype(bf16)
     got = lax.ppermute(send, "dp", [(i, i ^ 2) for i in range(16)])
     grad_prototypes = keep + got.astype(f32)
+    bottle_part = lax.dot_general(
+        proj_grad, student_hidden, (((0,), (0,)), ((), ())), preferred_element_type=f32
+    )
+    got_bottle = exchange(blocks_of(bottle_part, n_dp), "dp")
+    grad_bottleneck = jnp.sum(got_bottle.astype(f32), axis=0).T
+
     return (grad_prototypes, grad_bottleneck)
 
 

time: 229 us -> 219 us (0.956)
  waiting for transfers between devices: 51.8 us -> 38.7 us
  starting transfers between devices: 43.3 us -> 47.3 us
  Pallas kernels: 21.8 us -> 19.5 us
    all_to_all x5, waiting for transfers between devices: 44 us -> 27.7 us  [exchange(): return lax.all_to_all(copies, axis, 0, 0, tiled=True)]
    ppermute x1, starting transfers between devices: 0.28 us -> 5.8 us  [on_device(): got = lax.ppermute(send, 'dp', [(i, i ^ 2) for i in range(16)])]
    ppermute x9, waiting for transfers between devices: 7.81 us -> 11 us  [spread_sum(): got = lax.ppermute(part, axis, [(i, target(i, hop)) for i in range(16)])]
  transfers between devices with their start and end apart: 16 -> 16, of which waited for: 6 -> 7; matrix products, arithmetic and copies ran while one was open for 6% -> 7% of each run, Pallas kernels for 0% -> 0%
where the time goes in v3:
time: 219 us; the launch traced here: 218 us
  blocking collectives  90.7 us (41%)
  starting transfers between devices  47.3 us (22%)
  waiting for transfers between devices  38.7 us (18%)
  Pallas kernels  19.5 us (9%)
  other arithmetic  13.2 us (6%)
  matrix products  4.12 us (2%)
  local copies, waits for them, and re-layouts  3.86 us (2%)
    all_to_all x6, blocking collectives, exchange(): return lax.all_to_all(copies, axis, 0, 0, tiled=True)  90.7 us
    all_to_all x5, waiting for transfers between devices, exchange(): return lax.all_to_all(copies, axis, 0, 0, tiled=True)  27.7 us
    all_to_all x5, starting transfers between devices, exchange(): return lax.all_to_all(copies, axis, 0, 0, tiled=True)  27.2 us
    pallas_call x10, Pallas kernels, on_core(): pl.pallas_call(kernel, out_shape=tuple(outs), in_specs=[pl.BlockSpec(memo...  19.5 us
    ppermute x9, starting transfers between devices, spread_sum(): got = lax.ppermute(part, axis, [(i, target(i, hop)) for i in range(16)])  14.2 us
    ppermute x9, waiting for transfers between devices, spread_sum(): got = lax.ppermute(part, axis, [(i, target(i, hop)) for i in range(16)])  11 us
    ppermute x1, starting transfers between devices, on_device(): got = lax.ppermute(send, 'dp', [(i, i ^ 2) for i in range(16)])  5.8 us
    convert_element_type x1, other arithmetic, on_device(): teach_wlow = (teacher_prototypes.astype(f32) * teach_norm).astype(bf16)  4.54 us
  transfers between devices with their start and end apart: 16, of which 7 were waited for; matrix products, arithmetic and copies ran while one was open for 7% of the time, Pallas kernels for 0%

profile of v3, /device:TPU:32, one launch (start us, length us, event | category | flops | bytes accessed | tf_op | source)
XLA Modules:
  0.0 218.4 jit_solution(1073227811317402095)
XLA Ops:
  0.6 2.0 convolution_convert_fusion
  2.6 8.5 %all-to-all-start = ((bf16[16,48,256]{2,1,0:T(8,128)(2,1)}), bf16[16,48,256]{2,1,0:T(8,128)(2,1)S(1)}, u32[]{:S(2)}, u32[]{:S(2)}) async-start(bf16[16,48,256]{2,1,0:T(8,128)(2,1)} %bitcast), calls=%async_computation | async-start | bytes 786432 | tf_op jit(solution)/shard_map/all_to_all | solution.py:284
  11.1 1.2 fusion.14
  12.4 0.8 dynamic-slice_bitcast_fusion.2
  13.2 2.7 %collective-permute-start.2 = (f32[4,48,256]{2,1,0:T(8,128)}, f32[4,48,256]{2,1,0:T(8,128)}, u32[]{:S(2)}, u32[]{:S(2)}) collective-permute-start(f32[4,48,256]{2,1,0:T(8,128)} %get-tuple-element.60), channel_id=1, source_target_pairs={{0,3},{1,0},{2,1},{3,2},{4,7},{5,4},{6,5},{7,6},{8,11},{9,8},{10,9... | collective-permute-start | bytes 589832 | tf_op jit(solution)/shard_map/ppermute | solution.py:291
  15.9 2.3 %collective-permute-start = (f32[4,48,256]{2,1,0:T(8,128)}, f32[4,48,256]{2,1,0:T(8,128)}, u32[]{:S(2)}, u32[]{:S(2)}) collective-permute-start(f32[4,48,256]{2,1,0:T(8,128)} %get-tuple-element.59), channel_id=1, source_target_pairs={{0,2},{1,3},{2,0},{3,1},{4,6},{5,7},{6,4},{7,5},{8,10},{9,11},{10,... | collective-permute-start | bytes 589832 | tf_op jit(solution)/shard_map/ppermute | solution.py:291
  18.2 2.0 fusion
  20.8 5.1 %collective-permute-done.2 = f32[4,48,256]{2,1,0:T(8,128)} collective-permute-done((f32[4,48,256]{2,1,0:T(8,128)}, f32[4,48,256]{2,1,0:T(8,128)}, u32[]{:S(2)}, u32[]{:S(2)}) %collective-permute-start.2) | collective-permute-done | bytes 196640 | tf_op jit(solution)/shard_map/ppermute | solution.py:291
  25.9 3.2 %collective-permute-done.1 = f32[4,48,256]{2,1,0:T(8,128)} collective-permute-done((f32[4,48,256]{2,1,0:T(8,128)}, f32[4,48,256]{2,1,0:T(8,128)}, u32[]{:S(2)}, u32[]{:S(2)}) %collective-permute-start.1) | collective-permute-done | bytes 196640 | tf_op jit(solution)/shard_map/ppermute | solution.py:291
  29.1 1.8 fusion.10
  30.9 0.9 shard_map.77
  31.8 4.7 %all-to-all-start.1 = ((bf16[16,48,256]{2,1,0:T(8,128)(2,1)}), bf16[16,48,256]{2,1,0:T(8,128)(2,1)S(1)}, u32[]{:S(2)}, u32[]{:S(2)}) async-start(bf16[16,48,256]{2,1,0:T(8,128)(2,1)} %shard_map.77), calls=%async_computation.1 | async-start | bytes 786432 | tf_op jit(solution)/shard_map/all_to_all | solution.py:284
  36.5 4.5 %fusion.1 = (bf16[256,4096]{1,0:T(8,128)(2,1)}, bf16[256,4096]{1,0:T(8,128)(2,1)}) fusion(bf16[256,4096]{1,0:T(8,128)(2,1)} %param.10, f32[4096]{0:T(1024)S(1)} %add_rsqrt_fusion.1, f32[4096]{0:T(1024)S(1)} %add_rsqrt_fusion, bf16[256,4096]{1,0:T(8,128)(2,1)S(1)} %copy-done.1), kind=kLoop, calls=%fused_computation.5 | loop fusion | flops 6291456 | bytes 8421376 | tf_op jit(solution)/shard_map/convert_element_type | solution.py:332
  41.2 1.9 collective-permute-start.4
  43.2 4.2 %collective-permute-start.3 = (f32[48,256]{1,0:T(8,128)S(1)}, f32[48,256]{1,0:T(8,128)S(1)}, u32[]{:S(2)}, u32[]{:S(2)}) collective-permute-start(f32[48,256]{1,0:T(8,128)S(1)} %get-tuple-element.62), channel_id=1, source_target_pairs={{0,8},{1,9},{2,10},{3,11},{4,12},{5,13},{6,14},{7,15},{8,0},{9,1},... | collective-permute-start | bytes 147464 | tf_op jit(solution)/shard_map/ppermute | solution.py:291
  47.3 1.1 collective-permute-done.5
  48.5 1.6 collective-permute-done.3
  50.0 1.6 copy-done.3
  51.6 1.8 shard_map.78
  53.5 18.9 %all_to_all.55.got_ref = bf16[16,32,128]{2,1,0:T(8,128)(2,1)S(1)} all-to-all(bf16[16,32,128]{2,1,0:T(8,128)(2,1)S(1)} %get-tuple-element.41), channel_id=1, replica_groups=mesh['dp'=16,'proto'=16] {'dp'}, dimensions={0} | all-to-all | bytes 262144 | tf_op jit(solution)/shard_map/all_to_all | solution.py:284
  72.4 1.4 shard_map.79
  73.7 13.9 %all_to_all.56.got_ref = bf16[16,16,128]{2,1,0:T(8,128)(2,1)S(1)} all-to-all(bf16[16,16,128]{2,1,0:T(8,128)(2,1)S(1)} %shard_map.79), channel_id=1, replica_groups=mesh['dp'=16,'proto'=16] {'proto'}, dimensions={0} | all-to-all | bytes 131072 | tf_op jit(solution)/shard_map/all_to_all | solution.py:284
  87.6 1.3 shard_map.80
  88.9 14.6 %all_to_all.57.got_ref = bf16[16,32,128]{2,1,0:T(8,128)(2,1)S(1)} all-to-all(bf16[16,32,128]{2,1,0:T(8,128)(2,1)S(1)} %shard_map.80), channel_id=1, replica_groups=mesh['dp'=16,'proto'=16] {'dp'}, dimensions={0} | all-to-all | bytes 262144 | tf_op jit(solution)/shard_map/all_to_all | solution.py:284
  103.6 1.4 shard_map.81
  105.0 17.4 %all_to_all.58.got_ref = bf16[16,112,128]{2,1,0:T(8,128)(2,1)S(1)} all-to-all(bf16[16,112,128]{2,1,0:T(8,128)(2,1)S(1)} %shard_map.81), channel_id=1, replica_groups=mesh['dp'=16,'proto'=16] {'proto'}, dimensions={0} | all-to-all | bytes 917504 | tf_op jit(solution)/shard_map/all_to_all | solution.py:284
  122.4 1.3 shard_map.82
  123.7 14.6 %all_to_all.59.got_ref.cols_ref = bf16[16,32,128]{2,1,0:T(8,128)(2,1)S(1)} all-to-all(bf16[16,32,128]{2,1,0:T(8,128)(2,1)S(1)} %shard_map.82), channel_id=1, replica_groups=mesh['dp'=16,'proto'=16] {'dp'}, dimensions={0} | all-to-all | bytes 262144 | tf_op jit(solution)/shard_map/all_to_all | solution.py:284
  138.3 1.9 shard_map.83
  140.3 1.4 shard_map.84
  141.6 11.2 %all_to_all.60.rows_ref = bf16[16,32,128]{2,1,0:T(8,128)(2,1)S(1)} all-to-all(bf16[16,32,128]{2,1,0:T(8,128)(2,1)S(1)} %shard_map.84), channel_id=1, replica_groups=mesh['dp'=16,'proto'=16] {'proto'}, dimensions={0} | all-to-all | bytes 262144 | tf_op jit(solution)/shard_map/all_to_all | solution.py:284
  152.9 7.2 %shard_map.85 = (bf16[16,64,256]{2,1,0:T(8,128)(2,1)}, f32[8,16,4096]{2,1,0:T(8,128)}, bf16[8,16,4096]{2,1,0:T(8,128)(2,1)}) custom-call(s32[1]{0:T(128)} %bitcast.15.core_ref, f32[768,4096]{1,0:T(8,128)S(1)} %get-tuple-element.40.expo_ref, bf16[768,4096]{1,0:T(8,128)(2,1)S(1)} %get-tuple-element.45.stud_ref, ...), custom_call_target="tpu_custom_call" | custom-call | tf_op jit(solution)/shard_map/pallas_call | solution.py:44
  160.2 5.5 %all-to-all-start.8 = ((bf16[16,64,256]{2,1,0:T(8,128)(2,1)}), bf16[16,64,256]{2,1,0:T(8,128)(2,1)S(1)}, u32[]{:S(2)}, u32[]{:S(2)}) async-start(bf16[16,64,256]{2,1,0:T(8,128)(2,1)} %get-tuple-element.50), calls=%async_computation.8 | async-start | bytes 1048576 | tf_op jit(solution)/shard_map/all_to_all | solution.py:284
  165.7 1.8 convert_add_fusion
  167.5 1.3 copy-done.4
  168.9 0.8 collective-permute-start.9
  169.8 1.3 collective-permute-start.8
  171.0 0.8 collective-permute-start.7
  171.9 9.6 %all-to-all-done.8.got_ref = bf16[16,64,256]{2,1,0:T(8,128)(2,1)S(1)} async-done(((bf16[16,64,256]{2,1,0:T(8,128)(2,1)}), bf16[16,64,256]{2,1,0:T(8,128)(2,1)S(1)}, u32[]{:S(2)}, u32[]{:S(2)}) %all-to-all-start.8) | async-done | bytes 524320 | tf_op jit(solution)/shard_map/all_to_all | solution.py:284
  181.4 1.0 shard_map.86
  182.4 5.1 %all-to-all-start.9 = ((bf16[16,48,256]{2,1,0:T(8,128)(2,1)}), bf16[16,48,256]{2,1,0:T(8,128)(2,1)S(1)}, u32[]{:S(2)}, u32[]{:S(2)}) async-start(bf16[16,48,256]{2,1,0:T(8,128)(2,1)} %shard_map.86), calls=%async_computation.9 | async-start | bytes 786432 | tf_op jit(solution)/shard_map/all_to_all | solution.py:284
  187.5 1.2 fusion.5
  188.6 10.2 %all-to-all-done.9 = bf16[16,48,256]{2,1,0:T(8,128)(2,1)S(1)} async-done(((bf16[16,48,256]{2,1,0:T(8,128)(2,1)}), bf16[16,48,256]{2,1,0:T(8,128)(2,1)S(1)}, u32[]{:S(2)}, u32[]{:S(2)}) %all-to-all-start.9) | async-done | bytes 393248 | tf_op jit(solution)/shard_map/all_to_all | solution.py:284
  198.8 0.9 convolution_convert_fusion.1
  199.8 3.5 %all-to-all-start.10 = ((bf16[16,16,128]{2,1,0:T(8,128)(2,1)}), bf16[16,16,128]{2,1,0:T(8,128)(2,1)S(1)}, u32[]{:S(2)}, u32[]{:S(2)}) async-start(bf16[16,16,128]{2,1,0:T(8,128)(2,1)} %bitcast.24), calls=%async_computation.10 | async-start | bytes 131072 | tf_op jit(solution)/shard_map/all_to_all | solution.py:284
  203.3 5.8 %collective-permute-start.10 = (bf16[16,4096]{1,0:T(8,128)(2,1)S(1)}, bf16[16,4096]{1,0:T(8,128)(2,1)S(1)}, u32[]{:S(2)}, u32[]{:S(2)}) collective-permute-start(bf16[16,4096]{1,0:T(8,128)(2,1)S(1)} %fusion.11), channel_id=1, source_target_pairs={{0,32},{16,48},{32,0},{48,16},{64,96},{80,112},{96,64},{112,80},{1... | collective-permute-start | bytes 393224 | tf_op jit(solution)/shard_map/ppermute | solution.py:422
  209.1 8.0 %all-to-all-done.10 = bf16[16,16,128]{2,1,0:T(8,128)(2,1)S(1)} async-done(((bf16[16,16,128]{2,1,0:T(8,128)(2,1)}), bf16[16,16,128]{2,1,0:T(8,128)(2,1)S(1)}, u32[]{:S(2)}, u32[]{:S(2)}) %all-to-all-start.10) | async-done | bytes 65568 | tf_op jit(solution)/shard_map/all_to_all | solution.py:284
  217.7 0.7 bitcast_add_fusion.1
  (30 shorter events, 1.5 us)
Async XLA Ops:
  0.6 10.5 %copy-start = (bf16[768,128]{1,0:T(8,128)(2,1)S(1)}, bf16[768,128]{1,0:T(8,128)(2,1)}, u32[]{:S(2)}) copy-start(bf16[768,128]{1,0:T(8,128)(2,1)} %param.7) | copy-start | bytes 589828
  2.6 28.3 %all-to-all-start = ((bf16[16,48,256]{2,1,0:T(8,128)(2,1)}), bf16[16,48,256]{2,1,0:T(8,128)(2,1)S(1)}, u32[]{:S(2)}, u32[]{:S(2)}) async-start(bf16[16,48,256]{2,1,0:T(8,128)(2,1)} %bitcast), calls=%async_computation | async-start | bytes 786432 | tf_op jit(solution)/shard_map/all_to_all | solution.py:284
  11.1 9.2 %copy-start.1 = (bf16[256,4096]{1,0:T(8,128)(2,1)S(1)}, bf16[256,4096]{1,0:T(8,128)(2,1)}, u32[]{:S(2)}) copy-start(bf16[256,4096]{1,0:T(8,128)(2,1)} %raw_ref.1) | copy-start | bytes 6291460
  13.2 12.7 %collective-permute-start.2 = (f32[4,48,256]{2,1,0:T(8,128)}, f32[4,48,256]{2,1,0:T(8,128)}, u32[]{:S(2)}, u32[]{:S(2)}) collective-permute-start(f32[4,48,256]{2,1,0:T(8,128)} %get-tuple-element.60), channel_id=1, source_target_pairs={{0,3},{1,0},{2,1},{3,2},{4,7},{5,4},{6,5},{7,6},{8,11},{9,8},{10,9... | collective-permute-start | bytes 589832 | tf_op jit(solution)/shard_map/ppermute | solution.py:291
  15.9 13.2 %collective-permute-start.1 = (f32[4,48,256]{2,1,0:T(8,128)}, f32[4,48,256]{2,1,0:T(8,128)}, u32[]{:S(2)}, u32[]{:S(2)}) collective-permute-start(f32[4,48,256]{2,1,0:T(8,128)} %get-tuple-element.61), channel_id=1, source_target_pairs={{0,1},{1,2},{2,3},{3,0},{4,5},{5,6},{6,7},{7,4},{8,9},{9,10},{10,1... | collective-permute-start | bytes 589832 | tf_op jit(solution)/shard_map/ppermute | solution.py:291
  15.9 13.2 %collective-permute-start = (f32[4,48,256]{2,1,0:T(8,128)}, f32[4,48,256]{2,1,0:T(8,128)}, u32[]{:S(2)}, u32[]{:S(2)}) collective-permute-start(f32[4,48,256]{2,1,0:T(8,128)} %get-tuple-element.59), channel_id=1, source_target_pairs={{0,2},{1,3},{2,0},{3,1},{4,6},{5,7},{6,4},{7,5},{8,10},{9,11},{10,... | collective-permute-start | bytes 589832 | tf_op jit(solution)/shard_map/ppermute | solution.py:291
  31.8 18.2 %all-to-all-start.1 = ((bf16[16,48,256]{2,1,0:T(8,128)(2,1)}), bf16[16,48,256]{2,1,0:T(8,128)(2,1)S(1)}, u32[]{:S(2)}, u32[]{:S(2)}) async-start(bf16[16,48,256]{2,1,0:T(8,128)(2,1)} %shard_map.77), calls=%async_computation.1 | async-start | bytes 786432 | tf_op jit(solution)/shard_map/all_to_all | solution.py:284
  36.5 4.5 %copy-start.5 = (f32[4,48,256]{2,1,0:T(8,128)S(1)}, f32[4,48,256]{2,1,0:T(8,128)}, u32[]{:S(2)}) copy-start(f32[4,48,256]{2,1,0:T(8,128)} %fusion.10) | copy-start | bytes 589828
  41.0 7.4 %collective-permute-start.5 = (f32[48,256]{1,0:T(8,128)S(1)}, f32[48,256]{1,0:T(8,128)S(1)}, u32[]{:S(2)}, u32[]{:S(2)}) collective-permute-start(f32[48,256]{1,0:T(8,128)S(1)} %get-tuple-element.63), channel_id=1, source_target_pairs={{0,12},{1,13},{2,14},{3,15},{4,0},{5,1},{6,2},{7,3},{8,4},{9,5},{1... | collective-permute-start | bytes 147464 | tf_op jit(solution)/shard_map/ppermute | solution.py:291
  41.2 7.2 %collective-permute-start.4 = (f32[48,256]{1,0:T(8,128)S(1)}, f32[48,256]{1,0:T(8,128)S(1)}, u32[]{:S(2)}, u32[]{:S(2)}) collective-permute-start(f32[48,256]{1,0:T(8,128)S(1)} %get-tuple-element.64), channel_id=1, source_target_pairs={{0,4},{1,5},{2,6},{3,7},{4,8},{5,9},{6,10},{7,11},{8,12},{9,13},{1... | collective-permute-start | bytes 147464 | tf_op jit(solution)/shard_map/ppermute | solution.py:291
  43.2 6.9 %collective-permute-start.3 = (f32[48,256]{1,0:T(8,128)S(1)}, f32[48,256]{1,0:T(8,128)S(1)}, u32[]{:S(2)}, u32[]{:S(2)}) collective-permute-start(f32[48,256]{1,0:T(8,128)S(1)} %get-tuple-element.62), channel_id=1, source_target_pairs={{0,8},{1,9},{2,10},{3,11},{4,12},{5,13},{6,14},{7,15},{8,0},{9,1},... | collective-permute-start | bytes 147464 | tf_op jit(solution)/shard_map/ppermute | solution.py:291
  50.0 1.6 copy-start.3
  122.4 16.0 %copy-start.2 = (bf16[256,4096]{1,0:T(8,128)(2,1)S(1)}, bf16[256,4096]{1,0:T(8,128)(2,1)}, u32[]{:S(2)}) copy-start(bf16[256,4096]{1,0:T(8,128)(2,1)} %get-tuple-element.44.w_ref.wlow_ref) | copy-start | bytes 6291460
  160.0 5.7 %collective-permute-start.6 = (bf16[8,16,4096]{2,1,0:T(8,128)(2,1)}, bf16[8,16,4096]{2,1,0:T(8,128)(2,1)S(1)}, u32[]{:S(2)}, u32[]{:S(2)}) collective-permute-start(bf16[8,16,4096]{2,1,0:T(8,128)(2,1)} %get-tuple-element.52), channel_id=1, source_target_pairs={{0,16},{16,0},{32,48},{48,32},{64,80},{80,64},{96,112},{112,96},{1... | collective-permute-start | bytes 3145736 | tf_op jit(solution)/shard_map/ppermute | solution.py:416
  160.2 21.2 %all-to-all-start.8 = ((bf16[16,64,256]{2,1,0:T(8,128)(2,1)}), bf16[16,64,256]{2,1,0:T(8,128)(2,1)S(1)}, u32[]{:S(2)}, u32[]{:S(2)}) async-start(bf16[16,64,256]{2,1,0:T(8,128)(2,1)} %get-tuple-element.50), calls=%async_computation.8 | async-start | bytes 1048576 | tf_op jit(solution)/shard_map/all_to_all | solution.py:284
  167.5 1.3 copy-start.4
  168.9 18.5 %collective-permute-start.9 = (bf16[2,16,4096]{2,1,0:T(8,128)(2,1)S(1)}, bf16[2,16,4096]{2,1,0:T(8,128)(2,1)S(1)}, u32[]{:S(2)}, u32[]{:S(2)}) collective-permute-start(bf16[2,16,4096]{2,1,0:T(8,128)(2,1)S(1)} %get-tuple-element.57), channel_id=1, source_target_pairs={{0,192},{16,208},{32,224},{48,240},{64,0},{80,16},{96,32},{112,48}... | collective-permute-start | bytes 786440 | tf_op jit(solution)/shard_map/ppermute | solution.py:291
  169.8 17.7 %collective-permute-start.8 = (bf16[2,16,4096]{2,1,0:T(8,128)(2,1)S(1)}, bf16[2,16,4096]{2,1,0:T(8,128)(2,1)S(1)}, u32[]{:S(2)}, u32[]{:S(2)}) collective-permute-start(bf16[2,16,4096]{2,1,0:T(8,128)(2,1)S(1)} %get-tuple-element.58), channel_id=1, source_target_pairs={{0,64},{16,80},{32,96},{48,112},{64,128},{80,144},{96,160},{112,17... | collective-permute-start | bytes 786440 | tf_op jit(solution)/shard_map/ppermute | solution.py:291
  171.0 16.4 %collective-permute-start.7 = (bf16[2,16,4096]{2,1,0:T(8,128)(2,1)S(1)}, bf16[2,16,4096]{2,1,0:T(8,128)(2,1)S(1)}, u32[]{:S(2)}, u32[]{:S(2)}) collective-permute-start(bf16[2,16,4096]{2,1,0:T(8,128)(2,1)S(1)} %get-tuple-element.56), channel_id=1, source_target_pairs={{0,128},{16,144},{32,160},{48,176},{64,192},{80,208},{96,224},{112... | collective-permute-start | bytes 786440 | tf_op jit(solution)/shard_map/ppermute | solution.py:291
  182.4 16.4 %all-to-all-start.9 = ((bf16[16,48,256]{2,1,0:T(8,128)(2,1)}), bf16[16,48,256]{2,1,0:T(8,128)(2,1)S(1)}, u32[]{:S(2)}, u32[]{:S(2)}) async-start(bf16[16,48,256]{2,1,0:T(8,128)(2,1)} %shard_map.86), calls=%async_computation.9 | async-start | bytes 786432 | tf_op jit(solution)/shard_map/all_to_all | solution.py:284
  199.8 17.3 %all-to-all-start.10 = ((bf16[16,16,128]{2,1,0:T(8,128)(2,1)}), bf16[16,16,128]{2,1,0:T(8,128)(2,1)S(1)}, u32[]{:S(2)}, u32[]{:S(2)}) async-start(bf16[16,16,128]{2,1,0:T(8,128)(2,1)} %bitcast.24), calls=%async_computation.10 | async-start | bytes 131072 | tf_op jit(solution)/shard_map/all_to_all | solution.py:284
  203.3 14.4 %collective-permute-start.10 = (bf16[16,4096]{1,0:T(8,128)(2,1)S(1)}, bf16[16,4096]{1,0:T(8,128)(2,1)S(1)}, u32[]{:S(2)}, u32[]{:S(2)}) collective-permute-start(bf16[16,4096]{1,0:T(8,128)(2,1)S(1)} %fusion.11), channel_id=1, source_target_pairs={{0,32},{16,48},{32,0},{48,16},{64,96},{80,112},{96,64},{112,80},{1... | collective-permute-start | bytes 393224 | tf_op jit(solution)/shard_map/ppermute | solution.py:422

commit v4 on v3

--- a/solution.py
+++ b/solution.py
@@ -15,8 +15,10 @@
 
 LANES = 128
 WIDE = 512
+GRAD_WIDE = 1024
 LIMIT = 16 * 2**20
 KEEP = jnp.float32
+HOPS = (2, 1, 3)
 BLOCK = 16
 
 
@@ -88,13 +90,31 @@
         out_ref[p] = unit
 
 
+def parts_kernel(at_ref, hidden_ref, weight_ref, *refs):
+    part_ref = refs[-1]
+    count, share, width = part_ref.shape
+    part = jnp.dot(hidden_ref[...], weight_ref[...], preferred_element_type=jnp.float32)
+    part_ref[...] = part.reshape(count, share, width)
+    for out_ref, hop in zip(refs[:-1], (0,) + HOPS):
+        for line in range(4):
+            out_ref[line] = part_ref[line * 4 + ((at_ref[0] + hop) & 3)]
+
+
+def line_kernel(at_ref, own_ref, one_ref, two_ref, three_ref, unused_ref, *refs):
+    sum_ref = refs[-1]
+    sum_ref[...] = own_ref[...] + one_ref[...] + two_ref[...] + three_ref[...]
+    for out_ref, hop in zip(refs[:-1], (0,) + HOPS):
+        out_ref[...] = sum_ref[(at_ref[0] + hop) & 3]
+
+
 def proj_kernel(got_ref, share_ref, out_ref):
     unit, scale = unit_rows(share_ref[...])
-    share, width = unit.shape
+    share = unit.shape[0]
     got = jnp.sum(got_ref[...].astype(jnp.float32), axis=0)
-    along = jnp.where(diagonal(share, width), got[share : share + 1], 0.0)
+    along = jnp.where(diagonal(share, LANES), got[2 * share : 2 * share + 1], 0.0)
     low = unit.astype(jnp.bfloat16).astype(jnp.float32)
-    feat = got[:share] + low * jnp.sum(along, axis=1, keepdims=True)
+    feat = jnp.concatenate([got[:share], got[share : 2 * share]], axis=1)
+    feat = feat + low * jnp.sum(along, axis=1, keepdims=True)
     inner = jnp.sum(unit * feat, axis=1, keepdims=True)
     rows = (scale * (feat - unit * inner)).astype(out_ref.dtype)
     for p in range(out_ref.shape[0]):
@@ -215,12 +235,12 @@
     core = core_ref[0]
     low = low_ref[...]
     stores = []
-    for k in range(columns // WIDE):
-        cols = pl.ds(k * WIDE, WIDE)
+    for k in range(columns // GRAD_WIDE):
+        cols = pl.ds(k * GRAD_WIDE, GRAD_WIDE)
         pieces = []
-        for t in range(WIDE // LANES):
-            at = pl.ds(k * WIDE + t * LANES, LANES)
-            scale = colscale_ref[pl.ds(k * (WIDE // LANES) + t, 1), :]
+        for t in range(GRAD_WIDE // LANES):
+            at = pl.ds(k * GRAD_WIDE + t * LANES, LANES)
+            scale = colscale_ref[pl.ds(k * (GRAD_WIDE // LANES) + t, 1), :]
             pieces.append(
                 (
                     stud_ref[:, at].astype(jnp.float32) * prob_ref[...]
@@ -239,7 +259,7 @@
         unit = raw_ref[:, cols].astype(jnp.float32) * norm
         dots = jnp.sum(unit * proto, axis=0, keepdims=True)
         part = norm * (proto - unit * dots)
-        part = part.reshape(8, 2, 16, WIDE)
+        part = part.reshape(8, 2, 16, GRAD_WIDE)
         slot = k % 2
         if k >= 2:
             for copy in stores[k - 2]:
@@ -264,14 +284,15 @@
     feat = (feat - low * inner).astype(jnp.bfloat16)
     count = feat_ref.shape[0]
     share = rows // count
-    spot = diagonal(share, feat.shape[1])
+    spot = diagonal(share, LANES)
     for p in range(count):
         mine = slice(p * share, (p + 1) * share)
-        feat_ref[p, pl.ds(0, share), :] = feat[mine]
+        feat_ref[p, pl.ds(0, share), :] = feat[mine, :LANES]
+        feat_ref[p, pl.ds(share, share), :] = feat[mine, LANES:]
         along = jnp.sum(jnp.where(spot, inner[mine], 0.0), axis=0, keepdims=True)
-        feat_ref[p, pl.ds(share, BLOCK), :] = jnp.broadcast_to(
-            along, (BLOCK, feat.shape[1])
-        ).astype(jnp.bfloat16)
+        feat_ref[p, pl.ds(2 * share, BLOCK), :] = jnp.broadcast_to(along, (BLOCK, LANES)).astype(
+            jnp.bfloat16
+        )
     last = pltpu.make_async_copy(feat_ref, feat_far, out_sems.at[2, 0])
     last.start()
     for pair in stores[-2:]:
@@ -286,7 +307,7 @@
 
 def spread_sum(parts, axis, dim, me, target, dtype=jnp.float32):
     total = lax.dynamic_index_in_dim(parts, me, dim, keepdims=False)
-    for hop in (2, 1, 3):
+    for hop in HOPS:
         part = lax.dynamic_index_in_dim(parts, (me + hop) % 4, dim, keepdims=False).astype(dtype)
         got = lax.ppermute(part, axis, [(i, target(i, hop)) for i in range(16)])
         total = total + got.astype(jnp.float32)
@@ -320,19 +341,39 @@
     share = rows // n_proto
     teach_norm = col_scales(teacher_prototypes)
     stud_norm = col_scales(student_prototypes)
-    stud_part = jnp.dot(student_hidden, student_bottleneck, preferred_element_type=f32)
-    stud_part = stud_part.reshape(4, 4, share, width)
-    stud_line = spread_sum(stud_part, "proto", 1, me % 4, lambda i, hop: i // 4 * 4 + (i + hop) % 4)
+    own, *sends = on_core(
+        parts_kernel,
+        [shape((4, share, width), f32)] * 4,
+        (jnp.reshape(me % 4, (1,)), student_hidden, student_bottleneck),
+        scratch=[pltpu.VMEM((n_proto, share, width), f32)],
+        smem=(0,),
+    )
+    line = [own]
+    for hop, part in zip(HOPS, sends):
+        line.append(
+            lax.ppermute(part, "proto", [(i, i // 4 * 4 + (i + hop) % 4) for i in range(16)])
+        )
 
     (copies,) = on_core(share_kernel, [shape(got.shape, bf16)], (got,))
-    copies, teach_norm, stud_norm, stud_line = lax.optimization_barrier(
-        (copies, teach_norm, stud_norm, stud_line)
+    copies, teach_norm, stud_norm, line[0] = lax.optimization_barrier(
+        (copies, teach_norm, stud_norm, own)
     )
     teach_low = exchange(copies, "proto").reshape(rows, width)
     teach_wlow = (teacher_prototypes.astype(f32) * teach_norm).astype(bf16)
     stud_wlow = (student_prototypes.astype(f32) * stud_norm).astype(bf16)
-    teach_wlow, stud_wlow, stud_line = lax.optimization_barrier((teach_wlow, stud_wlow, stud_line))
-    stud_share = spread_sum(stud_line, "proto", 0, me // 4, lambda i, hop: (i + 4 * hop) % 16)
+    stud_share, *sends = on_core(
+        line_kernel,
+        [shape((share, width), f32)] * 4,
+        [jnp.reshape(me // 4, (1,))] + line + [copies],
+        scratch=[pltpu.VMEM((4, share, width), f32)],
+        smem=(0,),
+        far=(5,),
+    )
+    teach_wlow, stud_wlow, *sends = lax.optimization_barrier((teach_wlow, stud_wlow, *sends))
+    for hop, part in zip(HOPS, sends):
+        stud_share = stud_share + lax.ppermute(
+            part, "proto", [(i, (i + 4 * hop) % 16) for i in range(16)]
+        )
 
     teach_low, teach_wlow, stud_norm, stud_wlow, stud_share, core, high, y_at = (
         lax.optimization_barrier(
@@ -387,7 +428,7 @@
     feat_part, keep, send = on_core(
         grad_kernel,
         [
-            pltpu.HBM((n_proto, share + BLOCK, width), bf16),
+            pltpu.HBM((n_proto, 2 * share + BLOCK, LANES), bf16),
             pltpu.HBM((8, 16, columns), f32),
             pltpu.HBM((8, 16, columns), bf16),
         ],
@@ -396,9 +437,9 @@
             student_prototypes, stud_norm, got_cols, got_rows,
         ),
         scratch=[
-            pltpu.VMEM((n_proto, share + BLOCK, width), bf16),
-            pltpu.VMEM((2, 8, 16, WIDE), f32),
-            pltpu.VMEM((2, 8, 16, WIDE), bf16),
+            pltpu.VMEM((n_proto, 2 * share + BLOCK, LANES), bf16),
+            pltpu.VMEM((2, 8, 16, GRAD_WIDE), f32),
+            pltpu.VMEM((2, 8, 16, GRAD_WIDE), bf16),
             pltpu.SemaphoreType.DMA((3, 2)),
             pltpu.VMEM((rows, LANES), f32),
             pltpu.VMEM((rows, LANES), f32),

time: 219 us -> 213 us (0.973)
  waiting for transfers between devices: 38.7 us -> 28.5 us
  Pallas kernels: 19.5 us -> 21.7 us
    ppermute x0 -> x6, starting transfers between devices: none -> 12.4 us  [the longest x3 6.21 us: on_device(): lax.ppermute(part, 'proto', [(i, i // 4 * 4 + (i + hop) % 4) for i in ran...]
    ppermute x9 -> x3, starting transfers between devices: 14.2 us -> 2.93 us  [spread_sum(): got = lax.ppermute(part, axis, [(i, target(i, hop)) for i in range(16)])]
    ppermute x9 -> x3, waiting for transfers between devices: 11 us -> 0.01 us  [spread_sum(): got = lax.ppermute(part, axis, [(i, target(i, hop)) for i in range(16)])]
    ppermute x0 -> x6, waiting for transfers between devices: none -> 2.81 us  [the longest x3 2.8 us: on_device(): lax.ppermute(part, 'proto', [(i, (i + 4 * hop) % 16) for i in range(16)])]
    pallas_call x10 -> x12, Pallas kernels: 19.5 us -> 21.7 us  [on_core(): pl.pallas_call(kernel, out_shape=tuple(outs), in_specs=[pl.BlockSpec(memo...]
  transfers between devices with their start and end apart: 16 -> 16, of which waited for: 7 -> 6; matrix products, arithmetic and copies ran while one was open for 7% -> 6% of each run, Pallas kernels for 0% -> 2%
where the time goes in v4:
time: 213 us; the launch traced here: 212 us
  blocking collectives  90.8 us (43%)
  starting transfers between devices  48.8 us (23%)
  waiting for transfers between devices  28.5 us (13%)
  Pallas kernels  21.7 us (10%)
  other arithmetic  12.6 us (6%)
  local copies, waits for them, and re-layouts  5.73 us (3%)
  matrix products  2.91 us (1%)
    all_to_all x6, blocking collectives, exchange(): return lax.all_to_all(copies, axis, 0, 0, tiled=True)  90.8 us
    all_to_all x5, starting transfers between devices, exchange(): return lax.all_to_all(copies, axis, 0, 0, tiled=True)  27.6 us
    all_to_all x5, waiting for transfers between devices, exchange(): return lax.all_to_all(copies, axis, 0, 0, tiled=True)  25.7 us
    pallas_call x12, Pallas kernels, on_core(): pl.pallas_call(kernel, out_shape=tuple(outs), in_specs=[pl.BlockSpec(memo...  21.7 us
    ppermute x3, starting transfers between devices, on_device(): lax.ppermute(part, 'proto', [(i, i // 4 * 4 + (i + hop) % 4) for i in ran...  6.21 us
    ppermute x3, starting transfers between devices, on_device(): lax.ppermute(part, 'proto', [(i, (i + 4 * hop) % 16) for i in range(16)])  6.19 us
    ppermute x1, starting transfers between devices, on_device(): got = lax.ppermute(send, 'dp', [(i, i ^ 2) for i in range(16)])  5.8 us
    convert_element_type x1, other arithmetic, on_device(): teach_wlow = (teacher_prototypes.astype(f32) * teach_norm).astype(bf16)  4.49 us
  transfers between devices with their start and end apart: 16, of which 6 were waited for; matrix products, arithmetic and copies ran while one was open for 6% of the time, Pallas kernels for 2%

profile of v4, /device:TPU:32, one launch (start us, length us, event | category | flops | bytes accessed | tf_op | source)
XLA Modules:
  0.0 212.0 jit_solution(16297524508444864654)
XLA Ops:
  0.6 0.9 copy-done
  1.6 2.0 convolution_convert_fusion
  3.5 8.5 %all-to-all-start = ((bf16[16,48,256]{2,1,0:T(8,128)(2,1)}), bf16[16,48,256]{2,1,0:T(8,128)(2,1)S(1)}, u32[]{:S(2)}, u32[]{:S(2)}) async-start(bf16[16,48,256]{2,1,0:T(8,128)(2,1)} %bitcast), calls=%async_computation | async-start | bytes 786432 | tf_op jit(solution)/shard_map/all_to_all | solution.py:305
  12.0 0.9 copy-done.4
  13.0 0.8 copy-done.6
  13.8 1.1 shard_map.78
  14.9 3.0 %collective-permute-start = (f32[4,48,256]{2,1,0:T(8,128)}, f32[4,48,256]{2,1,0:T(8,128)S(1)}, u32[]{:S(2)}, u32[]{:S(2)}) collective-permute-start(f32[4,48,256]{2,1,0:T(8,128)} %get-tuple-element.44), channel_id=1, source_target_pairs={{0,2},{1,3},{2,0},{3,1},{4,6},{5,7},{6,4},{7,5},{8,10},{9,11},{10,... | collective-permute-start | bytes 589832 | tf_op jit(solution)/shard_map/ppermute | solution.py:354
  18.5 2.7 %collective-permute-start.2 = (f32[4,48,256]{2,1,0:T(8,128)}, f32[4,48,256]{2,1,0:T(8,128)S(1)}, u32[]{:S(2)}, u32[]{:S(2)}) collective-permute-start(f32[4,48,256]{2,1,0:T(8,128)} %get-tuple-element.46), channel_id=1, source_target_pairs={{0,3},{1,0},{2,1},{3,2},{4,7},{5,4},{6,5},{7,6},{8,11},{9,8},{10,9... | collective-permute-start | bytes 589832 | tf_op jit(solution)/shard_map/ppermute | solution.py:354
  21.1 2.0 fusion
  24.3 0.9 shard_map.77.unused_ref
  25.2 5.0 %all-to-all-start.1 = ((bf16[16,48,256]{2,1,0:T(8,128)(2,1)}), bf16[16,48,256]{2,1,0:T(8,128)(2,1)S(1)}, u32[]{:S(2)}, u32[]{:S(2)}) async-start(bf16[16,48,256]{2,1,0:T(8,128)(2,1)} %shard_map.77.unused_ref), calls=%async_computation.1 | async-start | bytes 786432 | tf_op jit(solution)/shard_map/all_to_all | solution.py:305
  30.2 4.5 %fusion.1 = (bf16[256,4096]{1,0:T(8,128)(2,1)}, bf16[256,4096]{1,0:T(8,128)(2,1)}) fusion(bf16[256,4096]{1,0:T(8,128)(2,1)} %param.10, f32[4096]{0:T(1024)S(1)} %add_rsqrt_fusion.1, f32[4096]{0:T(1024)S(1)} %add_rsqrt_fusion, bf16[256,4096]{1,0:T(8,128)(2,1)S(1)} %copy-done.1), kind=kLoop, calls=%fused_computation.5 | loop fusion | flops 6291456 | bytes 8421376 | tf_op jit(solution)/shard_map/convert_element_type | solution.py:362
  34.7 0.7 shard_map.79
  35.5 1.9 collective-permute-start.4
  37.4 4.2 %collective-permute-start.3 = (f32[48,256]{1,0:T(8,128)}, f32[48,256]{1,0:T(8,128)S(1)}, u32[]{:S(2)}, u32[]{:S(2)}) collective-permute-start(f32[48,256]{1,0:T(8,128)} %get-tuple-element.53), channel_id=1, source_target_pairs={{0,8},{1,9},{2,10},{3,11},{4,12},{5,13},{6,14},{7,15},{8,0},{9,1},... | collective-permute-start | bytes 147464 | tf_op jit(solution)/shard_map/ppermute | solution.py:374
  41.6 0.7 collective-permute-done.5
  42.3 2.1 collective-permute-done.3
  44.4 1.6 copy-done.3
  46.0 1.8 shard_map.80
  47.8 18.9 %all_to_all.55.got_ref = bf16[16,32,128]{2,1,0:T(8,128)(2,1)S(1)} all-to-all(bf16[16,32,128]{2,1,0:T(8,128)(2,1)S(1)} %get-tuple-element.61), channel_id=1, replica_groups=mesh['dp'=16,'proto'=16] {'dp'}, dimensions={0} | all-to-all | bytes 262144 | tf_op jit(solution)/shard_map/all_to_all | solution.py:305
  66.7 1.5 shard_map.81
  68.2 14.0 %all_to_all.56.got_ref = bf16[16,16,128]{2,1,0:T(8,128)(2,1)S(1)} all-to-all(bf16[16,16,128]{2,1,0:T(8,128)(2,1)S(1)} %shard_map.81), channel_id=1, replica_groups=mesh['dp'=16,'proto'=16] {'proto'}, dimensions={0} | all-to-all | bytes 131072 | tf_op jit(solution)/shard_map/all_to_all | solution.py:305
  82.2 1.3 shard_map.82
  83.5 14.6 %all_to_all.57.got_ref = bf16[16,32,128]{2,1,0:T(8,128)(2,1)S(1)} all-to-all(bf16[16,32,128]{2,1,0:T(8,128)(2,1)S(1)} %shard_map.82), channel_id=1, replica_groups=mesh['dp'=16,'proto'=16] {'dp'}, dimensions={0} | all-to-all | bytes 262144 | tf_op jit(solution)/shard_map/all_to_all | solution.py:305
  98.2 1.5 shard_map.83
  99.7 17.4 %all_to_all.58.got_ref = bf16[16,112,128]{2,1,0:T(8,128)(2,1)S(1)} all-to-all(bf16[16,112,128]{2,1,0:T(8,128)(2,1)S(1)} %shard_map.83), channel_id=1, replica_groups=mesh['dp'=16,'proto'=16] {'proto'}, dimensions={0} | all-to-all | bytes 917504 | tf_op jit(solution)/shard_map/all_to_all | solution.py:305
  117.1 1.3 shard_map.84
  118.4 14.6 %all_to_all.59.got_ref.cols_ref = bf16[16,32,128]{2,1,0:T(8,128)(2,1)S(1)} all-to-all(bf16[16,32,128]{2,1,0:T(8,128)(2,1)S(1)} %shard_map.84), channel_id=1, replica_groups=mesh['dp'=16,'proto'=16] {'dp'}, dimensions={0} | all-to-all | bytes 262144 | tf_op jit(solution)/shard_map/all_to_all | solution.py:305
  133.1 1.9 shard_map.85
  135.0 1.5 shard_map.86
  136.5 11.2 %all_to_all.60.rows_ref = bf16[16,32,128]{2,1,0:T(8,128)(2,1)S(1)} all-to-all(bf16[16,32,128]{2,1,0:T(8,128)(2,1)S(1)} %shard_map.86), channel_id=1, replica_groups=mesh['dp'=16,'proto'=16] {'proto'}, dimensions={0} | all-to-all | bytes 262144 | tf_op jit(solution)/shard_map/all_to_all | solution.py:305
  147.7 7.1 %shard_map.87 = (bf16[16,112,128]{2,1,0:T(8,128)(2,1)}, f32[8,16,4096]{2,1,0:T(8,128)}, bf16[8,16,4096]{2,1,0:T(8,128)(2,1)}) custom-call(s32[1]{0:T(128)} %bitcast.8.core_ref, f32[768,4096]{1,0:T(8,128)S(1)} %get-tuple-element.60.expo_ref, bf16[768,4096]{1,0:T(8,128)(2,1)S(1)} %get-tuple-element.65.stud_ref, ...), custom_call_target="tpu_custom_call" | custom-call | tf_op jit(solution)/shard_map/pallas_call | solution.py:46
  155.0 5.5 %all-to-all-start.8 = ((bf16[16,112,128]{2,1,0:T(8,128)(2,1)}), bf16[16,112,128]{2,1,0:T(8,128)(2,1)S(1)}, u32[]{:S(2)}, u32[]{:S(2)}) async-start(bf16[16,112,128]{2,1,0:T(8,128)(2,1)} %get-tuple-element.70), calls=%async_computation.8 | async-start | bytes 917504 | tf_op jit(solution)/shard_map/all_to_all | solution.py:305
  160.5 3.1 %convert_add_fusion = f32[8,16,4096]{2,1,0:T(8,128)} fusion(f32[8,16,4096]{2,1,0:T(8,128)} %get-tuple-element.71, bf16[8,16,4096]{2,1,0:T(8,128)(2,1)S(1)} %collective-permute-done.6), kind=kLoop, calls=%fused_computation.8 | loop fusion | flops 1048576 | bytes 5242880 | tf_op jit(solution)/shard_map/add | solution.py:458
  163.6 1.4 fusion.6
  165.1 0.8 collective-permute-start.9
  165.9 1.3 collective-permute-start.8
  167.2 0.8 collective-permute-start.7
  168.0 6.8 %all-to-all-done.8.got_ref = bf16[16,112,128]{2,1,0:T(8,128)(2,1)S(1)} async-done(((bf16[16,112,128]{2,1,0:T(8,128)(2,1)}), bf16[16,112,128]{2,1,0:T(8,128)(2,1)S(1)}, u32[]{:S(2)}, u32[]{:S(2)}) %all-to-all-start.8) | async-done | bytes 458784 | tf_op jit(solution)/shard_map/all_to_all | solution.py:305
  174.9 1.0 shard_map.88
  175.8 5.1 %all-to-all-start.9 = ((bf16[16,48,256]{2,1,0:T(8,128)(2,1)}), bf16[16,48,256]{2,1,0:T(8,128)(2,1)S(1)}, u32[]{:S(2)}, u32[]{:S(2)}) async-start(bf16[16,48,256]{2,1,0:T(8,128)(2,1)} %shard_map.88), calls=%async_computation.9 | async-start | bytes 786432 | tf_op jit(solution)/shard_map/all_to_all | solution.py:305
  180.9 1.2 fusion.5
  182.1 10.2 %all-to-all-done.9 = bf16[16,48,256]{2,1,0:T(8,128)(2,1)S(1)} async-done(((bf16[16,48,256]{2,1,0:T(8,128)(2,1)}), bf16[16,48,256]{2,1,0:T(8,128)(2,1)S(1)}, u32[]{:S(2)}, u32[]{:S(2)}) %all-to-all-start.9) | async-done | bytes 393248 | tf_op jit(solution)/shard_map/all_to_all | solution.py:305
  192.3 0.9 convolution_convert_fusion.1
  193.3 3.5 %all-to-all-start.10 = ((bf16[16,16,128]{2,1,0:T(8,128)(2,1)}), bf16[16,16,128]{2,1,0:T(8,128)(2,1)S(1)}, u32[]{:S(2)}, u32[]{:S(2)}) async-start(bf16[16,16,128]{2,1,0:T(8,128)(2,1)} %bitcast.17), calls=%async_computation.10 | async-start | bytes 131072 | tf_op jit(solution)/shard_map/all_to_all | solution.py:305
  196.8 5.8 %collective-permute-start.10 = (bf16[16,4096]{1,0:T(8,128)(2,1)S(1)}, bf16[16,4096]{1,0:T(8,128)(2,1)S(1)}, u32[]{:S(2)}, u32[]{:S(2)}) collective-permute-start(bf16[16,4096]{1,0:T(8,128)(2,1)S(1)} %fusion.9), channel_id=1, source_target_pairs={{0,32},{16,48},{32,0},{48,16},{64,96},{80,112},{96,64},{112,80},{1... | collective-permute-start | bytes 393224 | tf_op jit(solution)/shard_map/ppermute | solution.py:463
  202.6 8.0 %all-to-all-done.10 = bf16[16,16,128]{2,1,0:T(8,128)(2,1)S(1)} async-done(((bf16[16,16,128]{2,1,0:T(8,128)(2,1)}), bf16[16,16,128]{2,1,0:T(8,128)(2,1)S(1)}, u32[]{:S(2)}, u32[]{:S(2)}) %all-to-all-start.10) | async-done | bytes 65568 | tf_op jit(solution)/shard_map/all_to_all | solution.py:305
  211.2 0.7 bitcast_add_fusion.1
  (30 shorter events, 2.5 us)
Async XLA Ops:
  0.6 0.9 copy-start
  1.6 21.6 %copy-start.1 = (bf16[256,4096]{1,0:T(8,128)(2,1)S(1)}, bf16[256,4096]{1,0:T(8,128)(2,1)}, u32[]{:S(2)}) copy-start(bf16[256,4096]{1,0:T(8,128)(2,1)} %raw_ref.1) | copy-start | bytes 6291460
  3.5 20.7 %all-to-all-start = ((bf16[16,48,256]{2,1,0:T(8,128)(2,1)}), bf16[16,48,256]{2,1,0:T(8,128)(2,1)S(1)}, u32[]{:S(2)}, u32[]{:S(2)}) async-start(bf16[16,48,256]{2,1,0:T(8,128)(2,1)} %bitcast), calls=%async_computation | async-start | bytes 786432 | tf_op jit(solution)/shard_map/all_to_all | solution.py:305
  12.0 0.9 copy-start.4
  13.0 0.8 copy-start.6
  14.9 19.8 %collective-permute-start = (f32[4,48,256]{2,1,0:T(8,128)}, f32[4,48,256]{2,1,0:T(8,128)S(1)}, u32[]{:S(2)}, u32[]{:S(2)}) collective-permute-start(f32[4,48,256]{2,1,0:T(8,128)} %get-tuple-element.44), channel_id=1, source_target_pairs={{0,2},{1,3},{2,0},{3,1},{4,6},{5,7},{6,4},{7,5},{8,10},{9,11},{10,... | collective-permute-start | bytes 589832 | tf_op jit(solution)/shard_map/ppermute | solution.py:354
  17.9 16.8 %collective-permute-start.1 = (f32[4,48,256]{2,1,0:T(8,128)}, f32[4,48,256]{2,1,0:T(8,128)S(1)}, u32[]{:S(2)}, u32[]{:S(2)}) collective-permute-start(f32[4,48,256]{2,1,0:T(8,128)} %get-tuple-element.45), channel_id=1, source_target_pairs={{0,1},{1,2},{2,3},{3,0},{4,5},{5,6},{6,7},{7,4},{8,9},{9,10},{10,1... | collective-permute-start | bytes 589832 | tf_op jit(solution)/shard_map/ppermute | solution.py:354
  18.5 16.2 %collective-permute-start.2 = (f32[4,48,256]{2,1,0:T(8,128)}, f32[4,48,256]{2,1,0:T(8,128)S(1)}, u32[]{:S(2)}, u32[]{:S(2)}) collective-permute-start(f32[4,48,256]{2,1,0:T(8,128)} %get-tuple-element.46), channel_id=1, source_target_pairs={{0,3},{1,0},{2,1},{3,2},{4,7},{5,4},{6,5},{7,6},{8,11},{9,8},{10,9... | collective-permute-start | bytes 589832 | tf_op jit(solution)/shard_map/ppermute | solution.py:354
  25.2 19.2 %all-to-all-start.1 = ((bf16[16,48,256]{2,1,0:T(8,128)(2,1)}), bf16[16,48,256]{2,1,0:T(8,128)(2,1)S(1)}, u32[]{:S(2)}, u32[]{:S(2)}) async-start(bf16[16,48,256]{2,1,0:T(8,128)(2,1)} %shard_map.77.unused_ref), calls=%async_computation.1 | async-start | bytes 786432 | tf_op jit(solution)/shard_map/all_to_all | solution.py:305
  35.4 6.9 %collective-permute-start.5 = (f32[48,256]{1,0:T(8,128)}, f32[48,256]{1,0:T(8,128)S(1)}, u32[]{:S(2)}, u32[]{:S(2)}) collective-permute-start(f32[48,256]{1,0:T(8,128)} %get-tuple-element.55), channel_id=1, source_target_pairs={{0,12},{1,13},{2,14},{3,15},{4,0},{5,1},{6,2},{7,3},{8,4},{9,5},{1... | collective-permute-start | bytes 147464 | tf_op jit(solution)/shard_map/ppermute | solution.py:374
  35.5 6.8 %collective-permute-start.4 = (f32[48,256]{1,0:T(8,128)}, f32[48,256]{1,0:T(8,128)S(1)}, u32[]{:S(2)}, u32[]{:S(2)}) collective-permute-start(f32[48,256]{1,0:T(8,128)} %get-tuple-element.54), channel_id=1, source_target_pairs={{0,4},{1,5},{2,6},{3,7},{4,8},{5,9},{6,10},{7,11},{8,12},{9,13},{1... | collective-permute-start | bytes 147464 | tf_op jit(solution)/shard_map/ppermute | solution.py:374
  37.4 7.0 %collective-permute-start.3 = (f32[48,256]{1,0:T(8,128)}, f32[48,256]{1,0:T(8,128)S(1)}, u32[]{:S(2)}, u32[]{:S(2)}) collective-permute-start(f32[48,256]{1,0:T(8,128)} %get-tuple-element.53), channel_id=1, source_target_pairs={{0,8},{1,9},{2,10},{3,11},{4,12},{5,13},{6,14},{7,15},{8,0},{9,1},... | collective-permute-start | bytes 147464 | tf_op jit(solution)/shard_map/ppermute | solution.py:374
  44.4 1.6 copy-start.3
  117.1 16.0 %copy-start.2 = (bf16[256,4096]{1,0:T(8,128)(2,1)S(1)}, bf16[256,4096]{1,0:T(8,128)(2,1)}, u32[]{:S(2)}) copy-start(bf16[256,4096]{1,0:T(8,128)(2,1)} %get-tuple-element.64.w_ref.wlow_ref) | copy-start | bytes 6291460
  154.9 5.7 %collective-permute-start.6 = (bf16[8,16,4096]{2,1,0:T(8,128)(2,1)}, bf16[8,16,4096]{2,1,0:T(8,128)(2,1)S(1)}, u32[]{:S(2)}, u32[]{:S(2)}) collective-permute-start(bf16[8,16,4096]{2,1,0:T(8,128)(2,1)} %get-tuple-element.72), channel_id=1, source_target_pairs={{0,16},{16,0},{32,48},{48,32},{64,80},{80,64},{96,112},{112,96},{1... | collective-permute-start | bytes 3145736 | tf_op jit(solution)/shard_map/ppermute | solution.py:457
  155.0 19.8 %all-to-all-start.8 = ((bf16[16,112,128]{2,1,0:T(8,128)(2,1)}), bf16[16,112,128]{2,1,0:T(8,128)(2,1)S(1)}, u32[]{:S(2)}, u32[]{:S(2)}) async-start(bf16[16,112,128]{2,1,0:T(8,128)(2,1)} %get-tuple-element.70), calls=%async_computation.8 | async-start | bytes 917504 | tf_op jit(solution)/shard_map/all_to_all | solution.py:305
  165.1 27.3 %copy-start.5 = (bf16[768,128]{1,0:T(8,128)(2,1)S(1)}, bf16[768,128]{1,0:T(8,128)(2,1)}, u32[]{:S(2)}) copy-start(bf16[768,128]{1,0:T(8,128)(2,1)} %hidden_ref.1) | copy-start | bytes 589828
  165.1 15.8 %collective-permute-start.9 = (bf16[2,16,4096]{2,1,0:T(8,128)(2,1)S(1)}, bf16[2,16,4096]{2,1,0:T(8,128)(2,1)S(1)}, u32[]{:S(2)}, u32[]{:S(2)}) collective-permute-start(bf16[2,16,4096]{2,1,0:T(8,128)(2,1)S(1)} %get-tuple-element.77), channel_id=1, source_target_pairs={{0,192},{16,208},{32,224},{48,240},{64,0},{80,16},{96,32},{112,48}... | collective-permute-start | bytes 786440 | tf_op jit(solution)/shard_map/ppermute | solution.py:312
  165.9 15.0 %collective-permute-start.8 = (bf16[2,16,4096]{2,1,0:T(8,128)(2,1)S(1)}, bf16[2,16,4096]{2,1,0:T(8,128)(2,1)S(1)}, u32[]{:S(2)}, u32[]{:S(2)}) collective-permute-start(bf16[2,16,4096]{2,1,0:T(8,128)(2,1)S(1)} %get-tuple-element.78), channel_id=1, source_target_pairs={{0,64},{16,80},{32,96},{48,112},{64,128},{80,144},{96,160},{112,17... | collective-permute-start | bytes 786440 | tf_op jit(solution)/shard_map/ppermute | solution.py:312
  167.2 13.7 %collective-permute-start.7 = (bf16[2,16,4096]{2,1,0:T(8,128)(2,1)S(1)}, bf16[2,16,4096]{2,1,0:T(8,128)(2,1)S(1)}, u32[]{:S(2)}, u32[]{:S(2)}) collective-permute-start(bf16[2,16,4096]{2,1,0:T(8,128)(2,1)S(1)} %get-tuple-element.76), channel_id=1, source_target_pairs={{0,128},{16,144},{32,160},{48,176},{64,192},{80,208},{96,224},{112... | collective-permute-start | bytes 786440 | tf_op jit(solution)/shard_map/ppermute | solution.py:312
  175.8 16.5 %all-to-all-start.9 = ((bf16[16,48,256]{2,1,0:T(8,128)(2,1)}), bf16[16,48,256]{2,1,0:T(8,128)(2,1)S(1)}, u32[]{:S(2)}, u32[]{:S(2)}) async-start(bf16[16,48,256]{2,1,0:T(8,128)(2,1)} %shard_map.88), calls=%async_computation.9 | async-start | bytes 786432 | tf_op jit(solution)/shard_map/all_to_all | solution.py:305
  193.3 17.3 %all-to-all-start.10 = ((bf16[16,16,128]{2,1,0:T(8,128)(2,1)}), bf16[16,16,128]{2,1,0:T(8,128)(2,1)S(1)}, u32[]{:S(2)}, u32[]{:S(2)}) async-start(bf16[16,16,128]{2,1,0:T(8,128)(2,1)} %bitcast.17), calls=%async_computation.10 | async-start | bytes 131072 | tf_op jit(solution)/shard_map/all_to_all | solution.py:305
  196.8 14.4 %collective-permute-start.10 = (bf16[16,4096]{1,0:T(8,128)(2,1)S(1)}, bf16[16,4096]{1,0:T(8,128)(2,1)S(1)}, u32[]{:S(2)}, u32[]{:S(2)}) collective-permute-start(bf16[16,4096]{1,0:T(8,128)(2,1)S(1)} %fusion.9), channel_id=1, source_target_pairs={{0,32},{16,48},{32,0},{48,16},{64,96},{80,112},{96,64},{112,80},{1... | collective-permute-start | bytes 393224 | tf_op jit(solution)/shard_map/ppermute | solution.py:463

commit v5 on v4

--- a/solution.py
+++ b/solution.py
@@ -1,3 +1,5 @@
+import functools
+
 import jax
 import jax.numpy as jnp
 from jax import lax
@@ -136,12 +138,12 @@
         out_ref[p] = sums
 
 
-def student_kernel(got_ref, w_ref, expo_ref, totals_ref, low_ref, acc_ref, sums_ref):
-    share = (got_ref.shape[1] - BLOCK) // 2
-    for p in range(got_ref.shape[0]):
-        for half in range(2):
+def student_kernel(first_ref, second_ref, w_ref, expo_ref, totals_ref, low_ref, acc_ref, sums_ref):
+    share = first_ref.shape[1] - BLOCK
+    for p in range(first_ref.shape[0]):
+        for half, got_ref in enumerate((first_ref, second_ref)):
             low_ref[pl.ds(p * share, share), pl.ds(half * LANES, LANES)] = got_ref[
-                p, pl.ds(BLOCK + half * share, share), :
+                p, pl.ds(BLOCK, share), :
             ]
     low = low_ref[...]
     for k in range(w_ref.shape[1] // WIDE):
@@ -154,7 +156,7 @@
     put_row_sums(acc_ref, totals_ref, sums_ref)
 
 
-def row_kernel(expo_ref, got_ref, *refs):
+def row_kernel(half, expo_ref, got_ref, *refs):
     extra_ref = refs[0] if len(refs) == 5 else None
     out_ref, scale_ref, acc_ref, sums_ref = refs[-4:]
     rows, columns = expo_ref.shape
@@ -181,11 +183,9 @@
             out_ref[p, pl.ds(BLOCK, BLOCK), :] = extra_ref[0]
     elif extra_ref is not None:
         unit, unused_scale = unit_rows(extra_ref[...])
-        unit = unit.astype(out_ref.dtype)
-        share = unit.shape[0]
+        unit = unit[:, half * LANES : (half + 1) * LANES].astype(out_ref.dtype)
         for p in range(out_ref.shape[0]):
-            out_ref[p, pl.ds(BLOCK, share), :] = unit[:, :LANES]
-            out_ref[p, pl.ds(BLOCK + share, share), :] = unit[:, LANES:]
+            out_ref[p, pl.ds(BLOCK, unit.shape[0]), :] = unit
 
 
 def col_kernel(expo_ref, got_ref, out_ref, scale_ref, sums_ref):
@@ -369,7 +369,6 @@
         smem=(0,),
         far=(5,),
     )
-    teach_wlow, stud_wlow, *sends = lax.optimization_barrier((teach_wlow, stud_wlow, *sends))
     for hop, part in zip(HOPS, sends):
         stud_share = stud_share + lax.ppermute(
             part, "proto", [(i, (i + 4 * hop) % 16) for i in range(16)]
@@ -390,13 +389,14 @@
         (teach_low, teach_wlow),
         scratch=[col_sums],
     )
+    halves = []
     for step in range(ITERS):
         got_cols = exchange(copies, "dp")
         count, extra = BLOCK, ()
-        if step == ITERS - 2:
-            count, extra = BLOCK + 2 * share, (stud_share,)
+        if step < ITERS - 1:
+            count, extra = BLOCK + share, (stud_share,)
         if step == ITERS - 1:
-            got_rows, got_cols = lax.optimization_barrier((got_rows, got_cols))
+            halves[1], got_cols = lax.optimization_barrier((halves[1], got_cols))
             stud_expo, totals, stud_low = on_core(
                 student_kernel,
                 [
@@ -404,18 +404,19 @@
                     shape((1, BLOCK, LANES), bf16),
                     shape((rows, width), bf16),
                 ],
-                (got_rows, stud_wlow),
+                (*halves, stud_wlow),
                 scratch=row_acc,
             )
             count, extra = 2 * BLOCK, (totals,)
         (copies,) = on_core(
-            row_kernel,
+            functools.partial(row_kernel, step),
             [shape((n_proto, count, LANES), bf16)],
             (expo, got_cols) + extra,
             scratch=[col_sums] + row_acc,
             pinned=(0,),
         )
         got_rows = exchange(copies, "proto")
+        halves.append(got_rows)
         if step < ITERS - 1:
             (copies,) = on_core(
                 col_kernel,

time: 213 us -> 210 us (0.986)
  blocking collectives: 90.8 us -> 87.8 us
    all_to_all x6, blocking collectives: 90.8 us -> 87.8 us  [exchange(): return lax.all_to_all(copies, axis, 0, 0, tiled=True)]
  transfers between devices with their start and end apart: 16 -> 16, of which waited for: 6 -> 6; matrix products, arithmetic and copies ran while one was open for 6% -> 6% of each run, Pallas kernels for 2% -> 1%
where the time goes in v5:
time: 210 us; the launch traced here: 209 us
  blocking collectives  87.8 us (42%)
  starting transfers between devices  48.9 us (23%)
  waiting for transfers between devices  29.2 us (14%)
  Pallas kernels  20.5 us (10%)
  other arithmetic  12.6 us (6%)
  local copies, waits for them, and re-layouts  5.73 us (3%)
  matrix products  2.91 us (1%)
    all_to_all x6, blocking collectives, exchange(): return lax.all_to_all(copies, axis, 0, 0, tiled=True)  87.8 us
    all_to_all x5, starting transfers between devices, exchange(): return lax.all_to_all(copies, axis, 0, 0, tiled=True)  27.6 us
    all_to_all x5, waiting for transfers between devices, exchange(): return lax.all_to_all(copies, axis, 0, 0, tiled=True)  26.9 us
    pallas_call x12, Pallas kernels, on_core(): pl.pallas_call(kernel, out_shape=tuple(outs), in_specs=[pl.BlockSpec(memo...  20.5 us
    ppermute x3, starting transfers between devices, on_device(): lax.ppermute(part, 'proto', [(i, (i + 4 * hop) % 16) for i in range(16)])  6.27 us
    ppermute x3, starting transfers between devices, on_device(): lax.ppermute(part, 'proto', [(i, i // 4 * 4 + (i + hop) % 4) for i in ran...  6.21 us
    ppermute x1, starting transfers between devices, on_device(): got = lax.ppermute(send, 'dp', [(i, i ^ 2) for i in range(16)])  5.8 us
    convert_element_type x1, other arithmetic, on_device(): teach_wlow = (teacher_prototypes.astype(f32) * teach_norm).astype(bf16)  4.5 us
  transfers between devices with their start and end apart: 16, of which 6 were waited for; matrix products, arithmetic and copies ran while one was open for 6% of the time, Pallas kernels for 1%

profile of v5, /device:TPU:32, one launch (start us, length us, event | category | flops | bytes accessed | tf_op | source)
XLA Modules:
  0.0 208.7 jit_solution(3666681249239830908)
XLA Ops:
  0.6 0.9 copy-done
  1.6 2.0 convolution_convert_fusion
  3.5 8.5 %all-to-all-start = ((bf16[16,48,256]{2,1,0:T(8,128)(2,1)}), bf16[16,48,256]{2,1,0:T(8,128)(2,1)S(1)}, u32[]{:S(2)}, u32[]{:S(2)}) async-start(bf16[16,48,256]{2,1,0:T(8,128)(2,1)} %bitcast), calls=%async_computation | async-start | bytes 786432 | tf_op jit(solution)/shard_map/all_to_all | solution.py:305
  12.0 0.9 copy-done.4
  13.0 0.8 copy-done.6
  13.8 1.1 shard_map.78
  14.9 3.0 %collective-permute-start = (f32[4,48,256]{2,1,0:T(8,128)}, f32[4,48,256]{2,1,0:T(8,128)S(1)}, u32[]{:S(2)}, u32[]{:S(2)}) collective-permute-start(f32[4,48,256]{2,1,0:T(8,128)} %get-tuple-element.39), channel_id=1, source_target_pairs={{0,2},{1,3},{2,0},{3,1},{4,6},{5,7},{6,4},{7,5},{8,10},{9,11},{10,... | collective-permute-start | bytes 589832 | tf_op jit(solution)/shard_map/ppermute | solution.py:354
  18.5 2.7 %collective-permute-start.2 = (f32[4,48,256]{2,1,0:T(8,128)}, f32[4,48,256]{2,1,0:T(8,128)S(1)}, u32[]{:S(2)}, u32[]{:S(2)}) collective-permute-start(f32[4,48,256]{2,1,0:T(8,128)} %get-tuple-element.41), channel_id=1, source_target_pairs={{0,3},{1,0},{2,1},{3,2},{4,7},{5,4},{6,5},{7,6},{8,11},{9,8},{10,9... | collective-permute-start | bytes 589832 | tf_op jit(solution)/shard_map/ppermute | solution.py:354
  21.1 2.0 fusion
  24.3 0.9 shard_map.77.unused_ref
  25.2 5.0 %all-to-all-start.1 = ((bf16[16,48,256]{2,1,0:T(8,128)(2,1)}), bf16[16,48,256]{2,1,0:T(8,128)(2,1)S(1)}, u32[]{:S(2)}, u32[]{:S(2)}) async-start(bf16[16,48,256]{2,1,0:T(8,128)(2,1)} %shard_map.77.unused_ref), calls=%async_computation.1 | async-start | bytes 786432 | tf_op jit(solution)/shard_map/all_to_all | solution.py:305
  30.5 1.9 collective-permute-start.4
  32.4 4.2 %collective-permute-start.3 = (f32[48,256]{1,0:T(8,128)S(1)}, f32[48,256]{1,0:T(8,128)S(1)}, u32[]{:S(2)}, u32[]{:S(2)}) collective-permute-start(f32[48,256]{1,0:T(8,128)S(1)} %get-tuple-element.43), channel_id=1, source_target_pairs={{0,8},{1,9},{2,10},{3,11},{4,12},{5,13},{6,14},{7,15},{8,0},{9,1},... | collective-permute-start | bytes 147464 | tf_op jit(solution)/shard_map/ppermute | solution.py:373
  36.6 4.5 %fusion.1 = (bf16[256,4096]{1,0:T(8,128)(2,1)}, bf16[256,4096]{1,0:T(8,128)(2,1)S(1)}) fusion(bf16[256,4096]{1,0:T(8,128)(2,1)} %param.10, f32[4096]{0:T(1024)S(1)} %add_rsqrt_fusion.1, f32[4096]{0:T(1024)S(1)} %add_rsqrt_fusion, bf16[256,4096]{1,0:T(8,128)(2,1)} %raw_ref.1), kind=kLoop, calls=%fused_computation.5 | loop fusion | flops 6291456 | bytes 8421376 | tf_op jit(solution)/shard_map/convert_element_type | solution.py:362
  41.1 2.3 %collective-permute-done.5 = f32[48,256]{1,0:T(8,128)S(1)} collective-permute-done((f32[48,256]{1,0:T(8,128)S(1)}, f32[48,256]{1,0:T(8,128)S(1)}, u32[]{:S(2)}, u32[]{:S(2)}) %collective-permute-start.5) | collective-permute-done | bytes 49184 | tf_op jit(solution)/shard_map/ppermute | solution.py:373
  43.4 1.2 all-to-all-done.1
  44.6 1.6 copy-done.3
  46.2 1.8 shard_map.80
  48.0 20.3 %all_to_all.55.got_ref = bf16[16,32,128]{2,1,0:T(8,128)(2,1)S(1)} all-to-all(bf16[16,32,128]{2,1,0:T(8,128)(2,1)S(1)} %get-tuple-element.51), channel_id=1, replica_groups=mesh['dp'=16,'proto'=16] {'dp'}, dimensions={0} | all-to-all | bytes 262144 | tf_op jit(solution)/shard_map/all_to_all | solution.py:305
  68.3 1.4 shard_map.81
  69.8 13.7 %all_to_all.56.got_ref.first_ref = bf16[16,64,128]{2,1,0:T(8,128)(2,1)S(1)} all-to-all(bf16[16,64,128]{2,1,0:T(8,128)(2,1)S(1)} %shard_map.81), channel_id=1, replica_groups=mesh['dp'=16,'proto'=16] {'proto'}, dimensions={0} | all-to-all | bytes 524288 | tf_op jit(solution)/shard_map/all_to_all | solution.py:305
  83.4 1.3 shard_map.82
  84.7 14.6 %all_to_all.57.got_ref = bf16[16,32,128]{2,1,0:T(8,128)(2,1)S(1)} all-to-all(bf16[16,32,128]{2,1,0:T(8,128)(2,1)S(1)} %shard_map.82), channel_id=1, replica_groups=mesh['dp'=16,'proto'=16] {'dp'}, dimensions={0} | all-to-all | bytes 262144 | tf_op jit(solution)/shard_map/all_to_all | solution.py:305
  99.4 1.4 shard_map.83
  100.8 13.5 %all_to_all.58.got_ref.second_ref = bf16[16,64,128]{2,1,0:T(8,128)(2,1)S(1)} all-to-all(bf16[16,64,128]{2,1,0:T(8,128)(2,1)S(1)} %shard_map.83), channel_id=1, replica_groups=mesh['dp'=16,'proto'=16] {'proto'}, dimensions={0} | all-to-all | bytes 524288 | tf_op jit(solution)/shard_map/all_to_all | solution.py:305
  114.3 1.3 shard_map.84
  115.6 14.6 %all_to_all.59.got_ref.cols_ref = bf16[16,32,128]{2,1,0:T(8,128)(2,1)S(1)} all-to-all(bf16[16,32,128]{2,1,0:T(8,128)(2,1)S(1)} %shard_map.84), channel_id=1, replica_groups=mesh['dp'=16,'proto'=16] {'dp'}, dimensions={0} | all-to-all | bytes 262144 | tf_op jit(solution)/shard_map/all_to_all | solution.py:305
  130.2 1.9 shard_map.85
  132.2 1.4 shard_map.86
  133.6 11.1 %all_to_all.60.rows_ref = bf16[16,32,128]{2,1,0:T(8,128)(2,1)S(1)} all-to-all(bf16[16,32,128]{2,1,0:T(8,128)(2,1)S(1)} %shard_map.86), channel_id=1, replica_groups=mesh['dp'=16,'proto'=16] {'proto'}, dimensions={0} | all-to-all | bytes 262144 | tf_op jit(solution)/shard_map/all_to_all | solution.py:305
  144.7 6.9 %shard_map.87 = (bf16[16,112,128]{2,1,0:T(8,128)(2,1)}, f32[8,16,4096]{2,1,0:T(8,128)}, bf16[8,16,4096]{2,1,0:T(8,128)(2,1)}) custom-call(s32[1]{0:T(128)} %bitcast.8.core_ref, f32[768,4096]{1,0:T(8,128)S(1)} %get-tuple-element.50.expo_ref, bf16[768,4096]{1,0:T(8,128)(2,1)S(1)} %get-tuple-element.55.stud_ref, ...), custom_call_target="tpu_custom_call" | custom-call | tf_op jit(solution)/shard_map/pallas_call | solution.py:48
  151.8 5.5 %all-to-all-start.8 = ((bf16[16,112,128]{2,1,0:T(8,128)(2,1)}), bf16[16,112,128]{2,1,0:T(8,128)(2,1)S(1)}, u32[]{:S(2)}, u32[]{:S(2)}) async-start(bf16[16,112,128]{2,1,0:T(8,128)(2,1)} %get-tuple-element.60), calls=%async_computation.8 | async-start | bytes 917504 | tf_op jit(solution)/shard_map/all_to_all | solution.py:305
  157.2 3.1 %convert_add_fusion = f32[8,16,4096]{2,1,0:T(8,128)} fusion(f32[8,16,4096]{2,1,0:T(8,128)} %get-tuple-element.61, bf16[8,16,4096]{2,1,0:T(8,128)(2,1)S(1)} %collective-permute-done.6), kind=kLoop, calls=%fused_computation.8 | loop fusion | flops 1048576 | bytes 5242880 | tf_op jit(solution)/shard_map/add | solution.py:459
  160.4 1.4 fusion.6
  161.8 0.8 collective-permute-start.9
  162.6 1.3 collective-permute-start.8
  163.9 0.8 collective-permute-start.7
  164.7 6.8 %all-to-all-done.8.got_ref = bf16[16,112,128]{2,1,0:T(8,128)(2,1)S(1)} async-done(((bf16[16,112,128]{2,1,0:T(8,128)(2,1)}), bf16[16,112,128]{2,1,0:T(8,128)(2,1)S(1)}, u32[]{:S(2)}, u32[]{:S(2)}) %all-to-all-start.8) | async-done | bytes 458784 | tf_op jit(solution)/shard_map/all_to_all | solution.py:305
  171.6 1.0 shard_map.88
  172.5 5.1 %all-to-all-start.9 = ((bf16[16,48,256]{2,1,0:T(8,128)(2,1)}), bf16[16,48,256]{2,1,0:T(8,128)(2,1)S(1)}, u32[]{:S(2)}, u32[]{:S(2)}) async-start(bf16[16,48,256]{2,1,0:T(8,128)(2,1)} %shard_map.88), calls=%async_computation.9 | async-start | bytes 786432 | tf_op jit(solution)/shard_map/all_to_all | solution.py:305
  177.7 1.2 fusion.5
  178.8 10.2 %all-to-all-done.9 = bf16[16,48,256]{2,1,0:T(8,128)(2,1)S(1)} async-done(((bf16[16,48,256]{2,1,0:T(8,128)(2,1)}), bf16[16,48,256]{2,1,0:T(8,128)(2,1)S(1)}, u32[]{:S(2)}, u32[]{:S(2)}) %all-to-all-start.9) | async-done | bytes 393248 | tf_op jit(solution)/shard_map/all_to_all | solution.py:305
  189.1 0.9 convolution_convert_fusion.1
  190.0 3.5 %all-to-all-start.10 = ((bf16[16,16,128]{2,1,0:T(8,128)(2,1)}), bf16[16,16,128]{2,1,0:T(8,128)(2,1)S(1)}, u32[]{:S(2)}, u32[]{:S(2)}) async-start(bf16[16,16,128]{2,1,0:T(8,128)(2,1)} %bitcast.17), calls=%async_computation.10 | async-start | bytes 131072 | tf_op jit(solution)/shard_map/all_to_all | solution.py:305
  193.5 5.8 %collective-permute-start.10 = (bf16[16,4096]{1,0:T(8,128)(2,1)S(1)}, bf16[16,4096]{1,0:T(8,128)(2,1)S(1)}, u32[]{:S(2)}, u32[]{:S(2)}) collective-permute-start(bf16[16,4096]{1,0:T(8,128)(2,1)S(1)} %fusion.9), channel_id=1, source_target_pairs={{0,32},{16,48},{32,0},{48,16},{64,96},{80,112},{96,64},{112,80},{1... | collective-permute-start | bytes 393224 | tf_op jit(solution)/shard_map/ppermute | solution.py:464
  199.3 8.0 %all-to-all-done.10 = bf16[16,16,128]{2,1,0:T(8,128)(2,1)S(1)} async-done(((bf16[16,16,128]{2,1,0:T(8,128)(2,1)}), bf16[16,16,128]{2,1,0:T(8,128)(2,1)S(1)}, u32[]{:S(2)}, u32[]{:S(2)}) %all-to-all-start.10) | async-done | bytes 65568 | tf_op jit(solution)/shard_map/all_to_all | solution.py:305
  207.3 0.6 convert_reduce_fusion
  207.9 0.7 bitcast_add_fusion.1
  (30 shorter events, 2.0 us)
Async XLA Ops:
  0.6 0.9 copy-start
  1.6 21.7 %copy-start.1 = (bf16[256,4096]{1,0:T(8,128)(2,1)S(1)}, bf16[256,4096]{1,0:T(8,128)(2,1)}, u32[]{:S(2)}) copy-start(bf16[256,4096]{1,0:T(8,128)(2,1)} %raw_ref.1) | copy-start | bytes 6291460
  3.5 20.7 %all-to-all-start = ((bf16[16,48,256]{2,1,0:T(8,128)(2,1)}), bf16[16,48,256]{2,1,0:T(8,128)(2,1)S(1)}, u32[]{:S(2)}, u32[]{:S(2)}) async-start(bf16[16,48,256]{2,1,0:T(8,128)(2,1)} %bitcast), calls=%async_computation | async-start | bytes 786432 | tf_op jit(solution)/shard_map/all_to_all | solution.py:305
  12.0 0.9 copy-start.4
  13.0 0.8 copy-start.6
  14.9 15.3 %collective-permute-start = (f32[4,48,256]{2,1,0:T(8,128)}, f32[4,48,256]{2,1,0:T(8,128)S(1)}, u32[]{:S(2)}, u32[]{:S(2)}) collective-permute-start(f32[4,48,256]{2,1,0:T(8,128)} %get-tuple-element.39), channel_id=1, source_target_pairs={{0,2},{1,3},{2,0},{3,1},{4,6},{5,7},{6,4},{7,5},{8,10},{9,11},{10,... | collective-permute-start | bytes 589832 | tf_op jit(solution)/shard_map/ppermute | solution.py:354
  17.9 12.3 %collective-permute-start.1 = (f32[4,48,256]{2,1,0:T(8,128)}, f32[4,48,256]{2,1,0:T(8,128)S(1)}, u32[]{:S(2)}, u32[]{:S(2)}) collective-permute-start(f32[4,48,256]{2,1,0:T(8,128)} %get-tuple-element.40), channel_id=1, source_target_pairs={{0,1},{1,2},{2,3},{3,0},{4,5},{5,6},{6,7},{7,4},{8,9},{9,10},{10,1... | collective-permute-start | bytes 589832 | tf_op jit(solution)/shard_map/ppermute | solution.py:354
  18.5 11.8 %collective-permute-start.2 = (f32[4,48,256]{2,1,0:T(8,128)}, f32[4,48,256]{2,1,0:T(8,128)S(1)}, u32[]{:S(2)}, u32[]{:S(2)}) collective-permute-start(f32[4,48,256]{2,1,0:T(8,128)} %get-tuple-element.41), channel_id=1, source_target_pairs={{0,3},{1,0},{2,1},{3,2},{4,7},{5,4},{6,5},{7,6},{8,11},{9,8},{10,9... | collective-permute-start | bytes 589832 | tf_op jit(solution)/shard_map/ppermute | solution.py:354
  25.2 19.5 %all-to-all-start.1 = ((bf16[16,48,256]{2,1,0:T(8,128)(2,1)}), bf16[16,48,256]{2,1,0:T(8,128)(2,1)S(1)}, u32[]{:S(2)}, u32[]{:S(2)}) async-start(bf16[16,48,256]{2,1,0:T(8,128)(2,1)} %shard_map.77.unused_ref), calls=%async_computation.1 | async-start | bytes 786432 | tf_op jit(solution)/shard_map/all_to_all | solution.py:305
  30.3 13.1 %collective-permute-start.5 = (f32[48,256]{1,0:T(8,128)S(1)}, f32[48,256]{1,0:T(8,128)S(1)}, u32[]{:S(2)}, u32[]{:S(2)}) collective-permute-start(f32[48,256]{1,0:T(8,128)S(1)} %get-tuple-element.45), channel_id=1, source_target_pairs={{0,12},{1,13},{2,14},{3,15},{4,0},{5,1},{6,2},{7,3},{8,4},{9,5},{1... | collective-permute-start | bytes 147464 | tf_op jit(solution)/shard_map/ppermute | solution.py:373
  30.5 12.9 %collective-permute-start.4 = (f32[48,256]{1,0:T(8,128)S(1)}, f32[48,256]{1,0:T(8,128)S(1)}, u32[]{:S(2)}, u32[]{:S(2)}) collective-permute-start(f32[48,256]{1,0:T(8,128)S(1)} %get-tuple-element.44), channel_id=1, source_target_pairs={{0,4},{1,5},{2,6},{3,7},{4,8},{5,9},{6,10},{7,11},{8,12},{9,13},{1... | collective-permute-start | bytes 147464 | tf_op jit(solution)/shard_map/ppermute | solution.py:373
  32.4 11.0 %collective-permute-start.3 = (f32[48,256]{1,0:T(8,128)S(1)}, f32[48,256]{1,0:T(8,128)S(1)}, u32[]{:S(2)}, u32[]{:S(2)}) collective-permute-start(f32[48,256]{1,0:T(8,128)S(1)} %get-tuple-element.43), channel_id=1, source_target_pairs={{0,8},{1,9},{2,10},{3,11},{4,12},{5,13},{6,14},{7,15},{8,0},{9,1},... | collective-permute-start | bytes 147464 | tf_op jit(solution)/shard_map/ppermute | solution.py:373
  44.6 1.6 copy-start.3
  132.2 12.5 %copy-start.2 = (bf16[256,4096]{1,0:T(8,128)(2,1)S(1)}, bf16[256,4096]{1,0:T(8,128)(2,1)}, u32[]{:S(2)}) copy-start(bf16[256,4096]{1,0:T(8,128)(2,1)} %raw_ref.1) | copy-start | bytes 6291460
  151.6 5.7 %collective-permute-start.6 = (bf16[8,16,4096]{2,1,0:T(8,128)(2,1)}, bf16[8,16,4096]{2,1,0:T(8,128)(2,1)S(1)}, u32[]{:S(2)}, u32[]{:S(2)}) collective-permute-start(bf16[8,16,4096]{2,1,0:T(8,128)(2,1)} %get-tuple-element.62), channel_id=1, source_target_pairs={{0,16},{16,0},{32,48},{48,32},{64,80},{80,64},{96,112},{112,96},{1... | collective-permute-start | bytes 3145736 | tf_op jit(solution)/shard_map/ppermute | solution.py:458
  151.8 19.8 %all-to-all-start.8 = ((bf16[16,112,128]{2,1,0:T(8,128)(2,1)}), bf16[16,112,128]{2,1,0:T(8,128)(2,1)S(1)}, u32[]{:S(2)}, u32[]{:S(2)}) async-start(bf16[16,112,128]{2,1,0:T(8,128)(2,1)} %get-tuple-element.60), calls=%async_computation.8 | async-start | bytes 917504 | tf_op jit(solution)/shard_map/all_to_all | solution.py:305
  161.8 27.3 %copy-start.5 = (bf16[768,128]{1,0:T(8,128)(2,1)S(1)}, bf16[768,128]{1,0:T(8,128)(2,1)}, u32[]{:S(2)}) copy-start(bf16[768,128]{1,0:T(8,128)(2,1)} %hidden_ref.1) | copy-start | bytes 589828
  161.8 15.8 %collective-permute-start.9 = (bf16[2,16,4096]{2,1,0:T(8,128)(2,1)S(1)}, bf16[2,16,4096]{2,1,0:T(8,128)(2,1)S(1)}, u32[]{:S(2)}, u32[]{:S(2)}) collective-permute-start(bf16[2,16,4096]{2,1,0:T(8,128)(2,1)S(1)} %get-tuple-element.67), channel_id=1, source_target_pairs={{0,192},{16,208},{32,224},{48,240},{64,0},{80,16},{96,32},{112,48}... | collective-permute-start | bytes 786440 | tf_op jit(solution)/shard_map/ppermute | solution.py:312
  162.6 15.0 %collective-permute-start.8 = (bf16[2,16,4096]{2,1,0:T(8,128)(2,1)S(1)}, bf16[2,16,4096]{2,1,0:T(8,128)(2,1)S(1)}, u32[]{:S(2)}, u32[]{:S(2)}) collective-permute-start(bf16[2,16,4096]{2,1,0:T(8,128)(2,1)S(1)} %get-tuple-element.68), channel_id=1, source_target_pairs={{0,64},{16,80},{32,96},{48,112},{64,128},{80,144},{96,160},{112,17... | collective-permute-start | bytes 786440 | tf_op jit(solution)/shard_map/ppermute | solution.py:312
  163.9 13.7 %collective-permute-start.7 = (bf16[2,16,4096]{2,1,0:T(8,128)(2,1)S(1)}, bf16[2,16,4096]{2,1,0:T(8,128)(2,1)S(1)}, u32[]{:S(2)}, u32[]{:S(2)}) collective-permute-start(bf16[2,16,4096]{2,1,0:T(8,128)(2,1)S(1)} %get-tuple-element.66), channel_id=1, source_target_pairs={{0,128},{16,144},{32,160},{48,176},{64,192},{80,208},{96,224},{112... | collective-permute-start | bytes 786440 | tf_op jit(solution)/shard_map/ppermute | solution.py:312
  172.5 16.5 %all-to-all-start.9 = ((bf16[16,48,256]{2,1,0:T(8,128)(2,1)}), bf16[16,48,256]{2,1,0:T(8,128)(2,1)S(1)}, u32[]{:S(2)}, u32[]{:S(2)}) async-start(bf16[16,48,256]{2,1,0:T(8,128)(2,1)} %shard_map.88), calls=%async_computation.9 | async-start | bytes 786432 | tf_op jit(solution)/shard_map/all_to_all | solution.py:305
  190.0 17.3 %all-to-all-start.10 = ((bf16[16,16,128]{2,1,0:T(8,128)(2,1)}), bf16[16,16,128]{2,1,0:T(8,128)(2,1)S(1)}, u32[]{:S(2)}, u32[]{:S(2)}) async-start(bf16[16,16,128]{2,1,0:T(8,128)(2,1)} %bitcast.17), calls=%async_computation.10 | async-start | bytes 131072 | tf_op jit(solution)/shard_map/all_to_all | solution.py:305
  193.5 14.4 %collective-permute-start.10 = (bf16[16,4096]{1,0:T(8,128)(2,1)S(1)}, bf16[16,4096]{1,0:T(8,128)(2,1)S(1)}, u32[]{:S(2)}, u32[]{:S(2)}) collective-permute-start(bf16[16,4096]{1,0:T(8,128)(2,1)S(1)} %fusion.9), channel_id=1, source_target_pairs={{0,32},{16,48},{32,0},{48,16},{64,96},{80,112},{96,64},{112,80},{1... | collective-permute-start | bytes 393224 | tf_op jit(solution)/shard_map/ppermute | solution.py:464

commit v6 on v5

--- a/solution.py
+++ b/solution.py
@@ -85,6 +85,23 @@
     return lax.broadcasted_iota(jnp.int32, shape, 0) == lax.broadcasted_iota(jnp.int32, shape, 1)
 
 
+def fetch(far_refs, near_refs, sems):
+    copies = [
+        pltpu.make_async_copy(far, near, sems.at[i])
+        for i, (far, near) in enumerate(zip(far_refs, near_refs))
+    ]
+    for copy in copies:
+        copy.start()
+    for copy in copies:
+        copy.wait()
+
+
+def project_kernel(hidden_far, weight_far, out_ref, hidden_ref, weight_ref, sems):
+    fetch((hidden_far, weight_far), (hidden_ref, weight_ref), sems)
+    part = jnp.dot(hidden_ref[...], weight_ref[...], preferred_element_type=jnp.float32)
+    out_ref[...] = part.astype(out_ref.dtype).reshape(out_ref.shape)
+
+
 def share_kernel(got_ref, out_ref):
     unit, unused_scale = unit_rows(jnp.sum(got_ref[...].astype(jnp.float32), axis=0))
     unit = unit.astype(out_ref.dtype)
@@ -92,12 +109,13 @@
         out_ref[p] = unit
 
 
-def parts_kernel(at_ref, hidden_ref, weight_ref, *refs):
-    part_ref = refs[-1]
+def parts_kernel(at_ref, hidden_far, weight_far, *refs):
+    outs, (part_ref, hidden_ref, weight_ref, sems) = refs[:4], refs[4:]
     count, share, width = part_ref.shape
+    fetch((hidden_far, weight_far), (hidden_ref, weight_ref), sems)
     part = jnp.dot(hidden_ref[...], weight_ref[...], preferred_element_type=jnp.float32)
     part_ref[...] = part.reshape(count, share, width)
-    for out_ref, hop in zip(refs[:-1], (0,) + HOPS):
+    for out_ref, hop in zip(outs, (0,) + HOPS):
         for line in range(4):
             out_ref[line] = part_ref[line * 4 + ((at_ref[0] + hop) & 3)]
 
@@ -333,20 +351,32 @@
     def blocks_of(part, count):
         return part.astype(bf16).reshape(count, part.shape[0] // count, part.shape[1])
 
-    teach_part = jnp.dot(teacher_hidden, teacher_bottleneck, preferred_element_type=f32)
-    got = exchange(blocks_of(teach_part, n_proto), "proto")
+    share = rows // n_proto
+    operands = [
+        pltpu.VMEM(teacher_hidden.shape, bf16),
+        pltpu.VMEM(teacher_bottleneck.shape, bf16),
+        pltpu.SemaphoreType.DMA((2,)),
+    ]
+    (blocks,) = on_core(
+        project_kernel,
+        [shape((n_proto, share, width), bf16)],
+        (teacher_hidden, teacher_bottleneck),
+        scratch=operands,
+        far=(0, 1),
+    )
+    got = exchange(blocks, "proto")
 
     me, where = lax.axis_index("proto"), lax.axis_index("dp")
     core, high, y_at = jnp.reshape(where % 2, (1,)), (where // 2) % 2, where // 4
-    share = rows // n_proto
     teach_norm = col_scales(teacher_prototypes)
     stud_norm = col_scales(student_prototypes)
     own, *sends = on_core(
         parts_kernel,
         [shape((4, share, width), f32)] * 4,
         (jnp.reshape(me % 4, (1,)), student_hidden, student_bottleneck),
-        scratch=[pltpu.VMEM((n_proto, share, width), f32)],
+        scratch=[pltpu.VMEM((n_proto, share, width), f32)] + operands,
         smem=(0,),
+        far=(1, 2),
     )
     line = [own]
     for hop, part in zip(HOPS, sends):

time: 210 us -> 209 us (level)
  Pallas kernels: 20.5 us -> 23.5 us
  local copies, waits for them, and re-layouts: 5.73 us -> 3.05 us
    pallas_call x12 -> x13, Pallas kernels: 20.5 us -> 23.5 us  [on_core(): pl.pallas_call(kernel, out_shape=tuple(outs), in_specs=[pl.BlockSpec(memo...]
    unnamed x14 -> x8, local copies, waits for them, and re-layouts: 4.29 us -> 1.61 us
  transfers between devices with their start and end apart: 16 -> 16, of which waited for: 6 -> 6; matrix products, arithmetic and copies ran while one was open for 6% -> 6% of each run, Pallas kernels for 1% -> 2%
where the time goes in v6:
time: 209 us; the launch traced here: 208 us
  blocking collectives  87.8 us (42%)
  starting transfers between devices  49 us (23%)
  waiting for transfers between devices  30 us (14%)
  Pallas kernels  23.5 us (11%)
  other arithmetic  12.6 us (6%)
  local copies, waits for them, and re-layouts  3.05 us (1%)
    all_to_all x6, blocking collectives, exchange(): return lax.all_to_all(copies, axis, 0, 0, tiled=True)  87.8 us
    all_to_all x5, waiting for transfers between devices, exchange(): return lax.all_to_all(copies, axis, 0, 0, tiled=True)  27.7 us
    all_to_all x5, starting transfers between devices, exchange(): return lax.all_to_all(copies, axis, 0, 0, tiled=True)  27.6 us
    pallas_call x13, Pallas kernels, on_core(): pl.pallas_call(kernel, out_shape=tuple(outs), in_specs=[pl.BlockSpec(memo...  23.5 us
    ppermute x3, starting transfers between devices, on_device(): lax.ppermute(part, 'proto', [(i, i // 4 * 4 + (i + hop) % 4) for i in ran...  6.29 us
    ppermute x3, starting transfers between devices, on_device(): lax.ppermute(part, 'proto', [(i, (i + 4 * hop) % 16) for i in range(16)])  6.27 us
    ppermute x1, starting transfers between devices, on_device(): got = lax.ppermute(send, 'dp', [(i, i ^ 2) for i in range(16)])  5.8 us
    convert_element_type x1, other arithmetic, on_device(): teach_wlow = (teacher_prototypes.astype(f32) * teach_norm).astype(bf16)  4.5 us
  transfers between devices with their start and end apart: 16, of which 6 were waited for; matrix products, arithmetic and copies ran while one was open for 6% of the time, Pallas kernels for 2%

profile of v6, /device:TPU:32, one launch (start us, length us, event | category | flops | bytes accessed | tf_op | source)
XLA Modules:
  0.0 207.9 jit_solution(6067660900697044330)
XLA Ops:
  0.6 2.1 %shard_map.77 = bf16[16,48,256]{2,1,0:T(8,128)(2,1)} custom-call(bf16[768,128]{1,0:T(8,128)(2,1)} %hidden_far.2, bf16[128,256]{1,0:T(8,128)(2,1)} %weight_far.2), custom_call_target="tpu_custom_call" | custom-call | tf_op jit(solution)/shard_map/pallas_call | solution.py:48
  2.7 8.5 %all-to-all-start = ((bf16[16,48,256]{2,1,0:T(8,128)(2,1)}), bf16[16,48,256]{2,1,0:T(8,128)(2,1)S(1)}, u32[]{:S(2)}, u32[]{:S(2)}) async-start(bf16[16,48,256]{2,1,0:T(8,128)(2,1)} %shard_map.77), calls=%async_computation | async-start | bytes 786432 | tf_op jit(solution)/shard_map/all_to_all | solution.py:323
  11.2 2.0 shard_map.79
  13.2 3.1 %collective-permute-start = (f32[4,48,256]{2,1,0:T(8,128)}, f32[4,48,256]{2,1,0:T(8,128)S(1)}, u32[]{:S(2)}, u32[]{:S(2)}) collective-permute-start(f32[4,48,256]{2,1,0:T(8,128)} %get-tuple-element.39), channel_id=1, source_target_pairs={{0,2},{1,3},{2,0},{3,1},{4,6},{5,7},{6,4},{7,5},{8,10},{9,11},{10,... | collective-permute-start | bytes 589832 | tf_op jit(solution)/shard_map/ppermute | solution.py:384
  16.3 0.6 collective-permute-start.1
  16.9 2.7 %collective-permute-start.2 = (f32[4,48,256]{2,1,0:T(8,128)S(1)}, f32[4,48,256]{2,1,0:T(8,128)S(1)}, u32[]{:S(2)}, u32[]{:S(2)}) collective-permute-start(f32[4,48,256]{2,1,0:T(8,128)S(1)} %get-tuple-element.41), channel_id=1, source_target_pairs={{0,3},{1,0},{2,1},{3,2},{4,7},{5,4},{6,5},{7,6},{8,11},{9,8},{10,9... | collective-permute-start | bytes 589832 | tf_op jit(solution)/shard_map/ppermute | solution.py:384
  19.5 2.0 fusion
  21.7 0.4 fusion.2
  22.1 1.4 all-to-all-done.got_ref
  23.5 0.9 shard_map.78.unused_ref
  24.4 5.0 %all-to-all-start.1 = ((bf16[16,48,256]{2,1,0:T(8,128)(2,1)}), bf16[16,48,256]{2,1,0:T(8,128)(2,1)S(1)}, u32[]{:S(2)}, u32[]{:S(2)}) async-start(bf16[16,48,256]{2,1,0:T(8,128)(2,1)} %shard_map.78.unused_ref), calls=%async_computation.1 | async-start | bytes 786432 | tf_op jit(solution)/shard_map/all_to_all | solution.py:323
  29.7 1.9 collective-permute-start.4
  31.6 4.2 %collective-permute-start.3 = (f32[48,256]{1,0:T(8,128)S(1)}, f32[48,256]{1,0:T(8,128)S(1)}, u32[]{:S(2)}, u32[]{:S(2)}) collective-permute-start(f32[48,256]{1,0:T(8,128)S(1)} %get-tuple-element.43), channel_id=1, source_target_pairs={{0,8},{1,9},{2,10},{3,11},{4,12},{5,13},{6,14},{7,15},{8,0},{9,1},... | collective-permute-start | bytes 147464 | tf_op jit(solution)/shard_map/ppermute | solution.py:403
  35.8 4.5 %fusion.1 = (bf16[256,4096]{1,0:T(8,128)(2,1)}, bf16[256,4096]{1,0:T(8,128)(2,1)S(1)}) fusion(bf16[256,4096]{1,0:T(8,128)(2,1)} %param.10, f32[4096]{0:T(1024)S(1)} %add_rsqrt_fusion.1, f32[4096]{0:T(1024)S(1)} %add_rsqrt_fusion, bf16[256,4096]{1,0:T(8,128)(2,1)} %raw_ref.1), kind=kLoop, calls=%fused_computation.5 | loop fusion | flops 6291456 | bytes 8421376 | tf_op jit(solution)/shard_map/convert_element_type | solution.py:392
  40.3 2.3 %collective-permute-done.5 = f32[48,256]{1,0:T(8,128)S(1)} collective-permute-done((f32[48,256]{1,0:T(8,128)S(1)}, f32[48,256]{1,0:T(8,128)S(1)}, u32[]{:S(2)}, u32[]{:S(2)}) %collective-permute-start.5) | collective-permute-done | bytes 49184 | tf_op jit(solution)/shard_map/ppermute | solution.py:403
  42.6 1.2 all-to-all-done.1
  43.8 1.6 copy-done.2
  45.4 1.8 shard_map.81
  47.3 20.3 %all_to_all.55.got_ref = bf16[16,32,128]{2,1,0:T(8,128)(2,1)S(1)} all-to-all(bf16[16,32,128]{2,1,0:T(8,128)(2,1)S(1)} %get-tuple-element.51), channel_id=1, replica_groups=mesh['dp'=16,'proto'=16] {'dp'}, dimensions={0} | all-to-all | bytes 262144 | tf_op jit(solution)/shard_map/all_to_all | solution.py:323
  67.5 1.4 shard_map.82
  68.9 13.6 %all_to_all.56.got_ref.first_ref = bf16[16,64,128]{2,1,0:T(8,128)(2,1)S(1)} all-to-all(bf16[16,64,128]{2,1,0:T(8,128)(2,1)S(1)} %shard_map.82), channel_id=1, replica_groups=mesh['dp'=16,'proto'=16] {'proto'}, dimensions={0} | all-to-all | bytes 524288 | tf_op jit(solution)/shard_map/all_to_all | solution.py:323
  82.6 1.3 shard_map.83
  83.9 14.6 %all_to_all.57.got_ref = bf16[16,32,128]{2,1,0:T(8,128)(2,1)S(1)} all-to-all(bf16[16,32,128]{2,1,0:T(8,128)(2,1)S(1)} %shard_map.83), channel_id=1, replica_groups=mesh['dp'=16,'proto'=16] {'dp'}, dimensions={0} | all-to-all | bytes 262144 | tf_op jit(solution)/shard_map/all_to_all | solution.py:323
  98.5 1.4 shard_map.84
  100.0 13.5 %all_to_all.58.got_ref.second_ref = bf16[16,64,128]{2,1,0:T(8,128)(2,1)S(1)} all-to-all(bf16[16,64,128]{2,1,0:T(8,128)(2,1)S(1)} %shard_map.84), channel_id=1, replica_groups=mesh['dp'=16,'proto'=16] {'proto'}, dimensions={0} | all-to-all | bytes 524288 | tf_op jit(solution)/shard_map/all_to_all | solution.py:323
  113.5 1.3 shard_map.85
  114.8 14.6 %all_to_all.59.got_ref.cols_ref = bf16[16,32,128]{2,1,0:T(8,128)(2,1)S(1)} all-to-all(bf16[16,32,128]{2,1,0:T(8,128)(2,1)S(1)} %shard_map.85), channel_id=1, replica_groups=mesh['dp'=16,'proto'=16] {'dp'}, dimensions={0} | all-to-all | bytes 262144 | tf_op jit(solution)/shard_map/all_to_all | solution.py:323
  129.4 1.9 shard_map.86
  131.4 1.4 shard_map.87
  132.7 11.1 %all_to_all.60.rows_ref = bf16[16,32,128]{2,1,0:T(8,128)(2,1)S(1)} all-to-all(bf16[16,32,128]{2,1,0:T(8,128)(2,1)S(1)} %shard_map.87), channel_id=1, replica_groups=mesh['dp'=16,'proto'=16] {'proto'}, dimensions={0} | all-to-all | bytes 262144 | tf_op jit(solution)/shard_map/all_to_all | solution.py:323
  143.8 6.9 %shard_map.88 = (bf16[16,112,128]{2,1,0:T(8,128)(2,1)}, f32[8,16,4096]{2,1,0:T(8,128)}, bf16[8,16,4096]{2,1,0:T(8,128)(2,1)}) custom-call(s32[1]{0:T(128)} %bitcast.7.core_ref, f32[768,4096]{1,0:T(8,128)S(1)} %get-tuple-element.50.expo_ref, bf16[768,4096]{1,0:T(8,128)(2,1)S(1)} %get-tuple-element.55.stud_ref, ...), custom_call_target="tpu_custom_call" | custom-call | tf_op jit(solution)/shard_map/pallas_call | solution.py:48
  151.0 5.5 %all-to-all-start.8 = ((bf16[16,112,128]{2,1,0:T(8,128)(2,1)}), bf16[16,112,128]{2,1,0:T(8,128)(2,1)S(1)}, u32[]{:S(2)}, u32[]{:S(2)}) async-start(bf16[16,112,128]{2,1,0:T(8,128)(2,1)} %get-tuple-element.60), calls=%async_computation.8 | async-start | bytes 917504 | tf_op jit(solution)/shard_map/all_to_all | solution.py:323
  156.4 3.1 %convert_add_fusion = f32[8,16,4096]{2,1,0:T(8,128)} fusion(f32[8,16,4096]{2,1,0:T(8,128)} %get-tuple-element.61, bf16[8,16,4096]{2,1,0:T(8,128)(2,1)S(1)} %collective-permute-done.6), kind=kLoop, calls=%fused_computation.8 | loop fusion | flops 1048576 | bytes 5242880 | tf_op jit(solution)/shard_map/add | solution.py:489
  159.6 1.4 fusion.6
  161.0 0.8 collective-permute-start.9
  161.8 1.3 collective-permute-start.8
  163.1 0.8 collective-permute-start.7
  164.0 6.8 %all-to-all-done.8.got_ref = bf16[16,112,128]{2,1,0:T(8,128)(2,1)S(1)} async-done(((bf16[16,112,128]{2,1,0:T(8,128)(2,1)}), bf16[16,112,128]{2,1,0:T(8,128)(2,1)S(1)}, u32[]{:S(2)}, u32[]{:S(2)}) %all-to-all-start.8) | async-done | bytes 458784 | tf_op jit(solution)/shard_map/all_to_all | solution.py:323
  170.8 1.0 shard_map.89
  171.7 5.1 %all-to-all-start.9 = ((bf16[16,48,256]{2,1,0:T(8,128)(2,1)}), bf16[16,48,256]{2,1,0:T(8,128)(2,1)S(1)}, u32[]{:S(2)}, u32[]{:S(2)}) async-start(bf16[16,48,256]{2,1,0:T(8,128)(2,1)} %shard_map.89), calls=%async_computation.9 | async-start | bytes 786432 | tf_op jit(solution)/shard_map/all_to_all | solution.py:323
  176.9 1.2 fusion.5
  178.0 10.2 %all-to-all-done.9 = bf16[16,48,256]{2,1,0:T(8,128)(2,1)S(1)} async-done(((bf16[16,48,256]{2,1,0:T(8,128)(2,1)}), bf16[16,48,256]{2,1,0:T(8,128)(2,1)S(1)}, u32[]{:S(2)}, u32[]{:S(2)}) %all-to-all-start.9) | async-done | bytes 393248 | tf_op jit(solution)/shard_map/all_to_all | solution.py:323
  188.3 0.9 convolution_convert_fusion
  189.2 3.5 %all-to-all-start.10 = ((bf16[16,16,128]{2,1,0:T(8,128)(2,1)}), bf16[16,16,128]{2,1,0:T(8,128)(2,1)S(1)}, u32[]{:S(2)}, u32[]{:S(2)}) async-start(bf16[16,16,128]{2,1,0:T(8,128)(2,1)} %bitcast.16), calls=%async_computation.10 | async-start | bytes 131072 | tf_op jit(solution)/shard_map/all_to_all | solution.py:323
  192.7 5.8 %collective-permute-start.10 = (bf16[16,4096]{1,0:T(8,128)(2,1)S(1)}, bf16[16,4096]{1,0:T(8,128)(2,1)S(1)}, u32[]{:S(2)}, u32[]{:S(2)}) collective-permute-start(bf16[16,4096]{1,0:T(8,128)(2,1)S(1)} %fusion.9), channel_id=1, source_target_pairs={{0,32},{16,48},{32,0},{48,16},{64,96},{80,112},{96,64},{112,80},{1... | collective-permute-start | bytes 393224 | tf_op jit(solution)/shard_map/ppermute | solution.py:494
  198.5 8.0 %all-to-all-done.10 = bf16[16,16,128]{2,1,0:T(8,128)(2,1)S(1)} async-done(((bf16[16,16,128]{2,1,0:T(8,128)(2,1)}), bf16[16,16,128]{2,1,0:T(8,128)(2,1)S(1)}, u32[]{:S(2)}, u32[]{:S(2)}) %all-to-all-start.10) | async-done | bytes 65568 | tf_op jit(solution)/shard_map/all_to_all | solution.py:323
  206.5 0.6 convert_reduce_fusion
  207.1 0.7 bitcast_add_fusion.1
  (24 shorter events, 0.4 us)
Async XLA Ops:
  0.6 21.0 %copy-start = (bf16[256,4096]{1,0:T(8,128)(2,1)S(1)}, bf16[256,4096]{1,0:T(8,128)(2,1)}, u32[]{:S(2)}) copy-start(bf16[256,4096]{1,0:T(8,128)(2,1)} %raw_ref.1) | copy-start | bytes 6291460
  2.7 20.8 %all-to-all-start = ((bf16[16,48,256]{2,1,0:T(8,128)(2,1)}), bf16[16,48,256]{2,1,0:T(8,128)(2,1)S(1)}, u32[]{:S(2)}, u32[]{:S(2)}) async-start(bf16[16,48,256]{2,1,0:T(8,128)(2,1)} %shard_map.77), calls=%async_computation | async-start | bytes 786432 | tf_op jit(solution)/shard_map/all_to_all | solution.py:323
  13.2 16.2 %collective-permute-start = (f32[4,48,256]{2,1,0:T(8,128)}, f32[4,48,256]{2,1,0:T(8,128)S(1)}, u32[]{:S(2)}, u32[]{:S(2)}) collective-permute-start(f32[4,48,256]{2,1,0:T(8,128)} %get-tuple-element.39), channel_id=1, source_target_pairs={{0,2},{1,3},{2,0},{3,1},{4,6},{5,7},{6,4},{7,5},{8,10},{9,11},{10,... | collective-permute-start | bytes 589832 | tf_op jit(solution)/shard_map/ppermute | solution.py:384
  16.3 13.1 %collective-permute-start.1 = (f32[4,48,256]{2,1,0:T(8,128)}, f32[4,48,256]{2,1,0:T(8,128)S(1)}, u32[]{:S(2)}, u32[]{:S(2)}) collective-permute-start(f32[4,48,256]{2,1,0:T(8,128)} %get-tuple-element.40), channel_id=1, source_target_pairs={{0,1},{1,2},{2,3},{3,0},{4,5},{5,6},{6,7},{7,4},{8,9},{9,10},{10,1... | collective-permute-start | bytes 589832 | tf_op jit(solution)/shard_map/ppermute | solution.py:384
  16.9 12.6 %collective-permute-start.2 = (f32[4,48,256]{2,1,0:T(8,128)S(1)}, f32[4,48,256]{2,1,0:T(8,128)S(1)}, u32[]{:S(2)}, u32[]{:S(2)}) collective-permute-start(f32[4,48,256]{2,1,0:T(8,128)S(1)} %get-tuple-element.41), channel_id=1, source_target_pairs={{0,3},{1,0},{2,1},{3,2},{4,7},{5,4},{6,5},{7,6},{8,11},{9,8},{10,9... | collective-permute-start | bytes 589832 | tf_op jit(solution)/shard_map/ppermute | solution.py:384
  24.4 19.5 %all-to-all-start.1 = ((bf16[16,48,256]{2,1,0:T(8,128)(2,1)}), bf16[16,48,256]{2,1,0:T(8,128)(2,1)S(1)}, u32[]{:S(2)}, u32[]{:S(2)}) async-start(bf16[16,48,256]{2,1,0:T(8,128)(2,1)} %shard_map.78.unused_ref), calls=%async_computation.1 | async-start | bytes 786432 | tf_op jit(solution)/shard_map/all_to_all | solution.py:323
  29.5 13.1 %collective-permute-start.5 = (f32[48,256]{1,0:T(8,128)S(1)}, f32[48,256]{1,0:T(8,128)S(1)}, u32[]{:S(2)}, u32[]{:S(2)}) collective-permute-start(f32[48,256]{1,0:T(8,128)S(1)} %get-tuple-element.45), channel_id=1, source_target_pairs={{0,12},{1,13},{2,14},{3,15},{4,0},{5,1},{6,2},{7,3},{8,4},{9,5},{1... | collective-permute-start | bytes 147464 | tf_op jit(solution)/shard_map/ppermute | solution.py:403
  29.7 12.9 %collective-permute-start.4 = (f32[48,256]{1,0:T(8,128)S(1)}, f32[48,256]{1,0:T(8,128)S(1)}, u32[]{:S(2)}, u32[]{:S(2)}) collective-permute-start(f32[48,256]{1,0:T(8,128)S(1)} %get-tuple-element.44), channel_id=1, source_target_pairs={{0,4},{1,5},{2,6},{3,7},{4,8},{5,9},{6,10},{7,11},{8,12},{9,13},{1... | collective-permute-start | bytes 147464 | tf_op jit(solution)/shard_map/ppermute | solution.py:403
  31.6 11.0 %collective-permute-start.3 = (f32[48,256]{1,0:T(8,128)S(1)}, f32[48,256]{1,0:T(8,128)S(1)}, u32[]{:S(2)}, u32[]{:S(2)}) collective-permute-start(f32[48,256]{1,0:T(8,128)S(1)} %get-tuple-element.43), channel_id=1, source_target_pairs={{0,8},{1,9},{2,10},{3,11},{4,12},{5,13},{6,14},{7,15},{8,0},{9,1},... | collective-permute-start | bytes 147464 | tf_op jit(solution)/shard_map/ppermute | solution.py:403
  43.8 1.6 copy-start.2
  131.4 12.5 %copy-start.1 = (bf16[256,4096]{1,0:T(8,128)(2,1)S(1)}, bf16[256,4096]{1,0:T(8,128)(2,1)}, u32[]{:S(2)}) copy-start(bf16[256,4096]{1,0:T(8,128)(2,1)} %raw_ref.1) | copy-start | bytes 6291460
  150.8 5.7 %collective-permute-start.6 = (bf16[8,16,4096]{2,1,0:T(8,128)(2,1)}, bf16[8,16,4096]{2,1,0:T(8,128)(2,1)S(1)}, u32[]{:S(2)}, u32[]{:S(2)}) collective-permute-start(bf16[8,16,4096]{2,1,0:T(8,128)(2,1)} %get-tuple-element.62), channel_id=1, source_target_pairs={{0,16},{16,0},{32,48},{48,32},{64,80},{80,64},{96,112},{112,96},{1... | collective-permute-start | bytes 3145736 | tf_op jit(solution)/shard_map/ppermute | solution.py:488
  151.0 19.8 %all-to-all-start.8 = ((bf16[16,112,128]{2,1,0:T(8,128)(2,1)}), bf16[16,112,128]{2,1,0:T(8,128)(2,1)S(1)}, u32[]{:S(2)}, u32[]{:S(2)}) async-start(bf16[16,112,128]{2,1,0:T(8,128)(2,1)} %get-tuple-element.60), calls=%async_computation.8 | async-start | bytes 917504 | tf_op jit(solution)/shard_map/all_to_all | solution.py:323
  161.0 27.3 %copy-start.3 = (bf16[768,128]{1,0:T(8,128)(2,1)S(1)}, bf16[768,128]{1,0:T(8,128)(2,1)}, u32[]{:S(2)}) copy-start(bf16[768,128]{1,0:T(8,128)(2,1)} %hidden_far.3) | copy-start | bytes 589828
  161.0 15.8 %collective-permute-start.9 = (bf16[2,16,4096]{2,1,0:T(8,128)(2,1)S(1)}, bf16[2,16,4096]{2,1,0:T(8,128)(2,1)S(1)}, u32[]{:S(2)}, u32[]{:S(2)}) collective-permute-start(bf16[2,16,4096]{2,1,0:T(8,128)(2,1)S(1)} %get-tuple-element.67), channel_id=1, source_target_pairs={{0,192},{16,208},{32,224},{48,240},{64,0},{80,16},{96,32},{112,48}... | collective-permute-start | bytes 786440 | tf_op jit(solution)/shard_map/ppermute | solution.py:330
  161.8 15.0 %collective-permute-start.8 = (bf16[2,16,4096]{2,1,0:T(8,128)(2,1)S(1)}, bf16[2,16,4096]{2,1,0:T(8,128)(2,1)S(1)}, u32[]{:S(2)}, u32[]{:S(2)}) collective-permute-start(bf16[2,16,4096]{2,1,0:T(8,128)(2,1)S(1)} %get-tuple-element.68), channel_id=1, source_target_pairs={{0,64},{16,80},{32,96},{48,112},{64,128},{80,144},{96,160},{112,17... | collective-permute-start | bytes 786440 | tf_op jit(solution)/shard_map/ppermute | solution.py:330
  163.1 13.7 %collective-permute-start.7 = (bf16[2,16,4096]{2,1,0:T(8,128)(2,1)S(1)}, bf16[2,16,4096]{2,1,0:T(8,128)(2,1)S(1)}, u32[]{:S(2)}, u32[]{:S(2)}) collective-permute-start(bf16[2,16,4096]{2,1,0:T(8,128)(2,1)S(1)} %get-tuple-element.66), channel_id=1, source_target_pairs={{0,128},{16,144},{32,160},{48,176},{64,192},{80,208},{96,224},{112... | collective-permute-start | bytes 786440 | tf_op jit(solution)/shard_map/ppermute | solution.py:330
  171.7 16.5 %all-to-all-start.9 = ((bf16[16,48,256]{2,1,0:T(8,128)(2,1)}), bf16[16,48,256]{2,1,0:T(8,128)(2,1)S(1)}, u32[]{:S(2)}, u32[]{:S(2)}) async-start(bf16[16,48,256]{2,1,0:T(8,128)(2,1)} %shard_map.89), calls=%async_computation.9 | async-start | bytes 786432 | tf_op jit(solution)/shard_map/all_to_all | solution.py:323
  189.2 17.3 %all-to-all-start.10 = ((bf16[16,16,128]{2,1,0:T(8,128)(2,1)}), bf16[16,16,128]{2,1,0:T(8,128)(2,1)S(1)}, u32[]{:S(2)}, u32[]{:S(2)}) async-start(bf16[16,16,128]{2,1,0:T(8,128)(2,1)} %bitcast.16), calls=%async_computation.10 | async-start | bytes 131072 | tf_op jit(solution)/shard_map/all_to_all | solution.py:323
  192.7 14.4 %collective-permute-start.10 = (bf16[16,4096]{1,0:T(8,128)(2,1)S(1)}, bf16[16,4096]{1,0:T(8,128)(2,1)S(1)}, u32[]{:S(2)}, u32[]{:S(2)}) collective-permute-start(bf16[16,4096]{1,0:T(8,128)(2,1)S(1)} %fusion.9), channel_id=1, source_target_pairs={{0,32},{16,48},{32,0},{48,16},{64,96},{80,112},{96,64},{112,80},{1... | collective-permute-start | bytes 393224 | tf_op jit(solution)/shard_map/ppermute | solution.py:494

commit v7 on v6

--- a/solution.py
+++ b/solution.py
@@ -282,7 +282,7 @@
         if k >= 2:
             for copy in stores[k - 2]:
                 copy.wait()
-        keep_ref[slot] = jnp.where(core == 0, part[:, 0], part[:, 1])
+        keep_ref[slot] = jnp.where(core == 0, part[:, 0], part[:, 1]).astype(jnp.bfloat16)
         send_ref[slot] = jnp.where(core == 0, part[:, 1], part[:, 0]).astype(jnp.bfloat16)
         stores.append(
             (
@@ -460,7 +460,7 @@
         grad_kernel,
         [
             pltpu.HBM((n_proto, 2 * share + BLOCK, LANES), bf16),
-            pltpu.HBM((8, 16, columns), f32),
+            pltpu.HBM((8, 16, columns), bf16),
             pltpu.HBM((8, 16, columns), bf16),
         ],
         (
@@ -469,7 +469,7 @@
         ),
         scratch=[
             pltpu.VMEM((n_proto, 2 * share + BLOCK, LANES), bf16),
-            pltpu.VMEM((2, 8, 16, GRAD_WIDE), f32),
+            pltpu.VMEM((2, 8, 16, GRAD_WIDE), bf16),
             pltpu.VMEM((2, 8, 16, GRAD_WIDE), bf16),
             pltpu.SemaphoreType.DMA((3, 2)),
             pltpu.VMEM((rows, LANES), f32),
@@ -486,7 +486,7 @@
     (copies,) = on_core(proj_kernel, [shape((n_proto, share, width), bf16)], (got, stud_share))
     proj_grad = exchange(copies, "proto").reshape(rows, width)
     got = lax.ppermute(send, "dp", [(i, i ^ 1) for i in range(16)])
-    pair = (keep + got.astype(f32)).reshape(4, 2, 16, columns)
+    pair = (keep.astype(f32) + got.astype(f32)).reshape(4, 2, 16, columns)
     quarter = spread_sum(pair, "dp", 0, y_at, lambda i, hop: (i + 4 * hop) % 16, bf16)
     proj_grad, quarter = lax.optimization_barrier((proj_grad, quarter))
     keep = jnp.where(high == 0, quarter[0], quarter[1])

time: 209 us -> 209 us (level)
  no operation moved by 1% of the time
where the time goes in v7:
time: 209 us; the launch traced here: 208 us
  blocking collectives  87.8 us (42%)
  starting transfers between devices  49 us (23%)
  waiting for transfers between devices  30.3 us (14%)
  Pallas kernels  23.4 us (11%)
  other arithmetic  12.3 us (6%)
  local copies, waits for them, and re-layouts  3.05 us (1%)
    all_to_all x6, blocking collectives, exchange(): return lax.all_to_all(copies, axis, 0, 0, tiled=True)  87.8 us
    all_to_all x5, waiting for transfers between devices, exchange(): return lax.all_to_all(copies, axis, 0, 0, tiled=True)  28 us
    all_to_all x5, starting transfers between devices, exchange(): return lax.all_to_all(copies, axis, 0, 0, tiled=True)  27.6 us
    pallas_call x13, Pallas kernels, on_core(): pl.pallas_call(kernel, out_shape=tuple(outs), in_specs=[pl.BlockSpec(memo...  23.4 us
    ppermute x3, starting transfers between devices, on_device(): lax.ppermute(part, 'proto', [(i, i // 4 * 4 + (i + hop) % 4) for i in ran...  6.29 us
    ppermute x3, starting transfers between devices, on_device(): lax.ppermute(part, 'proto', [(i, (i + 4 * hop) % 16) for i in range(16)])  6.27 us
    ppermute x1, starting transfers between devices, on_device(): got = lax.ppermute(send, 'dp', [(i, i ^ 2) for i in range(16)])  5.8 us
    convert_element_type x1, other arithmetic, on_device(): teach_wlow = (teacher_prototypes.astype(f32) * teach_norm).astype(bf16)  4.5 us
  transfers between devices with their start and end apart: 16, of which 6 were waited for; matrix products, arithmetic and copies ran while one was open for 6% of the time, Pallas kernels for 2%

profile of v7, /device:TPU:32, one launch (start us, length us, event | category | flops | bytes accessed | tf_op | source)
XLA Modules:
  0.0 207.7 jit_solution(892389799881107752)
XLA Ops:
  0.6 2.1 %shard_map.77 = bf16[16,48,256]{2,1,0:T(8,128)(2,1)} custom-call(bf16[768,128]{1,0:T(8,128)(2,1)} %hidden_far.2, bf16[128,256]{1,0:T(8,128)(2,1)} %weight_far.2), custom_call_target="tpu_custom_call" | custom-call | tf_op jit(solution)/shard_map/pallas_call | solution.py:48
  2.7 8.5 %all-to-all-start = ((bf16[16,48,256]{2,1,0:T(8,128)(2,1)}), bf16[16,48,256]{2,1,0:T(8,128)(2,1)S(1)}, u32[]{:S(2)}, u32[]{:S(2)}) async-start(bf16[16,48,256]{2,1,0:T(8,128)(2,1)} %shard_map.77), calls=%async_computation | async-start | bytes 786432 | tf_op jit(solution)/shard_map/all_to_all | solution.py:323
  11.2 2.0 shard_map.79
  13.2 3.1 %collective-permute-start = (f32[4,48,256]{2,1,0:T(8,128)}, f32[4,48,256]{2,1,0:T(8,128)S(1)}, u32[]{:S(2)}, u32[]{:S(2)}) collective-permute-start(f32[4,48,256]{2,1,0:T(8,128)} %get-tuple-element.39), channel_id=1, source_target_pairs={{0,2},{1,3},{2,0},{3,1},{4,6},{5,7},{6,4},{7,5},{8,10},{9,11},{10,... | collective-permute-start | bytes 589832 | tf_op jit(solution)/shard_map/ppermute | solution.py:384
  16.3 0.6 collective-permute-start.1
  16.9 2.7 %collective-permute-start.2 = (f32[4,48,256]{2,1,0:T(8,128)S(1)}, f32[4,48,256]{2,1,0:T(8,128)S(1)}, u32[]{:S(2)}, u32[]{:S(2)}) collective-permute-start(f32[4,48,256]{2,1,0:T(8,128)S(1)} %get-tuple-element.41), channel_id=1, source_target_pairs={{0,3},{1,0},{2,1},{3,2},{4,7},{5,4},{6,5},{7,6},{8,11},{9,8},{10,9... | collective-permute-start | bytes 589832 | tf_op jit(solution)/shard_map/ppermute | solution.py:384
  19.5 2.0 fusion
  21.7 0.4 fusion.2
  22.1 1.4 all-to-all-done.got_ref
  23.5 0.9 shard_map.78.unused_ref
  24.4 5.0 %all-to-all-start.1 = ((bf16[16,48,256]{2,1,0:T(8,128)(2,1)}), bf16[16,48,256]{2,1,0:T(8,128)(2,1)S(1)}, u32[]{:S(2)}, u32[]{:S(2)}) async-start(bf16[16,48,256]{2,1,0:T(8,128)(2,1)} %shard_map.78.unused_ref), calls=%async_computation.1 | async-start | bytes 786432 | tf_op jit(solution)/shard_map/all_to_all | solution.py:323
  29.7 1.9 collective-permute-start.4
  31.6 4.2 %collective-permute-start.3 = (f32[48,256]{1,0:T(8,128)S(1)}, f32[48,256]{1,0:T(8,128)S(1)}, u32[]{:S(2)}, u32[]{:S(2)}) collective-permute-start(f32[48,256]{1,0:T(8,128)S(1)} %get-tuple-element.43), channel_id=1, source_target_pairs={{0,8},{1,9},{2,10},{3,11},{4,12},{5,13},{6,14},{7,15},{8,0},{9,1},... | collective-permute-start | bytes 147464 | tf_op jit(solution)/shard_map/ppermute | solution.py:403
  35.8 4.5 %fusion.1 = (bf16[256,4096]{1,0:T(8,128)(2,1)}, bf16[256,4096]{1,0:T(8,128)(2,1)S(1)}) fusion(bf16[256,4096]{1,0:T(8,128)(2,1)} %param.10, f32[4096]{0:T(1024)S(1)} %add_rsqrt_fusion.1, f32[4096]{0:T(1024)S(1)} %add_rsqrt_fusion, bf16[256,4096]{1,0:T(8,128)(2,1)} %raw_ref.1), kind=kLoop, calls=%fused_computation.5 | loop fusion | flops 6291456 | bytes 8421376 | tf_op jit(solution)/shard_map/convert_element_type | solution.py:392
  40.3 2.3 %collective-permute-done.5 = f32[48,256]{1,0:T(8,128)S(1)} collective-permute-done((f32[48,256]{1,0:T(8,128)S(1)}, f32[48,256]{1,0:T(8,128)S(1)}, u32[]{:S(2)}, u32[]{:S(2)}) %collective-permute-start.5) | collective-permute-done | bytes 49184 | tf_op jit(solution)/shard_map/ppermute | solution.py:403
  42.6 1.2 all-to-all-done.1
  43.8 1.6 copy-done.2
  45.4 1.8 shard_map.81
  47.3 20.3 %all_to_all.55.got_ref = bf16[16,32,128]{2,1,0:T(8,128)(2,1)S(1)} all-to-all(bf16[16,32,128]{2,1,0:T(8,128)(2,1)S(1)} %get-tuple-element.51), channel_id=1, replica_groups=mesh['dp'=16,'proto'=16] {'dp'}, dimensions={0} | all-to-all | bytes 262144 | tf_op jit(solution)/shard_map/all_to_all | solution.py:323
  67.5 1.4 shard_map.82
  68.9 13.6 %all_to_all.56.got_ref.first_ref = bf16[16,64,128]{2,1,0:T(8,128)(2,1)S(1)} all-to-all(bf16[16,64,128]{2,1,0:T(8,128)(2,1)S(1)} %shard_map.82), channel_id=1, replica_groups=mesh['dp'=16,'proto'=16] {'proto'}, dimensions={0} | all-to-all | bytes 524288 | tf_op jit(solution)/shard_map/all_to_all | solution.py:323
  82.6 1.3 shard_map.83
  83.9 14.6 %all_to_all.57.got_ref = bf16[16,32,128]{2,1,0:T(8,128)(2,1)S(1)} all-to-all(bf16[16,32,128]{2,1,0:T(8,128)(2,1)S(1)} %shard_map.83), channel_id=1, replica_groups=mesh['dp'=16,'proto'=16] {'dp'}, dimensions={0} | all-to-all | bytes 262144 | tf_op jit(solution)/shard_map/all_to_all | solution.py:323
  98.5 1.4 shard_map.84
  100.0 13.5 %all_to_all.58.got_ref.second_ref = bf16[16,64,128]{2,1,0:T(8,128)(2,1)S(1)} all-to-all(bf16[16,64,128]{2,1,0:T(8,128)(2,1)S(1)} %shard_map.84), channel_id=1, replica_groups=mesh['dp'=16,'proto'=16] {'proto'}, dimensions={0} | all-to-all | bytes 524288 | tf_op jit(solution)/shard_map/all_to_all | solution.py:323
  113.5 1.3 shard_map.85
  114.8 14.6 %all_to_all.59.got_ref.cols_ref = bf16[16,32,128]{2,1,0:T(8,128)(2,1)S(1)} all-to-all(bf16[16,32,128]{2,1,0:T(8,128)(2,1)S(1)} %shard_map.85), channel_id=1, replica_groups=mesh['dp'=16,'proto'=16] {'dp'}, dimensions={0} | all-to-all | bytes 262144 | tf_op jit(solution)/shard_map/all_to_all | solution.py:323
  129.4 1.9 shard_map.86
  131.4 1.4 shard_map.87
  132.7 11.1 %all_to_all.60.rows_ref = bf16[16,32,128]{2,1,0:T(8,128)(2,1)S(1)} all-to-all(bf16[16,32,128]{2,1,0:T(8,128)(2,1)S(1)} %shard_map.87), channel_id=1, replica_groups=mesh['dp'=16,'proto'=16] {'proto'}, dimensions={0} | all-to-all | bytes 262144 | tf_op jit(solution)/shard_map/all_to_all | solution.py:323
  143.8 6.8 %shard_map.88 = (bf16[16,112,128]{2,1,0:T(8,128)(2,1)}, bf16[8,16,4096]{2,1,0:T(8,128)(2,1)}, bf16[8,16,4096]{2,1,0:T(8,128)(2,1)}) custom-call(s32[1]{0:T(128)} %bitcast.7.core_ref, f32[768,4096]{1,0:T(8,128)S(1)} %get-tuple-element.50.expo_ref, bf16[768,4096]{1,0:T(8,128)(2,1)S(1)} %get-tuple-element.55.stud_ref, ...), custom_call_target="tpu_custom_call" | custom-call | tf_op jit(solution)/shard_map/pallas_call | solution.py:48
  150.8 5.5 %all-to-all-start.8 = ((bf16[16,112,128]{2,1,0:T(8,128)(2,1)}), bf16[16,112,128]{2,1,0:T(8,128)(2,1)S(1)}, u32[]{:S(2)}, u32[]{:S(2)}) async-start(bf16[16,112,128]{2,1,0:T(8,128)(2,1)} %get-tuple-element.60), calls=%async_computation.8 | async-start | bytes 917504 | tf_op jit(solution)/shard_map/all_to_all | solution.py:323
  156.3 2.8 %convert_add_fusion = f32[8,16,4096]{2,1,0:T(8,128)} fusion(bf16[8,16,4096]{2,1,0:T(8,128)(2,1)S(1)} %collective-permute-done.6, bf16[8,16,4096]{2,1,0:T(8,128)(2,1)} %get-tuple-element.61), kind=kLoop, calls=%fused_computation.8 | loop fusion | flops 1572864 | bytes 4194304 | tf_op jit(solution)/shard_map/add | solution.py:489
  159.1 1.4 fusion.6
  160.6 0.8 collective-permute-start.9
  161.4 1.3 collective-permute-start.8
  162.7 0.8 collective-permute-start.7
  163.5 7.2 %all-to-all-done.8.got_ref = bf16[16,112,128]{2,1,0:T(8,128)(2,1)S(1)} async-done(((bf16[16,112,128]{2,1,0:T(8,128)(2,1)}), bf16[16,112,128]{2,1,0:T(8,128)(2,1)S(1)}, u32[]{:S(2)}, u32[]{:S(2)}) %all-to-all-start.8) | async-done | bytes 458784 | tf_op jit(solution)/shard_map/all_to_all | solution.py:323
  170.7 0.9 shard_map.89
  171.6 5.1 %all-to-all-start.9 = ((bf16[16,48,256]{2,1,0:T(8,128)(2,1)}), bf16[16,48,256]{2,1,0:T(8,128)(2,1)S(1)}, u32[]{:S(2)}, u32[]{:S(2)}) async-start(bf16[16,48,256]{2,1,0:T(8,128)(2,1)} %shard_map.89), calls=%async_computation.9 | async-start | bytes 786432 | tf_op jit(solution)/shard_map/all_to_all | solution.py:323
  176.7 1.2 fusion.5
  177.9 10.2 %all-to-all-done.9 = bf16[16,48,256]{2,1,0:T(8,128)(2,1)S(1)} async-done(((bf16[16,48,256]{2,1,0:T(8,128)(2,1)}), bf16[16,48,256]{2,1,0:T(8,128)(2,1)S(1)}, u32[]{:S(2)}, u32[]{:S(2)}) %all-to-all-start.9) | async-done | bytes 393248 | tf_op jit(solution)/shard_map/all_to_all | solution.py:323
  188.1 0.9 convolution_convert_fusion
  189.1 3.5 %all-to-all-start.10 = ((bf16[16,16,128]{2,1,0:T(8,128)(2,1)}), bf16[16,16,128]{2,1,0:T(8,128)(2,1)S(1)}, u32[]{:S(2)}, u32[]{:S(2)}) async-start(bf16[16,16,128]{2,1,0:T(8,128)(2,1)} %bitcast.16), calls=%async_computation.10 | async-start | bytes 131072 | tf_op jit(solution)/shard_map/all_to_all | solution.py:323
  192.6 5.8 %collective-permute-start.10 = (bf16[16,4096]{1,0:T(8,128)(2,1)S(1)}, bf16[16,4096]{1,0:T(8,128)(2,1)S(1)}, u32[]{:S(2)}, u32[]{:S(2)}) collective-permute-start(bf16[16,4096]{1,0:T(8,128)(2,1)S(1)} %fusion.9), channel_id=1, source_target_pairs={{0,32},{16,48},{32,0},{48,16},{64,96},{80,112},{96,64},{112,80},{1... | collective-permute-start | bytes 393224 | tf_op jit(solution)/shard_map/ppermute | solution.py:494
  198.4 8.0 %all-to-all-done.10 = bf16[16,16,128]{2,1,0:T(8,128)(2,1)S(1)} async-done(((bf16[16,16,128]{2,1,0:T(8,128)(2,1)}), bf16[16,16,128]{2,1,0:T(8,128)(2,1)S(1)}, u32[]{:S(2)}, u32[]{:S(2)}) %all-to-all-start.10) | async-done | bytes 65568 | tf_op jit(solution)/shard_map/all_to_all | solution.py:323
  206.4 0.6 convert_reduce_fusion
  207.0 0.7 bitcast_add_fusion.1
  (24 shorter events, 0.4 us)
Async XLA Ops:
  0.6 21.0 %copy-start = (bf16[256,4096]{1,0:T(8,128)(2,1)S(1)}, bf16[256,4096]{1,0:T(8,128)(2,1)}, u32[]{:S(2)}) copy-start(bf16[256,4096]{1,0:T(8,128)(2,1)} %raw_ref.1) | copy-start | bytes 6291460
  2.7 20.8 %all-to-all-start = ((bf16[16,48,256]{2,1,0:T(8,128)(2,1)}), bf16[16,48,256]{2,1,0:T(8,128)(2,1)S(1)}, u32[]{:S(2)}, u32[]{:S(2)}) async-start(bf16[16,48,256]{2,1,0:T(8,128)(2,1)} %shard_map.77), calls=%async_computation | async-start | bytes 786432 | tf_op jit(solution)/shard_map/all_to_all | solution.py:323
  13.2 16.2 %collective-permute-start = (f32[4,48,256]{2,1,0:T(8,128)}, f32[4,48,256]{2,1,0:T(8,128)S(1)}, u32[]{:S(2)}, u32[]{:S(2)}) collective-permute-start(f32[4,48,256]{2,1,0:T(8,128)} %get-tuple-element.39), channel_id=1, source_target_pairs={{0,2},{1,3},{2,0},{3,1},{4,6},{5,7},{6,4},{7,5},{8,10},{9,11},{10,... | collective-permute-start | bytes 589832 | tf_op jit(solution)/shard_map/ppermute | solution.py:384
  16.3 13.1 %collective-permute-start.1 = (f32[4,48,256]{2,1,0:T(8,128)}, f32[4,48,256]{2,1,0:T(8,128)S(1)}, u32[]{:S(2)}, u32[]{:S(2)}) collective-permute-start(f32[4,48,256]{2,1,0:T(8,128)} %get-tuple-element.40), channel_id=1, source_target_pairs={{0,1},{1,2},{2,3},{3,0},{4,5},{5,6},{6,7},{7,4},{8,9},{9,10},{10,1... | collective-permute-start | bytes 589832 | tf_op jit(solution)/shard_map/ppermute | solution.py:384
  16.9 12.6 %collective-permute-start.2 = (f32[4,48,256]{2,1,0:T(8,128)S(1)}, f32[4,48,256]{2,1,0:T(8,128)S(1)}, u32[]{:S(2)}, u32[]{:S(2)}) collective-permute-start(f32[4,48,256]{2,1,0:T(8,128)S(1)} %get-tuple-element.41), channel_id=1, source_target_pairs={{0,3},{1,0},{2,1},{3,2},{4,7},{5,4},{6,5},{7,6},{8,11},{9,8},{10,9... | collective-permute-start | bytes 589832 | tf_op jit(solution)/shard_map/ppermute | solution.py:384
  24.4 19.5 %all-to-all-start.1 = ((bf16[16,48,256]{2,1,0:T(8,128)(2,1)}), bf16[16,48,256]{2,1,0:T(8,128)(2,1)S(1)}, u32[]{:S(2)}, u32[]{:S(2)}) async-start(bf16[16,48,256]{2,1,0:T(8,128)(2,1)} %shard_map.78.unused_ref), calls=%async_computation.1 | async-start | bytes 786432 | tf_op jit(solution)/shard_map/all_to_all | solution.py:323
  29.5 13.1 %collective-permute-start.5 = (f32[48,256]{1,0:T(8,128)S(1)}, f32[48,256]{1,0:T(8,128)S(1)}, u32[]{:S(2)}, u32[]{:S(2)}) collective-permute-start(f32[48,256]{1,0:T(8,128)S(1)} %get-tuple-element.45), channel_id=1, source_target_pairs={{0,12},{1,13},{2,14},{3,15},{4,0},{5,1},{6,2},{7,3},{8,4},{9,5},{1... | collective-permute-start | bytes 147464 | tf_op jit(solution)/shard_map/ppermute | solution.py:403
  29.7 12.9 %collective-permute-start.4 = (f32[48,256]{1,0:T(8,128)S(1)}, f32[48,256]{1,0:T(8,128)S(1)}, u32[]{:S(2)}, u32[]{:S(2)}) collective-permute-start(f32[48,256]{1,0:T(8,128)S(1)} %get-tuple-element.44), channel_id=1, source_target_pairs={{0,4},{1,5},{2,6},{3,7},{4,8},{5,9},{6,10},{7,11},{8,12},{9,13},{1... | collective-permute-start | bytes 147464 | tf_op jit(solution)/shard_map/ppermute | solution.py:403
  31.6 11.0 %collective-permute-start.3 = (f32[48,256]{1,0:T(8,128)S(1)}, f32[48,256]{1,0:T(8,128)S(1)}, u32[]{:S(2)}, u32[]{:S(2)}) collective-permute-start(f32[48,256]{1,0:T(8,128)S(1)} %get-tuple-element.43), channel_id=1, source_target_pairs={{0,8},{1,9},{2,10},{3,11},{4,12},{5,13},{6,14},{7,15},{8,0},{9,1},... | collective-permute-start | bytes 147464 | tf_op jit(solution)/shard_map/ppermute | solution.py:403
  43.8 1.6 copy-start.2
  131.4 12.5 %copy-start.1 = (bf16[256,4096]{1,0:T(8,128)(2,1)S(1)}, bf16[256,4096]{1,0:T(8,128)(2,1)}, u32[]{:S(2)}) copy-start(bf16[256,4096]{1,0:T(8,128)(2,1)} %raw_ref.1) | copy-start | bytes 6291460
  150.7 5.7 %collective-permute-start.6 = (bf16[8,16,4096]{2,1,0:T(8,128)(2,1)}, bf16[8,16,4096]{2,1,0:T(8,128)(2,1)S(1)}, u32[]{:S(2)}, u32[]{:S(2)}) collective-permute-start(bf16[8,16,4096]{2,1,0:T(8,128)(2,1)} %get-tuple-element.62), channel_id=1, source_target_pairs={{0,16},{16,0},{32,48},{48,32},{64,80},{80,64},{96,112},{112,96},{1... | collective-permute-start | bytes 3145736 | tf_op jit(solution)/shard_map/ppermute | solution.py:488
  150.8 19.8 %all-to-all-start.8 = ((bf16[16,112,128]{2,1,0:T(8,128)(2,1)}), bf16[16,112,128]{2,1,0:T(8,128)(2,1)S(1)}, u32[]{:S(2)}, u32[]{:S(2)}) async-start(bf16[16,112,128]{2,1,0:T(8,128)(2,1)} %get-tuple-element.60), calls=%async_computation.8 | async-start | bytes 917504 | tf_op jit(solution)/shard_map/all_to_all | solution.py:323
  160.6 27.6 %copy-start.3 = (bf16[768,128]{1,0:T(8,128)(2,1)S(1)}, bf16[768,128]{1,0:T(8,128)(2,1)}, u32[]{:S(2)}) copy-start(bf16[768,128]{1,0:T(8,128)(2,1)} %hidden_far.3) | copy-start | bytes 589828
  160.6 16.1 %collective-permute-start.9 = (bf16[2,16,4096]{2,1,0:T(8,128)(2,1)S(1)}, bf16[2,16,4096]{2,1,0:T(8,128)(2,1)S(1)}, u32[]{:S(2)}, u32[]{:S(2)}) collective-permute-start(bf16[2,16,4096]{2,1,0:T(8,128)(2,1)S(1)} %get-tuple-element.67), channel_id=1, source_target_pairs={{0,192},{16,208},{32,224},{48,240},{64,0},{80,16},{96,32},{112,48}... | collective-permute-start | bytes 786440 | tf_op jit(solution)/shard_map/ppermute | solution.py:330
  161.4 15.3 %collective-permute-start.8 = (bf16[2,16,4096]{2,1,0:T(8,128)(2,1)S(1)}, bf16[2,16,4096]{2,1,0:T(8,128)(2,1)S(1)}, u32[]{:S(2)}, u32[]{:S(2)}) collective-permute-start(bf16[2,16,4096]{2,1,0:T(8,128)(2,1)S(1)} %get-tuple-element.68), channel_id=1, source_target_pairs={{0,64},{16,80},{32,96},{48,112},{64,128},{80,144},{96,160},{112,17... | collective-permute-start | bytes 786440 | tf_op jit(solution)/shard_map/ppermute | solution.py:330
  162.7 14.0 %collective-permute-start.7 = (bf16[2,16,4096]{2,1,0:T(8,128)(2,1)S(1)}, bf16[2,16,4096]{2,1,0:T(8,128)(2,1)S(1)}, u32[]{:S(2)}, u32[]{:S(2)}) collective-permute-start(bf16[2,16,4096]{2,1,0:T(8,128)(2,1)S(1)} %get-tuple-element.66), channel_id=1, source_target_pairs={{0,128},{16,144},{32,160},{48,176},{64,192},{80,208},{96,224},{112... | collective-permute-start | bytes 786440 | tf_op jit(solution)/shard_map/ppermute | solution.py:330
  171.6 16.5 %all-to-all-start.9 = ((bf16[16,48,256]{2,1,0:T(8,128)(2,1)}), bf16[16,48,256]{2,1,0:T(8,128)(2,1)S(1)}, u32[]{:S(2)}, u32[]{:S(2)}) async-start(bf16[16,48,256]{2,1,0:T(8,128)(2,1)} %shard_map.89), calls=%async_computation.9 | async-start | bytes 786432 | tf_op jit(solution)/shard_map/all_to_all | solution.py:323
  189.1 17.3 %all-to-all-start.10 = ((bf16[16,16,128]{2,1,0:T(8,128)(2,1)}), bf16[16,16,128]{2,1,0:T(8,128)(2,1)S(1)}, u32[]{:S(2)}, u32[]{:S(2)}) async-start(bf16[16,16,128]{2,1,0:T(8,128)(2,1)} %bitcast.16), calls=%async_computation.10 | async-start | bytes 131072 | tf_op jit(solution)/shard_map/all_to_all | solution.py:323
  192.6 14.4 %collective-permute-start.10 = (bf16[16,4096]{1,0:T(8,128)(2,1)S(1)}, bf16[16,4096]{1,0:T(8,128)(2,1)S(1)}, u32[]{:S(2)}, u32[]{:S(2)}) collective-permute-start(bf16[16,4096]{1,0:T(8,128)(2,1)S(1)} %fusion.9), channel_id=1, source_target_pairs={{0,32},{16,48},{32,0},{48,16},{64,96},{80,112},{96,64},{112,80},{1... | collective-permute-start | bytes 393224 | tf_op jit(solution)/shard_map/ppermute | solution.py:494
